TPU v7x, 32 devices: a whole 2x2x4 slice. The times are simulated.
32 devices in a mesh: section: 2 (over y), expert: 16 (over z, x, core).
Axes of the slice: x: 2, y: 2, z: 4, core: 2. Of those that a mesh axis runs over, the one named last changes fastest.
Arguments:
- x_forward: bfloat16 [2, 1024, 1024], P('section', 'expert'), may hold values from -6 to 6
- route_forward: int32 [2, 1024, 8], P('section', 'expert'), may hold values from 0 to 15, all different within a row; in each aligned block of 64 rows (0 to 63, 64 to 127, ..., all dimensions but the last counted through in order) at most 36 rows name the same one
- gate_forward: float32 [2, 1024, 8], P('section', 'expert'), may hold values from 0.05 to 0.6
- x_backward: bfloat16 [2, 1024, 1024], P('section', 'expert'), may hold values from -6 to 6
- route_backward: int32 [2, 1024, 8], P('section', 'expert'), may hold values from 0 to 15, all different within a row; in each aligned block of 64 rows (0 to 63, 64 to 127, ..., all dimensions but the last counted through in order) at most 36 rows name the same one
- gate_backward: float32 [2, 1024, 8], P('section', 'expert'), may hold values from 0.05 to 0.6
- cotangent: bfloat16 [2, 1024, 1024], P('section', 'expert'), may hold values from -6 to 6
- w_gate: bfloat16 [2, 16, 1024, 384], P('section', 'expert'), may hold values from -0.1875 to 0.1875
- w_up: bfloat16 [2, 16, 1024, 384], P('section', 'expert'), may hold values from -0.1875 to 0.1875
- w_down: bfloat16 [2, 16, 384, 1024], P('section', 'expert'), may hold values from -0.3125 to 0.3125
Outputs:
- arrived_forward: bfloat16 [2, 1024, 1024], P('section', 'expert')
- arrived_backward: bfloat16 [2, 1024, 1024], P('section', 'expert')
Inputs may be any that keep to these rules, and one draw needn't show every extreme that they name: `route_forward`: each token names 8 different experts. Among the 64 tokens of one aligned block no expert is named more than 36 times, a bound that some block reaches; every expert is named somewhere. `route_backward`: as for route_forward.
All inputs are finite; a program needn't handle non-finite values.
Results may differ from a plain program's by a relative error of at most 0.0049.
Values may be sent and summed in bfloat16 or wider, within the bound.
No kernel may reach another device: no remote copies, remote signals or barrier semaphores. Data moves between devices by JAX's collectives and lax.ppermute only.
A program may use at most 64 MiB of HBM per device.

v0:
```python
import jax
import jax.numpy as jnp
from jax import lax
from jax.sharding import PartitionSpec as P


def passed_along(block, axis, distance):
    devices = range(lax.axis_size(axis))
    route = [((i - distance) % len(devices), i) for i in devices]
    return lax.ppermute(block, axis, route)


def route_tables(route, gates, capacity, experts):
    ids = route[0]
    one_hot = (ids.reshape(-1)[:, None] == jnp.arange(experts, dtype=jnp.int32)[None, :]).astype(
        jnp.int32
    )
    before = jnp.cumsum(one_hot, axis=0) - one_hot
    rank = jnp.sum(before * one_hot, axis=1).reshape(ids.shape)
    slots = ids * capacity + rank
    match = slots[None, :, :] == jnp.arange(experts * capacity, dtype=jnp.int32)[:, None, None]
    picker = jnp.sum(match.astype(jnp.float32), axis=2).astype(jnp.bfloat16)
    weights = jnp.sum(jnp.where(match, gates[0][None, :, :], 0.0), axis=2)
    return (picker, weights)


def expert_forward(rows, gate_mat, up_mat, down_mat):
    pre_gate = jnp.dot(rows, gate_mat, preferred_element_type=jnp.float32)
    pre_up = jnp.dot(rows, up_mat, preferred_element_type=jnp.float32)
    hidden = (pre_gate * jax.nn.sigmoid(pre_gate) * pre_up).astype(jnp.bfloat16)
    return jnp.dot(hidden, down_mat, preferred_element_type=jnp.float32).astype(jnp.bfloat16)


def expert_backward(rows, cots, gate_mat, up_mat, down_mat):
    pre_gate = jnp.dot(rows, gate_mat, preferred_element_type=jnp.float32)
    pre_up = jnp.dot(rows, up_mat, preferred_element_type=jnp.float32)
    sig_gate = jax.nn.sigmoid(pre_gate)
    d_hidden = lax.dot_general(
        cots, down_mat, (((1,), (1,)), ((), ())), preferred_element_type=jnp.float32
    )
    d_gate = (d_hidden * pre_up * sig_gate * (1.0 + pre_gate * (1.0 - sig_gate))).astype(
        jnp.bfloat16
    )
    d_up = (d_hidden * pre_gate * sig_gate).astype(jnp.bfloat16)
    total = lax.dot_general(
        d_gate, gate_mat, (((1,), (1,)), ((), ())), preferred_element_type=jnp.float32
    )
    total = total + lax.dot_general(
        d_up, up_mat, (((1,), (1,)), ((), ())), preferred_element_type=jnp.float32
    )
    return total.astype(jnp.bfloat16)


def on_device(
    x_forward,
    route_forward,
    gate_forward,
    x_backward,
    route_backward,
    gate_backward,
    cotangent,
    w_gate,
    w_up,
    w_down,
):
    experts = lax.axis_size("expert")
    tokens_here = x_forward.shape[1]
    width = x_forward.shape[2]
    topk = route_forward.shape[2]
    capacity = min(tokens_here, max(2, 9 * tokens_here * topk // (8 * experts)))
    gate_mat = w_gate[0, 0]
    up_mat = w_up[0, 0]
    down_mat = w_down[0, 0]
    picker_fwd, weights_fwd = route_tables(route_forward, gate_forward, capacity, experts)
    picker_bwd, weights_bwd = route_tables(route_backward, gate_backward, capacity, experts)
    send_x = (
        jnp.dot(picker_fwd, x_forward[0], preferred_element_type=jnp.float32)
        .astype(jnp.bfloat16)
        .reshape(experts, capacity, width)
    )
    send_xb = (
        jnp.dot(picker_bwd, x_backward[0], preferred_element_type=jnp.float32)
        .astype(jnp.bfloat16)
        .reshape(experts, capacity, width)
    )
    send_cot = (
        jnp.dot(picker_bwd, cotangent[0], preferred_element_type=jnp.float32)
        .astype(jnp.bfloat16)
        .reshape(experts, capacity, width)
    )
    received = lax.all_to_all(send_x, "expert", split_axis=0, concat_axis=0, tiled=True)
    shape = received.shape
    back_fwd = expert_forward(received.reshape(-1, width), gate_mat, up_mat, down_mat).reshape(
        shape
    )
    received = (
        lax.all_to_all(send_xb, "expert", split_axis=0, concat_axis=0, tiled=True),
        lax.all_to_all(send_cot, "expert", split_axis=0, concat_axis=0, tiled=True),
    )
    shape = received[0].shape
    result = expert_backward(
        received[0].reshape(-1, width), received[1].reshape(-1, width), gate_mat, up_mat, down_mat
    )
    back_bwd = result.reshape(shape)
    back_fwd, back_bwd = (
        lax.all_to_all(back_fwd, "expert", split_axis=0, concat_axis=0, tiled=True),
        lax.all_to_all(back_bwd, "expert", split_axis=0, concat_axis=0, tiled=True),
    )
    mixed_fwd = jnp.einsum(
        "st,sd->td",
        weights_fwd,
        back_fwd.reshape(-1, width).astype(jnp.float32),
        precision=lax.Precision.HIGHEST,
    )
    layer_out = (x_forward[0].astype(jnp.float32) + mixed_fwd).astype(jnp.bfloat16)
    mixed_bwd = jnp.einsum(
        "st,sd->td",
        weights_bwd,
        back_bwd.reshape(-1, width).astype(jnp.float32),
        precision=lax.Precision.HIGHEST,
    )
    input_grad = (cotangent[0].astype(jnp.float32) + mixed_bwd).astype(jnp.bfloat16)
    arrived_forward = passed_along(layer_out[None], "section", 1)
    arrived_backward = passed_along(input_grad[None], "section", -1)
    return (arrived_forward, arrived_backward)


def solution(mesh):
    in_specs = (
        P("section", "expert", None),
        P("section", "expert", None),
        P("section", "expert", None),
        P("section", "expert", None),
        P("section", "expert", None),
        P("section", "expert", None),
        P("section", "expert", None),
        P("section", "expert", None, None),
        P("section", "expert", None, None),
        P("section", "expert", None, None),
    )
    out_specs = (P("section", "expert", None), P("section", "expert", None))
    return jax.shard_map(
        on_device, mesh=mesh, in_specs=in_specs, out_specs=out_specs, check_vma=False
    )
```

profile of v0, /device:TPU:0, one launch (start us, length us, event | category | flops | bytes accessed | tf_op | source)
XLA Modules:
  0.0 195.3 jit_solution(15329495855236816442)
XLA Ops:
  4.9 1.5 convert_reduce_fusion
  6.4 1.4 convolution_convert_fusion
  7.8 1.2 reshape.86
  9.0 7.5 %all-to-all-start.3 = ((bf16[16,36,1024]{2,1,0:T(8,128)(2,1)}), bf16[16,36,1024]{2,1,0:T(8,128)(2,1)S(1)}, u32[]{:S(2)}, u32[]{:S(2)}) async-start(bf16[16,36,1024]{2,1,0:T(8,128)(2,1)} %reshape.86), calls=%async_computation.3 | async-start | bytes 2621440 | tf_op jit(solution)/shard_map/all_to_all | solution.py:97
  17.0 1.2 reshape.84
  18.2 25.7 %all-to-all-done.3 = bf16[16,36,1024]{2,1,0:T(8,128)(2,1)S(1)} async-done(((bf16[16,36,1024]{2,1,0:T(8,128)(2,1)}), bf16[16,36,1024]{2,1,0:T(8,128)(2,1)S(1)}, u32[]{:S(2)}, u32[]{:S(2)}) %all-to-all-start.3) | async-done | bytes 1179680 | tf_op jit(solution)/shard_map/all_to_all | solution.py:97
  44.0 8.0 %all-to-all-start.2 = ((bf16[16,36,1024]{2,1,0:T(8,128)(2,1)}), bf16[16,36,1024]{2,1,0:T(8,128)(2,1)S(1)}, u32[]{:S(2)}, u32[]{:S(2)}) async-start(bf16[16,36,1024]{2,1,0:T(8,128)(2,1)} %reshape.84), calls=%async_computation.2 | async-start | bytes 2621440 | tf_op jit(solution)/shard_map/all_to_all | solution.py:98
  55.0 3.1 %reduce-window.14 = s32[16,4,128]{2,0,1:T(8,128)} reduce-window(s32[16,4,128]{2,0,1:T(8,128)} %fusion.45, s32[]{:T(128)} %constant.11.clone.1), window={size=1x1x128 pad=0_0x0_0x127_0}, to_apply=%region_0.0 | reduce-window | flops 1040384 | bytes 65540 | tf_op jit(solution)/shard_map/reduce-window
  62.3 1.4 copy.45
  63.6 2.3 %convert_reduce_fusion.1 = (bf16[576,64]{0,1:T(8,128)(2,1)S(1)}, f32[576,64]{0,1:T(8,128)}) fusion(s32[64,8]{1,0:T(8,128)} %copy.44, f32[64,8]{1,0:T(8,128)} %copy.45), kind=kLoop, calls=%fused_computation.12 | loop fusion | flops 1400832 | bytes 225280 | tf_op jit(solution)/shard_map/reduce_sum | solution.py:22
  66.0 2.4 %convolution_convert_fusion.3 = bf16[576,1024]{1,0:T(8,128)(2,1)} fusion(bf16[1,64,1024]{2,1,0:T(8,128)(2,1)} %param.10, bf16[576,64]{0,1:T(8,128)(2,1)S(1)} %get-tuple-element.4), kind=kOutput, calls=%fused_computation.4 | convolution fusion | flops 76087296 | bytes 1384448 | tf_op jit(solution)/shard_map/dot_general | solution.py:77
  68.4 2.2 %reshape.78 = bf16[16,36,1024]{2,1,0:T(8,128)(2,1)} reshape(bf16[576,1024]{1,0:T(8,128)(2,1)} %convolution_convert_fusion.3) | data formatting | bytes 2359296 | tf_op jit(solution)/shard_map/reshape | solution.py:79
  70.6 8.7 %all-to-all-done.2 = bf16[16,36,1024]{2,1,0:T(8,128)(2,1)S(1)} async-done(((bf16[16,36,1024]{2,1,0:T(8,128)(2,1)}), bf16[16,36,1024]{2,1,0:T(8,128)(2,1)S(1)}, u32[]{:S(2)}, u32[]{:S(2)}) %all-to-all-start.2) | async-done | bytes 1179680 | tf_op jit(solution)/shard_map/all_to_all | solution.py:98
  79.4 8.1 %all-to-all-start = ((bf16[16,36,1024]{2,1,0:T(8,128)(2,1)}), bf16[16,36,1024]{2,1,0:T(8,128)(2,1)}, u32[]{:S(2)}, u32[]{:S(2)}) async-start(bf16[16,36,1024]{2,1,0:T(8,128)(2,1)} %reshape.78), calls=%async_computation | async-start | bytes 2621440 | tf_op jit(solution)/shard_map/all_to_all | solution.py:91
  90.3 3.0 %fusion.26 = f32[576,384]{1,0:T(8,128)} fusion(bf16[576,1024]{1,0:T(8,128)(2,1)S(1)} %copy-done.1, bf16[1,1,1024,384]{3,2,1,0:T(8,128)(2,1)} %param.17), kind=kOutput, calls=%fused_computation.41 | convolution fusion | flops 452984832 | bytes 2850816 | tf_op jit(solution)/shard_map/dot_general | solution.py:35
  93.3 1.7 fusion.17
  95.1 4.3 %fusion.4 = f32[576,1024]{1,0:T(8,128)} fusion(f32[576,384]{1,0:T(8,128)} %fusion.17, bf16[576,1024]{1,0:T(8,128)(2,1)S(1)} %copy-done.1, f32[576,384]{1,0:T(8,128)} %fusion.26, bf16[1,1,1024,384]{3,2,1,0:T(8,128)(2,1)S(1)} %copy-done, bf16[1,1,1024,384]{3,2,1,0:T(8,128)(2,1)S(1)} %copy-done.6), kind=kOutput, calls=%fused_computation.17 | convolution fusion | flops 908181504 | bytes 6881280 | tf_op jit(solution)/shard_map/dot_general | solution.py:45
  99.4 3.0 %add_convert_fusion = bf16[576,1024]{1,0:T(8,128)(2,1)S(1)} fusion(f32[576,1024]{1,0:T(8,128)} %fusion.4, bf16[1,1,1024,384]{3,2,1,0:T(8,128)(2,1)S(1)} %copy-done, f32[576,384]{1,0:T(8,128)} %fusion.17, f32[576,384]{1,0:T(8,128)} %fusion.26), kind=kOutput, calls=%fused_computation | convolution fusion | flops 455491584 | bytes 6094848 | tf_op jit(solution)/shard_map/dot_general | solution.py:48
  103.6 11.3 %all-to-all-done = bf16[16,36,1024]{2,1,0:T(8,128)(2,1)} async-done(((bf16[16,36,1024]{2,1,0:T(8,128)(2,1)}), bf16[16,36,1024]{2,1,0:T(8,128)(2,1)}, u32[]{:S(2)}, u32[]{:S(2)}) %all-to-all-start) | async-done | bytes 1179680 | tf_op jit(solution)/shard_map/all_to_all | solution.py:91
  114.9 8.0 %all-to-all-start.4 = ((bf16[16,36,1024]{2,1,0:T(8,128)(2,1)}), bf16[16,36,1024]{2,1,0:T(8,128)(2,1)S(1)}, u32[]{:S(2)}, u32[]{:S(2)}) async-start(bf16[16,36,1024]{2,1,0:T(8,128)(2,1)} %reshape.88), calls=%async_computation.4 | async-start | bytes 2621440 | tf_op jit(solution)/shard_map/all_to_all | solution.py:107
  122.9 1.4 reshape.79
  124.4 2.9 %fusion.28 = f32[576,384]{1,0:T(8,128)} fusion(bf16[576,1024]{1,0:T(8,128)(2,1)S(1)} %reshape.79, bf16[1,1,1024,384]{3,2,1,0:T(8,128)(2,1)} %param.17), kind=kOutput, calls=%fused_computation.43 | convolution fusion | flops 452984832 | bytes 2850816 | tf_op jit(solution)/shard_map/dot_general | solution.py:28
  127.2 3.8 %convolution_convert_fusion.2 = bf16[576,1024]{1,0:T(8,128)(2,1)} fusion(bf16[576,1024]{1,0:T(8,128)(2,1)S(1)} %reshape.79, f32[576,384]{1,0:T(8,128)} %fusion.28, bf16[1,1,384,1024]{3,2,1,0:T(8,128)(2,1)} %param.19, bf16[1,1,1024,384]{3,2,1,0:T(8,128)(2,1)S(1)} %copy-done), kind=kOutput, calls=%fused_computation.3 | convolution fusion | flops 907886592 | bytes 4816896 | tf_op jit(solution)/shard_map/dot_general | solution.py:31
  131.1 2.3 %reshape.80 = bf16[16,36,1024]{2,1,0:T(8,128)(2,1)} reshape(bf16[576,1024]{1,0:T(8,128)(2,1)} %convolution_convert_fusion.2) | data formatting | bytes 2359296 | tf_op jit(solution)/shard_map/reshape | solution.py:93
  133.3 17.0 %all-to-all-done.4 = bf16[16,36,1024]{2,1,0:T(8,128)(2,1)S(1)} async-done(((bf16[16,36,1024]{2,1,0:T(8,128)(2,1)}), bf16[16,36,1024]{2,1,0:T(8,128)(2,1)S(1)}, u32[]{:S(2)}, u32[]{:S(2)}) %all-to-all-start.4) | async-done | bytes 1179680 | tf_op jit(solution)/shard_map/all_to_all | solution.py:107
  150.4 8.0 %all-to-all-start.1 = ((bf16[16,36,1024]{2,1,0:T(8,128)(2,1)}), bf16[16,36,1024]{2,1,0:T(8,128)(2,1)S(1)}, u32[]{:S(2)}, u32[]{:S(2)}) async-start(bf16[16,36,1024]{2,1,0:T(8,128)(2,1)} %reshape.80), calls=%async_computation.1 | async-start | bytes 2621440 | tf_op jit(solution)/shard_map/all_to_all | solution.py:106
  159.5 2.8 %fusion.7 = bf16[1,64,1024]{2,1,0:T(8,128)(2,1)} fusion(f32[576,64]{0,1:T(8,128)} %get-tuple-element.3, bf16[576,1024]{1,0:T(8,128)(2,1)} %reshape.89, bf16[1,64,1024]{2,1,0:T(8,128)(2,1)S(1)} %copy-done.3), kind=kOutput, calls=%fused_computation.22 | convolution fusion | flops 453181440 | bytes 1589248 | tf_op jit(solution)/shard_map/st,sd->td/dot_general | solution.py:116
  162.3 1.5 collective-permute-start.1
  163.9 21.9 %all-to-all-done.1 = bf16[16,36,1024]{2,1,0:T(8,128)(2,1)S(1)} async-done(((bf16[16,36,1024]{2,1,0:T(8,128)(2,1)}), bf16[16,36,1024]{2,1,0:T(8,128)(2,1)S(1)}, u32[]{:S(2)}, u32[]{:S(2)}) %all-to-all-start.1) | async-done | bytes 1179680 | tf_op jit(solution)/shard_map/all_to_all | solution.py:106
  186.1 1.7 fusion.8
  187.8 1.6 collective-permute-start
  189.4 4.7 %collective-permute-done = bf16[1,64,1024]{2,1,0:T(8,128)(2,1)S(1)} collective-permute-done((bf16[1,64,1024]{2,1,0:T(8,128)(2,1)S(1)}, bf16[1,64,1024]{2,1,0:T(8,128)(2,1)S(1)}, u32[]{:S(2)}, u32[]{:S(2)}) %collective-permute-start) | collective-permute-done | bytes 131104 | tf_op jit(solution)/shard_map/ppermute | solution.py:10
  (51 shorter events, 18.7 us)
Async XLA Ops:
  0.6 94.4 %copy-start = (bf16[1,1,1024,384]{3,2,1,0:T(8,128)(2,1)S(1)}, bf16[1,1,1024,384]{3,2,1,0:T(8,128)(2,1)}, u32[]{:S(2)}) copy-start(bf16[1,1,1024,384]{3,2,1,0:T(8,128)(2,1)} %param.18) | copy-start | bytes 2359300
  9.0 7.5 %copy-start.3 = (bf16[1,64,1024]{2,1,0:T(8,128)(2,1)S(1)}, bf16[1,64,1024]{2,1,0:T(8,128)(2,1)}, u32[]{:S(2)}) copy-start(bf16[1,64,1024]{2,1,0:T(8,128)(2,1)} %param.16) | copy-start | bytes 393220
  9.0 34.9 %all-to-all-start.3 = ((bf16[16,36,1024]{2,1,0:T(8,128)(2,1)}), bf16[16,36,1024]{2,1,0:T(8,128)(2,1)S(1)}, u32[]{:S(2)}, u32[]{:S(2)}) async-start(bf16[16,36,1024]{2,1,0:T(8,128)(2,1)} %reshape.86), calls=%async_computation.3 | async-start | bytes 2621440 | tf_op jit(solution)/shard_map/all_to_all | solution.py:97
  18.2 33.7 %copy-start.5 = (s32[1,64,8]{1,2,0:T(8,128)S(1)}, s32[1,64,8]{1,2,0:T(8,128)}, u32[]{:S(2)}) copy-start(s32[1,64,8]{1,2,0:T(8,128)} %param.11) | copy-start | bytes 6148
  44.0 35.4 %all-to-all-start.2 = ((bf16[16,36,1024]{2,1,0:T(8,128)(2,1)}), bf16[16,36,1024]{2,1,0:T(8,128)(2,1)S(1)}, u32[]{:S(2)}, u32[]{:S(2)}) async-start(bf16[16,36,1024]{2,1,0:T(8,128)(2,1)} %reshape.84), calls=%async_computation.2 | async-start | bytes 2621440 | tf_op jit(solution)/shard_map/all_to_all | solution.py:98
  79.4 35.5 %all-to-all-start = ((bf16[16,36,1024]{2,1,0:T(8,128)(2,1)}), bf16[16,36,1024]{2,1,0:T(8,128)(2,1)}, u32[]{:S(2)}, u32[]{:S(2)}) async-start(bf16[16,36,1024]{2,1,0:T(8,128)(2,1)} %reshape.78), calls=%async_computation | async-start | bytes 2621440 | tf_op jit(solution)/shard_map/all_to_all | solution.py:91
  88.6 1.7 copy-start.1
  90.3 3.0 %copy-start.2 = (bf16[576,1024]{1,0:T(8,128)(2,1)S(1)}, bf16[576,1024]{1,0:T(8,128)(2,1)}, u32[]{:S(2)}) copy-start(bf16[576,1024]{1,0:T(8,128)(2,1)} %reshape.85) | copy-start | bytes 3538948
  90.3 3.0 %copy-start.7 = (bf16[1,1,384,1024]{3,2,1,0:T(8,128)(2,1)S(1)}, bf16[1,1,384,1024]{3,2,1,0:T(8,128)(2,1)}, u32[]{:S(2)}) copy-start(bf16[1,1,384,1024]{3,2,1,0:T(8,128)(2,1)} %param.19) | copy-start | bytes 2359300
  93.3 1.7 copy-start.6
  114.9 35.4 %all-to-all-start.4 = ((bf16[16,36,1024]{2,1,0:T(8,128)(2,1)}), bf16[16,36,1024]{2,1,0:T(8,128)(2,1)S(1)}, u32[]{:S(2)}, u32[]{:S(2)}) async-start(bf16[16,36,1024]{2,1,0:T(8,128)(2,1)} %reshape.88), calls=%async_computation.4 | async-start | bytes 2621440 | tf_op jit(solution)/shard_map/all_to_all | solution.py:107
  150.4 35.4 %all-to-all-start.1 = ((bf16[16,36,1024]{2,1,0:T(8,128)(2,1)}), bf16[16,36,1024]{2,1,0:T(8,128)(2,1)S(1)}, u32[]{:S(2)}, u32[]{:S(2)}) async-start(bf16[16,36,1024]{2,1,0:T(8,128)(2,1)} %reshape.80), calls=%async_computation.1 | async-start | bytes 2621440 | tf_op jit(solution)/shard_map/all_to_all | solution.py:106
  162.3 23.7 %copy-start.4 = (bf16[1,64,1024]{2,1,0:T(8,128)(2,1)S(1)}, bf16[1,64,1024]{2,1,0:T(8,128)(2,1)}, u32[]{:S(2)}) copy-start(bf16[1,64,1024]{2,1,0:T(8,128)(2,1)} %param.10) | copy-start | bytes 393220
  162.3 27.0 %collective-permute-start.1 = (bf16[1,64,1024]{2,1,0:T(8,128)(2,1)}, bf16[1,64,1024]{2,1,0:T(8,128)(2,1)S(1)}, u32[]{:S(2)}, u32[]{:S(2)}) collective-permute-start(bf16[1,64,1024]{2,1,0:T(8,128)(2,1)} %fusion.7), channel_id=1, source_target_pairs={{16,0},{0,16},{17,1},{1,17},{18,2},{2,18},{19,3},{3,19},{20,4},{4,... | collective-permute-start | bytes 393224 | tf_op jit(solution)/shard_map/ppermute | solution.py:10
  187.8 6.2 %collective-permute-start = (bf16[1,64,1024]{2,1,0:T(8,128)(2,1)S(1)}, bf16[1,64,1024]{2,1,0:T(8,128)(2,1)S(1)}, u32[]{:S(2)}, u32[]{:S(2)}) collective-permute-start(bf16[1,64,1024]{2,1,0:T(8,128)(2,1)S(1)} %fusion.8), channel_id=1, source_target_pairs={{16,0},{0,16},{17,1},{1,17},{18,2},{2,18},{19,3},{3,19},{20,4},{4,... | collective-permute-start | bytes 393224 | tf_op jit(solution)/shard_map/ppermute | solution.py:10
where the time goes:
time: 198 us; the launch traced here: 195 us
  waiting for transfers between devices  89.4 us (45%)
  starting transfers between devices  42.7 us (22%)
  matrix products  27.6 us (14%)
  local copies, waits for them, and re-layouts  24.4 us (12%)
  other arithmetic  10.5 us (5%)
    all_to_all x1, waiting for transfers between devices, on_device(): lax.all_to_all(send_xb, 'expert', split_axis=0, concat_axis=0, tiled=True)  25.7 us
    all_to_all x1, waiting for transfers between devices, on_device(): lax.all_to_all(back_fwd, 'expert', split_axis=0, concat_axis=0, tiled=True)  21.9 us
    all_to_all x1, waiting for transfers between devices, on_device(): lax.all_to_all(back_bwd, 'expert', split_axis=0, concat_axis=0, tiled=True)  17 us
    all_to_all x1, waiting for transfers between devices, on_device(): lax.all_to_all(send_x, 'expert', split_axis=0, concat_axis=0, tiled=True)  11.3 us
    all_to_all x1, waiting for transfers between devices, on_device(): lax.all_to_all(send_cot, 'expert', split_axis=0, concat_axis=0, tiled=True)  8.74 us
    all_to_all x1, starting transfers between devices, on_device(): lax.all_to_all(send_x, 'expert', split_axis=0, concat_axis=0, tiled=True)  8.06 us
    all_to_all x1, starting transfers between devices, on_device(): lax.all_to_all(send_cot, 'expert', split_axis=0, concat_axis=0, tiled=True)  8.01 us
    all_to_all x1, starting transfers between devices, on_device(): lax.all_to_all(back_fwd, 'expert', split_axis=0, concat_axis=0, tiled=True)  8.01 us
  transfers between devices with their start and end apart: 7, of which 6 were waited for; matrix products, arithmetic and copies ran while one was open for 27% of the time, Pallas kernels for 0%

commit v1 on v0

v1 whole, which is shorter than its diff:
```python
import functools

import jax
import jax.numpy as jnp
from jax import lax
from jax.experimental import pallas as pl
from jax.experimental.pallas import tpu as pltpu
from jax.sharding import PartitionSpec as P

F32 = jnp.float32
BF16 = jnp.bfloat16
LANES = 128
VMEM_LIMIT = 48 * 1024 * 1024


def passed_along(block, axis, distance):
    devices = range(lax.axis_size(axis))
    route = [((i - distance) % len(devices), i) for i in devices]
    return lax.ppermute(block, axis, route)


def swapped(block, bit):
    return lax.ppermute(block, "expert", [(i, i ^ bit) for i in range(lax.axis_size("expert"))])


def spread(block, bits):
    held, order = block, [0]
    for bit in bits[:-1]:
        held = jnp.concatenate([held, swapped(held, bit)], axis=0)
        order = order + [r | bit for r in order]
    return held, swapped(held, bits[-1]), order + [r | bits[-1] for r in order]


def halving_order(bits):
    order = [0]
    for bit in reversed(bits):
        order = [r | bit for r in order] + order
    return order


def gathered_back(send, keep, bits):
    for bit in bits[:-1]:
        total = keep + swapped(send, bit).astype(F32)
        half = total.shape[0] // 2
        send, keep = total[:half].astype(BF16), total[half:]
    return keep + swapped(send, bits[-1]).astype(F32)


def route_columns(route, gates):
    high = lax.reduce_precision(gates, 8, 7)
    rest = gates - high
    middle = lax.reduce_precision(rest, 8, 7)
    low = rest - middle
    return [route.astype(BF16), high.astype(BF16), middle.astype(BF16), low.astype(BF16)]


def rows_of(refs, order, wanted, rows, columns=None):
    parts = []
    half = len(order) // 2
    for r in wanted:
        at = order.index(r)
        ref = refs[at // half]
        block = pl.ds(at % half * rows, rows)
        parts.append(ref[block, :] if columns is None else ref[block, columns])
    return jnp.concatenate(parts, axis=0)


def gate_of(words, topk, first, expert):
    words = words.astype(F32)
    at = [words[:, (first + j) * topk : (first + j + 1) * topk] for j in range(4)]
    gates = at[1] + at[2] + at[3]
    chosen = at[0] == expert.astype(F32)
    return jnp.sum(jnp.where(chosen, gates, 0.0), axis=1, keepdims=True)


def times(a, b):
    return lax.dot_general(a, b, (((1,), (0,)), ((), ())), preferred_element_type=F32)


def times_transposed(a, b):
    return lax.dot_general(a, b, (((1,), (1,)), ((), ())), preferred_element_type=F32)


def forward_kernel(
    width, topk, rows, order, back, step, me_ref, xa, xb, gu0, d0, gu1, d1, send_ref, keep_ref
):
    half = len(back) // 2
    for out_ref, wanted in ((send_ref, back[:half]), (keep_ref, back[half:])):
        for start in range(0, half, step):
            now = wanted[start : start + step]
            both = rows_of((xa, xb), order, now, rows)
            x, words = both[:, :width], both[:, width:]
            total = None
            for flip, gu_ref, d_ref in ((0, gu0, d0), (1, gu1, d1)):
                pre = times(x, gu_ref[...])
                hidden_width = pre.shape[1] // 2
                gate, up = pre[:, :hidden_width], pre[:, hidden_width:]
                hidden = (gate * jax.nn.sigmoid(gate) * up).astype(BF16)
                out = times(hidden, d_ref[...]).astype(BF16).astype(F32)
                out = out * gate_of(words, topk, 0, me_ref[0] ^ flip)
                total = out if total is None else total + out
            out_ref[pl.ds(start * rows, len(now) * rows), :] = total.astype(out_ref.dtype)


def backward_kernel(
    topk,
    rows,
    orders,
    back,
    step,
    me_ref,
    wa,
    wb,
    xa,
    xb,
    ca,
    cb,
    gu0,
    d0,
    gu1,
    d1,
    send_ref,
    keep_ref,
):
    half = len(back) // 2
    for out_ref, wanted in ((send_ref, back[:half]), (keep_ref, back[half:])):
        for start in range(0, half, step):
            now = wanted[start : start + step]
            words = rows_of((wa, wb), orders[0], now, rows)
            x = rows_of((xa, xb), orders[1], now, rows)
            cot = rows_of((ca, cb), orders[2], now, rows)
            total = None
            for flip, gu_ref, d_ref in ((0, gu0, d0), (1, gu1, d1)):
                pre = times(x, gu_ref[...])
                hidden_width = pre.shape[1] // 2
                gate, up = pre[:, :hidden_width], pre[:, hidden_width:]
                sig = jax.nn.sigmoid(gate)
                d_hidden = times_transposed(cot, d_ref[...])
                d_gate = d_hidden * up * sig * (1.0 + gate * (1.0 - sig))
                d_up = d_hidden * gate * sig
                both = jnp.concatenate([d_gate.astype(BF16), d_up.astype(BF16)], axis=1)
                out = times_transposed(both, gu_ref[...]).astype(BF16).astype(F32)
                out = out * gate_of(words, topk, 4, me_ref[0] ^ flip)
                total = out if total is None else total + out
            out_ref[pl.ds(start * rows, len(now) * rows), :] = total.astype(out_ref.dtype)


def call(kernel, operands, out_rows, width, flops, words=()):
    whole = pl.BlockSpec(memory_space=pltpu.VMEM)
    specs = [pl.BlockSpec(memory_space=pltpu.SMEM)] + [whole] * (len(operands) - 1)
    for at in words:
        shape = operands[at].shape
        block = (shape[0], shape[1] - width)
        specs[at] = pl.BlockSpec(block, lambda i: (0, width // block[1]))
    shapes = (
        jax.ShapeDtypeStruct((out_rows, width), BF16),
        jax.ShapeDtypeStruct((out_rows, width), F32),
    )
    moved = sum(a.size * a.dtype.itemsize for a in operands)
    return pl.pallas_call(
        kernel,
        grid=(1,),
        out_shape=shapes,
        in_specs=specs,
        out_specs=(whole, whole),
        compiler_params=pltpu.CompilerParams(vmem_limit_bytes=VMEM_LIMIT),
        cost_estimate=pl.CostEstimate(
            flops=flops, bytes_accessed=moved + out_rows * width * 6, transcendentals=0
        ),
    )(*operands)


def on_device(
    x_forward,
    route_forward,
    gate_forward,
    x_backward,
    route_backward,
    gate_backward,
    cotangent,
    w_gate,
    w_up,
    w_down,
):
    experts = lax.axis_size("expert")
    rows, width = x_forward.shape[1:]
    topk = route_forward.shape[2]
    hidden_width = w_gate.shape[3]
    me = lax.axis_index("expert").astype(jnp.int32)

    bits = []
    while 2 << len(bits) < experts:
        bits.insert(0, 2 << len(bits))
    blocks = experts // 2

    columns = route_columns(route_forward[0], gate_forward[0])
    columns += route_columns(route_backward[0], gate_backward[0])
    padding = -(8 * topk) % LANES
    forward_rows = jnp.concatenate(
        [x_forward[0]] + columns + [jnp.zeros((rows, padding), BF16)], axis=1
    )

    gate_up0 = jnp.concatenate([w_gate[0, 0], w_up[0, 0]], axis=1)
    down0 = w_down[0, 0]
    gate_up1, down1 = swapped(gate_up0, 1), swapped(down0, 1)
    weights = (gate_up0, down0, gate_up1, down1)

    fa, fb, forward_order = spread(forward_rows, bits)
    xa, xb, x_order = spread(x_backward[0], bits)
    ca, cb, c_order = spread(cotangent[0], bits)

    back_bits = bits[::-1]
    back = halving_order(back_bits)
    step = min(4, blocks // 2)
    matmul = 2 * blocks * rows * width * hidden_width * 2
    place = jnp.reshape(me, (1,))
    send_f, keep_f = call(
        functools.partial(forward_kernel, width, topk, rows, forward_order, back, step),
        (place, fa, fb) + weights,
        blocks // 2 * rows,
        width,
        3 * matmul,
    )
    layer_out = x_forward[0].astype(F32) + gathered_back(send_f, keep_f, back_bits)
    arrived_forward = passed_along(layer_out.astype(BF16)[None], "section", 1)

    send_b, keep_b = call(
        functools.partial(
            backward_kernel, topk, rows, (forward_order, x_order, c_order), back, step
        ),
        (place, fa, fb, xa, xb, ca, cb) + weights,
        blocks // 2 * rows,
        width,
        5 * matmul,
        words=(1, 2),
    )
    input_grad = cotangent[0].astype(F32) + gathered_back(send_b, keep_b, back_bits)
    arrived_backward = passed_along(input_grad.astype(BF16)[None], "section", -1)
    return (arrived_forward, arrived_backward)


def solution(mesh):
    in_specs = (
        P("section", "expert", None),
        P("section", "expert", None),
        P("section", "expert", None),
        P("section", "expert", None),
        P("section", "expert", None),
        P("section", "expert", None),
        P("section", "expert", None),
        P("section", "expert", None, None),
        P("section", "expert", None, None),
        P("section", "expert", None, None),
    )
    out_specs = (P("section", "expert", None), P("section", "expert", None))
    return jax.shard_map(
        on_device, mesh=mesh, in_specs=in_specs, out_specs=out_specs, check_vma=False
    )
```

time: 198 us -> 120 us (0.61); the launches traced: 195 us -> 120 us
  matrix products: 27.6 us -> 0 us
  waiting for transfers between devices: 89.4 us -> 70.1 us
  local copies, waits for them, and re-layouts: 24.4 us -> 5.54 us
  starting transfers between devices: 42.7 us -> 26.6 us
  Pallas kernels: 0 us -> 14.4 us
  other arithmetic: 10.5 us -> 2.32 us
    all_to_all x5 -> x0, waiting for transfers between devices: 84.7 us -> none  [the longest x1 25.7 us: on_device(): lax.all_to_all(send_xb, 'expert', split_axis=0, concat_axis=0, tiled=True)]
    ppermute x0 -> x17, waiting for transfers between devices: none -> 66.6 us  [swapped(): lax.ppermute(block, 'expert', [(i, i ^ bit) for i in range(lax.axis_size(...]
    all_to_all x5 -> x0, starting transfers between devices: 39.6 us -> none  [the longest x1 8.06 us: on_device(): lax.all_to_all(send_x, 'expert', split_axis=0, concat_axis=0, tiled=True)]
    dot_general x11 -> x0, matrix products: 27.6 us -> none  [the longest x1 4.33 us: expert_backward(): lax.dot_general(d_gate, gate_mat, (((1,), (1,)), ((), ())), preferred_ele...]
    ppermute x0 -> x17, starting transfers between devices: none -> 23.4 us  [swapped(): lax.ppermute(block, 'expert', [(i, i ^ bit) for i in range(lax.axis_size(...]
    reshape x14 -> x0, local copies, waits for them, and re-layouts: 14.9 us -> none  [the longest x1 2.26 us: on_device(): expert_forward(received.reshape(-1, width), gate_mat, up_mat, down_mat)]
    pallas_call x0 -> x2, Pallas kernels: none -> 14.4 us  [call(): pl.pallas_call(kernel, grid=(1,), out_shape=shapes, in_specs=specs, out_s...]
    reduce_sum x4 -> x0, other arithmetic: 4.8 us -> none  [the longest x2 3.84 us: route_tables(): picker = jnp.sum(match.astype(jnp.float32), axis=2).astype(jnp.bfloat16)]
  transfers between devices with their start and end apart: 7 -> 19, of which waited for: 6 -> 12; matrix products, arithmetic and copies ran while one was open for 27% -> 5% of each run, Pallas kernels for 0% -> 5%
where the time goes in v1:
time: 120 us
  waiting for transfers between devices  70.1 us (58%)
  starting transfers between devices  26.6 us (22%)
  Pallas kernels  14.4 us (12%)
  local copies, waits for them, and re-layouts  5.54 us (5%)
  other arithmetic  2.32 us (2%)
    ppermute x17, waiting for transfers between devices, swapped(): lax.ppermute(block, 'expert', [(i, i ^ bit) for i in range(lax.axis_size(...  66.6 us
    ppermute x17, starting transfers between devices, swapped(): lax.ppermute(block, 'expert', [(i, i ^ bit) for i in range(lax.axis_size(...  23.4 us
    pallas_call x2, Pallas kernels, call(): pl.pallas_call(kernel, grid=(1,), out_shape=shapes, in_specs=specs, out_s...  14.4 us
    unnamed x18, local copies, waits for them, and re-layouts  4.42 us
    ppermute x2, waiting for transfers between devices, passed_along(): return lax.ppermute(block, axis, route)  3.45 us
    ppermute x2, starting transfers between devices, passed_along(): return lax.ppermute(block, axis, route)  3.17 us
  transfers between devices with their start and end apart: 19, of which 12 were waited for; matrix products, arithmetic and copies ran while one was open for 5% of the time, Pallas kernels for 5%

profile of v1, /device:TPU:0, one launch (start us, length us, event | category | flops | bytes accessed | tf_op | source)
XLA Modules:
  0.0 119.9 jit_solution(8619038105304600907)
XLA Ops:
  0.6 4.1 %collective-permute-start.12 = (bf16[64,1024]{1,0:T(8,128)(2,1)}, bf16[64,1024]{1,0:T(8,128)(2,1)S(1)}, u32[]{:S(2)}, u32[]{:S(2)}) collective-permute-start(bf16[64,1024]{1,0:T(8,128)(2,1)} %bitcast.31), channel_id=1, source_target_pairs={{0,8},{1,9},{2,10},{3,11},{4,12},{5,13},{6,14},{7,15},{8,0},{9,1},... | collective-permute-start | bytes 393224 | tf_op jit(solution)/shard_map/ppermute | solution.py:23
  4.7 0.8 copy.16
  5.5 0.8 copy.17
  6.3 0.8 copy.18
  7.0 0.8 copy.19
  7.9 1.0 concatenate.27
  9.0 1.5 %pad_maximum_fusion.gu0 = bf16[1024,768]{1,0:T(8,128)(2,1)S(1)} fusion(bf16[1024,384]{1,0:T(8,128)(2,1)} %bitcast.34, bf16[1024,384]{1,0:T(8,128)(2,1)} %bitcast.35), kind=kLoop, calls=%fused_computation | loop fusion | flops 3145728 | bytes 3145728 | tf_op jit(solution)/shard_map/concatenate | solution.py:203
  10.6 3.0 %collective-permute-start.9 = (bf16[64,1024]{1,0:T(8,128)(2,1)S(1)}, bf16[64,1024]{1,0:T(8,128)(2,1)S(1)}, u32[]{:S(2)}, u32[]{:S(2)}) collective-permute-start(bf16[64,1024]{1,0:T(8,128)(2,1)S(1)} %bitcast.37), channel_id=1, source_target_pairs={{0,8},{1,9},{2,10},{3,11},{4,12},{5,13},{6,14},{7,15},{8,0},{9,1},... | collective-permute-start | bytes 393224 | tf_op jit(solution)/shard_map/ppermute | solution.py:23
  13.6 1.8 %collective-permute-start.13 = (bf16[128,1024]{1,0:T(8,128)(2,1)S(1)}, bf16[128,1024]{1,0:T(8,128)(2,1)S(1)}, u32[]{:S(2)}, u32[]{:S(2)}) collective-permute-start(bf16[128,1024]{1,0:T(8,128)(2,1)S(1)} %pad_maximum_fusion.6), channel_id=1, source_target_pairs={{0,4},{1,5},{2,6},{3,7},{4,0},{5,1},{6,2},{7,3},{8,12},{9,13},{10,... | collective-permute-start | bytes 786440 | tf_op jit(solution)/shard_map/ppermute | solution.py:23
  15.4 7.0 %collective-permute-done = bf16[64,1152]{1,0:T(8,128)(2,1)S(1)} collective-permute-done((bf16[64,1152]{1,0:T(8,128)(2,1)S(1)}, bf16[64,1152]{1,0:T(8,128)(2,1)S(1)}, u32[]{:S(2)}, u32[]{:S(2)}) %collective-permute-start) | collective-permute-done | bytes 147488 | tf_op jit(solution)/shard_map/ppermute | solution.py:23
  22.6 1.5 %collective-permute-done.9 = bf16[64,1024]{1,0:T(8,128)(2,1)S(1)} collective-permute-done((bf16[64,1024]{1,0:T(8,128)(2,1)S(1)}, bf16[64,1024]{1,0:T(8,128)(2,1)S(1)}, u32[]{:S(2)}, u32[]{:S(2)}) %collective-permute-start.9) | collective-permute-done | bytes 131104 | tf_op jit(solution)/shard_map/ppermute | solution.py:23
  24.6 3.1 %collective-permute-done.13 = bf16[128,1024]{1,0:T(8,128)(2,1)S(1)} collective-permute-done((bf16[128,1024]{1,0:T(8,128)(2,1)S(1)}, bf16[128,1024]{1,0:T(8,128)(2,1)S(1)}, u32[]{:S(2)}, u32[]{:S(2)}) %collective-permute-start.13) | collective-permute-done | bytes 262176 | tf_op jit(solution)/shard_map/ppermute | solution.py:23
  27.7 1.6 %collective-permute-start.14 = (bf16[256,1024]{1,0:T(8,128)(2,1)S(1)}, bf16[256,1024]{1,0:T(8,128)(2,1)}, u32[]{:S(2)}, u32[]{:S(2)}) collective-permute-start(bf16[256,1024]{1,0:T(8,128)(2,1)S(1)} %pad_maximum_fusion.3.ca), channel_id=1, source_target_pairs={{0,2},{1,3},{2,0},{3,1},{4,6},{5,7},{6,4},{7,5},{8,10},{9,11},{10,... | collective-permute-start | bytes 1572872 | tf_op jit(solution)/shard_map/ppermute | solution.py:23
  29.3 4.7 %collective-permute-done.1 = bf16[128,1152]{1,0:T(8,128)(2,1)S(1)} collective-permute-done((bf16[128,1152]{1,0:T(8,128)(2,1)S(1)}, bf16[128,1152]{1,0:T(8,128)(2,1)S(1)}, u32[]{:S(2)}, u32[]{:S(2)}) %collective-permute-start.1) | collective-permute-done | bytes 294944 | tf_op jit(solution)/shard_map/ppermute | solution.py:23
  34.1 1.6 %collective-permute-start.2 = (bf16[256,1152]{1,0:T(8,128)(2,1)S(1)}, bf16[256,1152]{1,0:T(8,128)(2,1)}, u32[]{:S(2)}, u32[]{:S(2)}) collective-permute-start(bf16[256,1152]{1,0:T(8,128)(2,1)S(1)} %pad_maximum_fusion.1.xa.wa), channel_id=1, source_target_pairs={{0,2},{1,3},{2,0},{3,1},{4,6},{5,7},{6,4},{7,5},{8,10},{9,11},{10,... | collective-permute-start | bytes 1769480 | tf_op jit(solution)/shard_map/ppermute | solution.py:23
  35.6 3.2 %collective-permute-done.10 = bf16[128,1024]{1,0:T(8,128)(2,1)S(1)} collective-permute-done((bf16[128,1024]{1,0:T(8,128)(2,1)S(1)}, bf16[128,1024]{1,0:T(8,128)(2,1)S(1)}, u32[]{:S(2)}, u32[]{:S(2)}) %collective-permute-start.10) | collective-permute-done | bytes 262176 | tf_op jit(solution)/shard_map/ppermute | solution.py:23
  38.9 1.6 %collective-permute-start.11 = (bf16[256,1024]{1,0:T(8,128)(2,1)S(1)}, bf16[256,1024]{1,0:T(8,128)(2,1)}, u32[]{:S(2)}, u32[]{:S(2)}) collective-permute-start(bf16[256,1024]{1,0:T(8,128)(2,1)S(1)} %pad_maximum_fusion.2.xa), channel_id=1, source_target_pairs={{0,2},{1,3},{2,0},{3,1},{4,6},{5,7},{6,4},{7,5},{8,10},{9,11},{10,... | collective-permute-start | bytes 1572872 | tf_op jit(solution)/shard_map/ppermute | solution.py:23
  40.5 2.3 %collective-permute-done.14.cb = bf16[256,1024]{1,0:T(8,128)(2,1)} collective-permute-done((bf16[256,1024]{1,0:T(8,128)(2,1)S(1)}, bf16[256,1024]{1,0:T(8,128)(2,1)}, u32[]{:S(2)}, u32[]{:S(2)}) %collective-permute-start.14) | collective-permute-done | bytes 524320 | tf_op jit(solution)/shard_map/ppermute | solution.py:23
  42.8 21.4 %collective-permute-done.11.xb = bf16[256,1024]{1,0:T(8,128)(2,1)} collective-permute-done((bf16[256,1024]{1,0:T(8,128)(2,1)S(1)}, bf16[256,1024]{1,0:T(8,128)(2,1)}, u32[]{:S(2)}, u32[]{:S(2)}) %collective-permute-start.11) | collective-permute-done | bytes 524320 | tf_op jit(solution)/shard_map/ppermute | solution.py:23
  64.2 8.8 %shard_map.114 = (bf16[256,1024]{1,0:T(8,128)(2,1)S(1)}, f32[256,1024]{1,0:T(8,128)}) custom-call(s32[1]{0:T(128)} %bitcast.1.me_ref, bf16[256,1152]{1,0:T(8,128)(2,1)S(1)} %pad_maximum_fusion.1.xa.wa, bf16[256,1152]{1,0:T(8,128)(2,1)} %collective-permute-done.2.xb.wb, bf16[256,1024]{1,0:T(8,128)(2,1)S(1)} %pad_maximum_fusion.2.xa, ...), custom_call_target="tpu_custom_call" | custom-call | flops 4026531840 | bytes 9568260 | tf_op jit(solution)/shard_map/pallas_call | solution.py:160
  73.0 1.5 %collective-permute-start.15 = (bf16[256,1024]{1,0:T(8,128)(2,1)S(1)}, bf16[256,1024]{1,0:T(8,128)(2,1)S(1)}, u32[]{:S(2)}, u32[]{:S(2)}) collective-permute-start(bf16[256,1024]{1,0:T(8,128)(2,1)S(1)} %get-tuple-element.9), channel_id=1, source_target_pairs={{0,2},{1,3},{2,0},{3,1},{4,6},{5,7},{6,4},{7,5},{8,10},{9,11},{10,... | collective-permute-start | bytes 1572872 | tf_op jit(solution)/shard_map/ppermute | solution.py:23
  74.5 5.6 %shard_map.113 = (bf16[256,1024]{1,0:T(8,128)(2,1)S(1)}, f32[256,1024]{1,0:T(8,128)S(1)}) custom-call(s32[1]{0:T(128)} %bitcast.1.me_ref, bf16[256,1152]{1,0:T(8,128)(2,1)S(1)} %pad_maximum_fusion.1.xa.wa, bf16[256,1152]{1,0:T(8,128)(2,1)} %collective-permute-done.2.xb.wb, bf16[1024,768]{1,0:T(8,128)(2,1)S(1)} %copy-done.1, bf16[384,1024]{1,0:T(8,128)(2,1)} %bitcast.8.d0, ...), custom_call_target="tpu_custom_call" | custom-call | flops 2415919104 | bytes 7471108 | tf_op jit(solution)/shard_map/pallas_call | solution.py:160
  80.7 7.2 %collective-permute-done.15 = bf16[256,1024]{1,0:T(8,128)(2,1)S(1)} collective-permute-done((bf16[256,1024]{1,0:T(8,128)(2,1)S(1)}, bf16[256,1024]{1,0:T(8,128)(2,1)S(1)}, u32[]{:S(2)}, u32[]{:S(2)}) %collective-permute-start.15) | collective-permute-done | bytes 524320 | tf_op jit(solution)/shard_map/ppermute | solution.py:23
  88.2 7.5 %collective-permute-done.5 = bf16[256,1024]{1,0:T(8,128)(2,1)S(1)} collective-permute-done((bf16[256,1024]{1,0:T(8,128)(2,1)S(1)}, bf16[256,1024]{1,0:T(8,128)(2,1)S(1)}, u32[]{:S(2)}, u32[]{:S(2)}) %collective-permute-start.5) | collective-permute-done | bytes 524320 | tf_op jit(solution)/shard_map/ppermute | solution.py:23
  96.1 5.7 %collective-permute-start.17 = (bf16[64,1024]{1,0:T(8,128)(2,1)S(1)}, bf16[64,1024]{1,0:T(8,128)(2,1)S(1)}, u32[]{:S(2)}, u32[]{:S(2)}) collective-permute-start(bf16[64,1024]{1,0:T(8,128)(2,1)S(1)} %slice.66), channel_id=1, source_target_pairs={{0,8},{1,9},{2,10},{3,11},{4,12},{5,13},{6,14},{7,15},{8,0},{9,1},... | collective-permute-start | bytes 393224 | tf_op jit(solution)/shard_map/ppermute | solution.py:23
  101.8 4.2 %collective-permute-done.6 = bf16[128,1024]{1,0:T(8,128)(2,1)S(1)} collective-permute-done((bf16[128,1024]{1,0:T(8,128)(2,1)S(1)}, bf16[128,1024]{1,0:T(8,128)(2,1)S(1)}, u32[]{:S(2)}, u32[]{:S(2)}) %collective-permute-start.6) | collective-permute-done | bytes 262176 | tf_op jit(solution)/shard_map/ppermute | solution.py:23
  106.1 1.2 collective-permute-start.7
  107.4 1.6 %collective-permute-start.18 = (bf16[1,64,1024]{2,1,0:T(8,128)(2,1)S(1)}, bf16[1,64,1024]{2,1,0:T(8,128)(2,1)S(1)}, u32[]{:S(2)}, u32[]{:S(2)}) collective-permute-start(bf16[1,64,1024]{2,1,0:T(8,128)(2,1)S(1)} %fusion.5), channel_id=1, source_target_pairs={{16,0},{0,16},{17,1},{1,17},{18,2},{2,18},{19,3},{3,19},{20,4},{4,... | collective-permute-start | bytes 393224 | tf_op jit(solution)/shard_map/ppermute | solution.py:19
  109.0 4.5 %collective-permute-done.7 = bf16[64,1024]{1,0:T(8,128)(2,1)S(1)} collective-permute-done((bf16[64,1024]{1,0:T(8,128)(2,1)S(1)}, bf16[64,1024]{1,0:T(8,128)(2,1)S(1)}, u32[]{:S(2)}, u32[]{:S(2)}) %collective-permute-start.7) | collective-permute-done | bytes 131104 | tf_op jit(solution)/shard_map/ppermute | solution.py:23
  113.5 1.6 %collective-permute-start.8 = (bf16[1,64,1024]{2,1,0:T(8,128)(2,1)S(1)}, bf16[1,64,1024]{2,1,0:T(8,128)(2,1)S(1)}, u32[]{:S(2)}, u32[]{:S(2)}) collective-permute-start(bf16[1,64,1024]{2,1,0:T(8,128)(2,1)S(1)} %fusion.4), channel_id=1, source_target_pairs={{16,0},{0,16},{17,1},{1,17},{18,2},{2,18},{19,3},{3,19},{20,4},{4,... | collective-permute-start | bytes 393224 | tf_op jit(solution)/shard_map/ppermute | solution.py:19
  115.1 3.4 %collective-permute-done.8 = bf16[1,64,1024]{2,1,0:T(8,128)(2,1)S(1)} collective-permute-done((bf16[1,64,1024]{2,1,0:T(8,128)(2,1)S(1)}, bf16[1,64,1024]{2,1,0:T(8,128)(2,1)S(1)}, u32[]{:S(2)}, u32[]{:S(2)}) %collective-permute-start.8) | collective-permute-done | bytes 131104 | tf_op jit(solution)/shard_map/ppermute | solution.py:19
  118.6 0.7 copy.22
  (47 shorter events, 3.2 us)
Async XLA Ops:
  0.6 13.0 %collective-permute-start.12 = (bf16[64,1024]{1,0:T(8,128)(2,1)}, bf16[64,1024]{1,0:T(8,128)(2,1)S(1)}, u32[]{:S(2)}, u32[]{:S(2)}) collective-permute-start(bf16[64,1024]{1,0:T(8,128)(2,1)} %bitcast.31), channel_id=1, source_target_pairs={{0,8},{1,9},{2,10},{3,11},{4,12},{5,13},{6,14},{7,15},{8,0},{9,1},... | collective-permute-start | bytes 393224 | tf_op jit(solution)/shard_map/ppermute | solution.py:23
  8.9 13.5 %collective-permute-start = (bf16[64,1152]{1,0:T(8,128)(2,1)S(1)}, bf16[64,1152]{1,0:T(8,128)(2,1)S(1)}, u32[]{:S(2)}, u32[]{:S(2)}) collective-permute-start(bf16[64,1152]{1,0:T(8,128)(2,1)S(1)} %concatenate.27), channel_id=1, source_target_pairs={{0,8},{1,9},{2,10},{3,11},{4,12},{5,13},{6,14},{7,15},{8,0},{9,1},... | collective-permute-start | bytes 442376 | tf_op jit(solution)/shard_map/ppermute | solution.py:23
  9.0 1.7 %copy-start.5 = (bf16[1,64,1024]{2,1,0:T(8,128)(2,1)S(1)}, bf16[1,64,1024]{2,1,0:T(8,128)(2,1)}, u32[]{:S(2)}) copy-start(bf16[1,64,1024]{2,1,0:T(8,128)(2,1)} %param.13) | copy-start | bytes 393220
  9.0 4.6 %copy-start.2 = (bf16[1,64,1024]{2,1,0:T(8,128)(2,1)S(1)}, bf16[1,64,1024]{2,1,0:T(8,128)(2,1)}, u32[]{:S(2)}) copy-start(bf16[1,64,1024]{2,1,0:T(8,128)(2,1)} %param.16) | copy-start | bytes 393220
  10.5 23.5 %copy-start = (bf16[1024,768]{1,0:T(8,128)(2,1)}, bf16[1024,768]{1,0:T(8,128)(2,1)S(1)}, u32[]{:S(2)}) copy-start(bf16[1024,768]{1,0:T(8,128)(2,1)S(1)} %pad_maximum_fusion.gu0) | copy-start | bytes 4718596
  10.6 53.6 %collective-permute-start.3 = (bf16[1024,768]{1,0:T(8,128)(2,1)S(1)}, bf16[1024,768]{1,0:T(8,128)(2,1)}, u32[]{:S(2)}, u32[]{:S(2)}) collective-permute-start(bf16[1024,768]{1,0:T(8,128)(2,1)S(1)} %pad_maximum_fusion.gu0), channel_id=1, source_target_pairs={{0,1},{1,0},{2,3},{3,2},{4,5},{5,4},{6,7},{7,6},{8,9},{9,8},{10,11... | collective-permute-start | bytes 4718600 | tf_op jit(solution)/shard_map/ppermute | solution.py:23
  10.6 13.4 %collective-permute-start.9 = (bf16[64,1024]{1,0:T(8,128)(2,1)S(1)}, bf16[64,1024]{1,0:T(8,128)(2,1)S(1)}, u32[]{:S(2)}, u32[]{:S(2)}) collective-permute-start(bf16[64,1024]{1,0:T(8,128)(2,1)S(1)} %bitcast.37), channel_id=1, source_target_pairs={{0,8},{1,9},{2,10},{3,11},{4,12},{5,13},{6,14},{7,15},{8,0},{9,1},... | collective-permute-start | bytes 393224 | tf_op jit(solution)/shard_map/ppermute | solution.py:23
  13.6 14.1 %collective-permute-start.13 = (bf16[128,1024]{1,0:T(8,128)(2,1)S(1)}, bf16[128,1024]{1,0:T(8,128)(2,1)S(1)}, u32[]{:S(2)}, u32[]{:S(2)}) collective-permute-start(bf16[128,1024]{1,0:T(8,128)(2,1)S(1)} %pad_maximum_fusion.6), channel_id=1, source_target_pairs={{0,4},{1,5},{2,6},{3,7},{4,0},{5,1},{6,2},{7,3},{8,12},{9,13},{10,... | collective-permute-start | bytes 786440 | tf_op jit(solution)/shard_map/ppermute | solution.py:23
  22.4 11.6 %collective-permute-start.1 = (bf16[128,1152]{1,0:T(8,128)(2,1)S(1)}, bf16[128,1152]{1,0:T(8,128)(2,1)S(1)}, u32[]{:S(2)}, u32[]{:S(2)}) collective-permute-start(bf16[128,1152]{1,0:T(8,128)(2,1)S(1)} %pad_maximum_fusion.4), channel_id=1, source_target_pairs={{0,4},{1,5},{2,6},{3,7},{4,0},{5,1},{6,2},{7,3},{8,12},{9,13},{10,... | collective-permute-start | bytes 884744 | tf_op jit(solution)/shard_map/ppermute | solution.py:23
  22.5 17.9 %collective-permute-start.4 = (bf16[384,1024]{1,0:T(8,128)(2,1)}, bf16[384,1024]{1,0:T(8,128)(2,1)}, u32[]{:S(2)}, u32[]{:S(2)}) collective-permute-start(bf16[384,1024]{1,0:T(8,128)(2,1)} %bitcast.8.d0), channel_id=1, source_target_pairs={{0,1},{1,0},{2,3},{3,2},{4,5},{5,4},{6,7},{7,6},{8,9},{9,8},{10,11... | collective-permute-start | bytes 2359304 | tf_op jit(solution)/shard_map/ppermute | solution.py:23
  24.1 14.8 %collective-permute-start.10 = (bf16[128,1024]{1,0:T(8,128)(2,1)S(1)}, bf16[128,1024]{1,0:T(8,128)(2,1)S(1)}, u32[]{:S(2)}, u32[]{:S(2)}) collective-permute-start(bf16[128,1024]{1,0:T(8,128)(2,1)S(1)} %pad_maximum_fusion.5), channel_id=1, source_target_pairs={{0,4},{1,5},{2,6},{3,7},{4,0},{5,1},{6,2},{7,3},{8,12},{9,13},{10,... | collective-permute-start | bytes 786440 | tf_op jit(solution)/shard_map/ppermute | solution.py:23
  27.7 15.0 %collective-permute-start.14 = (bf16[256,1024]{1,0:T(8,128)(2,1)S(1)}, bf16[256,1024]{1,0:T(8,128)(2,1)}, u32[]{:S(2)}, u32[]{:S(2)}) collective-permute-start(bf16[256,1024]{1,0:T(8,128)(2,1)S(1)} %pad_maximum_fusion.3.ca), channel_id=1, source_target_pairs={{0,2},{1,3},{2,0},{3,1},{4,6},{5,7},{6,4},{7,5},{8,10},{9,11},{10,... | collective-permute-start | bytes 1572872 | tf_op jit(solution)/shard_map/ppermute | solution.py:23
  34.1 30.1 %collective-permute-start.2 = (bf16[256,1152]{1,0:T(8,128)(2,1)S(1)}, bf16[256,1152]{1,0:T(8,128)(2,1)}, u32[]{:S(2)}, u32[]{:S(2)}) collective-permute-start(bf16[256,1152]{1,0:T(8,128)(2,1)S(1)} %pad_maximum_fusion.1.xa.wa), channel_id=1, source_target_pairs={{0,2},{1,3},{2,0},{3,1},{4,6},{5,7},{6,4},{7,5},{8,10},{9,11},{10,... | collective-permute-start | bytes 1769480 | tf_op jit(solution)/shard_map/ppermute | solution.py:23
  38.9 25.3 %collective-permute-start.11 = (bf16[256,1024]{1,0:T(8,128)(2,1)S(1)}, bf16[256,1024]{1,0:T(8,128)(2,1)}, u32[]{:S(2)}, u32[]{:S(2)}) collective-permute-start(bf16[256,1024]{1,0:T(8,128)(2,1)S(1)} %pad_maximum_fusion.2.xa), channel_id=1, source_target_pairs={{0,2},{1,3},{2,0},{3,1},{4,6},{5,7},{6,4},{7,5},{8,10},{9,11},{10,... | collective-permute-start | bytes 1572872 | tf_op jit(solution)/shard_map/ppermute | solution.py:23
  64.2 10.4 %copy-start.1 = (bf16[1024,768]{1,0:T(8,128)(2,1)S(1)}, bf16[1024,768]{1,0:T(8,128)(2,1)}, u32[]{:S(2)}) copy-start(bf16[1024,768]{1,0:T(8,128)(2,1)} %copy-done) | copy-start | bytes 4718596
  73.0 14.9 %copy-start.3 = (f32[256,1024]{1,0:T(8,128)S(1)}, f32[256,1024]{1,0:T(8,128)}, u32[]{:S(2)}) copy-start(f32[256,1024]{1,0:T(8,128)} %get-tuple-element.8) | copy-start | bytes 3145732
  73.0 14.9 %collective-permute-start.15 = (bf16[256,1024]{1,0:T(8,128)(2,1)S(1)}, bf16[256,1024]{1,0:T(8,128)(2,1)S(1)}, u32[]{:S(2)}, u32[]{:S(2)}) collective-permute-start(bf16[256,1024]{1,0:T(8,128)(2,1)S(1)} %get-tuple-element.9), channel_id=1, source_target_pairs={{0,2},{1,3},{2,0},{3,1},{4,6},{5,7},{6,4},{7,5},{8,10},{9,11},{10,... | collective-permute-start | bytes 1572872 | tf_op jit(solution)/shard_map/ppermute | solution.py:23
  80.1 15.6 %collective-permute-start.5 = (bf16[256,1024]{1,0:T(8,128)(2,1)S(1)}, bf16[256,1024]{1,0:T(8,128)(2,1)S(1)}, u32[]{:S(2)}, u32[]{:S(2)}) collective-permute-start(bf16[256,1024]{1,0:T(8,128)(2,1)S(1)} %get-tuple-element.7), channel_id=1, source_target_pairs={{0,2},{1,3},{2,0},{3,1},{4,6},{5,7},{6,4},{7,5},{8,10},{9,11},{10,... | collective-permute-start | bytes 1572872 | tf_op jit(solution)/shard_map/ppermute | solution.py:23
  88.1 7.9 %collective-permute-start.16 = (bf16[128,1024]{1,0:T(8,128)(2,1)S(1)}, bf16[128,1024]{1,0:T(8,128)(2,1)S(1)}, u32[]{:S(2)}, u32[]{:S(2)}) collective-permute-start(bf16[128,1024]{1,0:T(8,128)(2,1)S(1)} %slice.64), channel_id=1, source_target_pairs={{0,4},{1,5},{2,6},{3,7},{4,0},{5,1},{6,2},{7,3},{8,12},{9,13},{10,... | collective-permute-start | bytes 786440 | tf_op jit(solution)/shard_map/ppermute | solution.py:23
  95.9 10.2 %collective-permute-start.6 = (bf16[128,1024]{1,0:T(8,128)(2,1)S(1)}, bf16[128,1024]{1,0:T(8,128)(2,1)S(1)}, u32[]{:S(2)}, u32[]{:S(2)}) collective-permute-start(bf16[128,1024]{1,0:T(8,128)(2,1)S(1)} %slice.65), channel_id=1, source_target_pairs={{0,4},{1,5},{2,6},{3,7},{4,0},{5,1},{6,2},{7,3},{8,12},{9,13},{10,... | collective-permute-start | bytes 786440 | tf_op jit(solution)/shard_map/ppermute | solution.py:23
  96.1 17.4 %copy-start.4 = (bf16[1,64,1024]{2,1,0:T(8,128)(2,1)S(1)}, bf16[1,64,1024]{2,1,0:T(8,128)(2,1)}, u32[]{:S(2)}) copy-start(bf16[1,64,1024]{2,1,0:T(8,128)(2,1)} %param.10) | copy-start | bytes 393220
  96.1 11.2 %collective-permute-start.17 = (bf16[64,1024]{1,0:T(8,128)(2,1)S(1)}, bf16[64,1024]{1,0:T(8,128)(2,1)S(1)}, u32[]{:S(2)}, u32[]{:S(2)}) collective-permute-start(bf16[64,1024]{1,0:T(8,128)(2,1)S(1)} %slice.66), channel_id=1, source_target_pairs={{0,8},{1,9},{2,10},{3,11},{4,12},{5,13},{6,14},{7,15},{8,0},{9,1},... | collective-permute-start | bytes 393224 | tf_op jit(solution)/shard_map/ppermute | solution.py:23
  106.1 7.3 %collective-permute-start.7 = (bf16[64,1024]{1,0:T(8,128)(2,1)S(1)}, bf16[64,1024]{1,0:T(8,128)(2,1)S(1)}, u32[]{:S(2)}, u32[]{:S(2)}) collective-permute-start(bf16[64,1024]{1,0:T(8,128)(2,1)S(1)} %slice.67), channel_id=1, source_target_pairs={{0,8},{1,9},{2,10},{3,11},{4,12},{5,13},{6,14},{7,15},{8,0},{9,1},... | collective-permute-start | bytes 393224 | tf_op jit(solution)/shard_map/ppermute | solution.py:23
  107.4 7.8 %collective-permute-start.18 = (bf16[1,64,1024]{2,1,0:T(8,128)(2,1)S(1)}, bf16[1,64,1024]{2,1,0:T(8,128)(2,1)S(1)}, u32[]{:S(2)}, u32[]{:S(2)}) collective-permute-start(bf16[1,64,1024]{2,1,0:T(8,128)(2,1)S(1)} %fusion.5), channel_id=1, source_target_pairs={{16,0},{0,16},{17,1},{1,17},{18,2},{2,18},{19,3},{3,19},{20,4},{4,... | collective-permute-start | bytes 393224 | tf_op jit(solution)/shard_map/ppermute | solution.py:19
  113.5 5.0 %collective-permute-start.8 = (bf16[1,64,1024]{2,1,0:T(8,128)(2,1)S(1)}, bf16[1,64,1024]{2,1,0:T(8,128)(2,1)S(1)}, u32[]{:S(2)}, u32[]{:S(2)}) collective-permute-start(bf16[1,64,1024]{2,1,0:T(8,128)(2,1)S(1)} %fusion.4), channel_id=1, source_target_pairs={{16,0},{0,16},{17,1},{1,17},{18,2},{2,18},{19,3},{3,19},{20,4},{4,... | collective-permute-start | bytes 393224 | tf_op jit(solution)/shard_map/ppermute | solution.py:19

commit v2 on v0

v2 whole, which is shorter than its diff:
```python
import functools

import jax
import jax.numpy as jnp
from jax import lax
from jax.experimental import pallas as pl
from jax.experimental.pallas import tpu as pltpu
from jax.sharding import PartitionSpec as P

F32 = jnp.float32
BF16 = jnp.bfloat16
LANES = 128
VMEM_LIMIT = 48 * 1024 * 1024
COST = 0.1
IN_TURN = "f,Fs,F,Fk,F,b:Fk,c:Fk,Bs,B,Bk,B"
JOIN = False
HBM = True
GU = 1
LITTLE = pl.CostEstimate(flops=1, bytes_accessed=1, transcendentals=0)
PLAN = dict(f="P", b="P", c="P", rf="P", rb="P", odd="QQ", cut="", ops="f,c,b,f,c,b,f,c,b,Fs,F,Fk,Bs,B,F,Bk:F0,B,F,B", step=4)


def passed_along(block, distance, paths, bit=0):
    sections, experts = lax.axis_size("section"), lax.axis_size("expert")
    route = [
        (s * experts + e, (s + distance) % sections * experts + (e ^ paths[e % 2].get(bit, 0)))
        for s in range(sections)
        for e in range(experts)
    ]
    return lax.ppermute(block, ("section", "expert"), route)


def swapped(block, paths, bit):
    route = [(i, i ^ paths[i % 2][bit]) for i in range(lax.axis_size("expert"))]
    return lax.ppermute(block, "expert", route)


class Spread:
    def __init__(self, block, paths, bits, cut):
        self.paths, self.bits, self.cut, self.came, self.held, self.order = paths, bits, cut, [], block, [0]
        self.parts, self.orders = [], []

    def done(self):
        return len(self.came) == len(self.bits) + self.cut

    def step(self, after=()):
        at, last = len(self.came), len(self.bits) - 1
        bit = self.bits[min(at, last)]
        if at <= last:
            parts = [self.held] + ([self.came[-1]] if 0 < at and (at < last or not self.cut) else [])
            parts = behind(parts, after)
            if len(parts) > 1:
                self.held = joined(parts, 0) if JOIN else jnp.concatenate(parts, axis=0)
                self.order = self.order + [r | self.bits[at - 1] for r in self.order]
            else:
                self.held = parts[0]
            payload, order = self.held, self.order
        else:
            (payload,) = behind([self.came[last - 1]], after)
            order = [r | self.bits[last - 1] for r in self.order]
        self.came.append(swapped(payload, self.paths, bit))
        if at >= last:
            self.parts += [payload, self.came[-1]]
            self.orders += [order, [r | bit for r in order]]


def behind(arrays, others):
    if not others:
        return list(arrays)
    return list(lax.optimization_barrier((*arrays, *others))[: len(arrays)])


def joining_kernel(axis, *refs):
    *parts, out_ref, sems = refs
    at, copies = 0, []
    for number, part in enumerate(parts):
        here = [slice(None)] * 2
        here[axis] = pl.ds(at, part.shape[axis])
        copies.append(pltpu.make_async_copy(part, out_ref.at[tuple(here)], sems.at[number]))
        copies[-1].start()
        at += part.shape[axis]
    for copy in copies:
        copy.wait()


def joined(parts, axis):
    shape = list(parts[0].shape)
    shape[axis] = sum(part.shape[axis] for part in parts)
    return pl.pallas_call(
        functools.partial(joining_kernel, axis),
        out_shape=jax.ShapeDtypeStruct(tuple(shape), parts[0].dtype),
        in_specs=[pl.BlockSpec(memory_space=pl.ANY)] * len(parts),
        out_specs=pl.BlockSpec(memory_space=pltpu.VMEM),
        scratch_shapes=[pltpu.SemaphoreType.DMA((len(parts),))],
        cost_estimate=LITTLE,
    )(*parts)


def halving_order(bits):
    order = [0]
    for bit in reversed(bits):
        order = [r | bit for r in order] + order
    return order


class Return:
    def __init__(self, sends, paths, bits, distance):
        self.sends, self.keep, self.came = sends, None, []
        self.paths, self.bits, self.distance = paths, bits, distance

    def done(self):
        return len(self.came) == len(self.bits) + len(self.sends)

    def step(self, after=()):
        at, first = len(self.came), len(self.sends)
        if at < first:
            (send,) = behind([self.sends[at]], after)
            self.came.append(swapped(send, self.paths, self.bits[0]))
            return
        if at == first and first == 2:
            half = self.keep.shape[0] // 2
            send, self.keep = self.keep[:half] + self.came[0].astype(F32), self.keep[half:]
        else:
            total = self.keep + self.came[-1].astype(F32)
            if at == 3 and first == 2:
                total = total + self.came[1].astype(F32)
            half = total.shape[0] // 2
            send, self.keep = total[:half], total[half:]
        bit = self.bits[at - first + 1]
        if bit != self.bits[-1]:
            (send,) = behind([send.astype(BF16)], after)
            self.came.append(swapped(send, self.paths, bit))
        else:
            send, keep = behind([send.astype(BF16), self.keep.astype(BF16)], after)
            self.came.append(passed_along(keep, self.distance, self.paths))
            self.came.append(passed_along(send, self.distance, self.paths, bit))


def packing_kernel(x_ref, route_f, gate_f, route_b, gate_b, out_ref):
    width, extra = x_ref.shape[1], out_ref.shape[1] - x_ref.shape[1]
    out_ref[:, :width] = x_ref[...]
    pieces = []
    for route_ref, gate_ref in ((route_f, gate_f), (route_b, gate_b)):
        pieces.append(route_ref[...].astype(F32))
        rest = gate_ref[...]
        for _ in range(3):
            pieces.append(rest.astype(BF16).astype(F32))
            rest = rest - pieces[-1]
    used = sum(piece.shape[0] for piece in pieces)
    if extra > used:
        pieces.append(jnp.zeros((extra - used, x_ref.shape[0]), F32))
    out_ref[:, width:] = jnp.transpose(jnp.concatenate(pieces, axis=0)).astype(BF16)


def packed(rows, *words):
    length, width = rows.shape
    extra = 8 * words[0].shape[1]
    return pl.pallas_call(
        packing_kernel,
        out_shape=jax.ShapeDtypeStruct((length, width + extra + -extra % LANES), BF16),
        cost_estimate=LITTLE,
    )(rows, *[jnp.transpose(array) for array in words])


def gate_of(words, topk, first, expert):
    words = words.astype(F32)
    at = [words[:, (first + j) * topk : (first + j + 1) * topk] for j in range(4)]
    gates = at[1] + at[2] + at[3]
    chosen = at[0] == expert.astype(F32)
    return jnp.sum(jnp.where(chosen, gates, 0.0), axis=1, keepdims=True)


def times(a, b):
    return lax.dot_general(a, b, (((1,), (0,)), ((), ())), preferred_element_type=F32)


def times_transposed(a, b):
    return lax.dot_general(a, b, (((1,), (1,)), ((), ())), preferred_element_type=F32)


def forward_rows(x, gate_up, down):
    pre = times(x, gate_up[...])
    width = pre.shape[1] // 2
    gate, up = pre[:, :width], pre[:, width:]
    hidden = (gate * jax.nn.sigmoid(gate) * up).astype(BF16)
    return times(hidden, down[...])


def backward_rows(x, cot, gate_up, down):
    pre = times(x, gate_up[...])
    width = pre.shape[1] // 2
    gate, up = pre[:, :width], pre[:, width:]
    sig = jax.nn.sigmoid(gate)
    d_hidden = times_transposed(cot, down[...])
    d_gate = d_hidden * up * sig * (1.0 + gate * (1.0 - sig))
    d_up = d_hidden * gate * sig
    both = jnp.concatenate([d_gate.astype(BF16), d_up.astype(BF16)], axis=1)
    return times_transposed(both, gate_up[...])


def expert_kernel(each, topk, first, rows, step, copies, me_ref, *refs):
    count = 1 + max(operand for each_copy in copies for operand, *_ in each_copy)
    buffers, sems = refs[-1 - len(copies) : -1], refs[-1]
    out_refs = refs[count : -1 - len(copies)]
    started = []
    for buffer, pieces in zip(buffers, copies, strict=True):
        row, group = 0, []
        for operand, at, length, column in pieces:
            copy = pltpu.make_async_copy(
                refs[operand].at[pl.ds(at, length), pl.ds(column, buffer.shape[1])],
                buffer.at[pl.ds(row, length), :],
                sems.at[sum(map(len, started)) + len(group)],
            )
            copy.start()
            group.append(copy)
            row += length
        started.append(group)

    def ready(number):
        for copy in started[number]:
            copy.wait()
        started[number] = []
        return buffers[number]

    inputs = len(copies) - 5
    length = out_refs[0].shape[0]
    total_rows = buffers[0].shape[0]
    totals = {}
    for flip in range(2):
        for start in range(0, total_rows, step * rows):
            tile = pl.ds(start, min(step * rows, total_rows - start))
            taken = [ready(number)[tile, :] for number in range(inputs)]
            gate_up, down = ready(inputs + 2 * flip), ready(inputs + 2 * flip + 1)
            out = each(*taken, gate_up, down).astype(BF16).astype(F32)
            out = out * gate_of(ready(len(copies) - 1)[tile, :], topk, first, me_ref[0] ^ flip)
            if flip == 0:
                totals[start] = out
                continue
            out = (totals[start] + out).astype(out_refs[0].dtype)
            for at in range(0, out.shape[0], rows):
                number, row = divmod(start + at, length)
                out_refs[number][pl.ds(row, rows), :] = out[at : at + rows]


def weighted(each, first, topk, rows, step, wanted, dtype, outputs, place, words, inputs, weights):
    width, hidden_width = weights[1].shape[1], weights[1].shape[0]
    operands, copies, scratch = [], [], []
    length = len(wanted) * rows

    def operand(array):
        for number, other in enumerate(operands):
            if other is array:
                return number
        operands.append(array)
        return len(operands) - 1

    def rows_from(parts, orders, columns, column):
        pieces = []
        for r in wanted:
            part, block = next((n, o.index(r)) for n, o in enumerate(orders) if r in o)
            number, at = operand(parts[part]), block * rows
            if pieces and pieces[-1][0] == number and pieces[-1][1] + pieces[-1][2] == at:
                pieces[-1] = (number, pieces[-1][1], pieces[-1][2] + rows, column)
            else:
                pieces.append((number, at, rows, column))
        copies.append(pieces)
        scratch.append(pltpu.VMEM((length, columns), BF16))

    for parts, orders in inputs:
        rows_from(parts, orders, width, 0)
    for array in weights:
        copies.append([(operand(array), 0, array.shape[0], 0)])
        scratch.append(pltpu.VMEM(array.shape, BF16))
    rows_from(*words, width)
    return pl.pallas_call(
        functools.partial(expert_kernel, each, topk, first, rows, step, copies),
        out_shape=[jax.ShapeDtypeStruct((length // outputs, width), dtype)] * outputs,
        in_specs=[pl.BlockSpec(memory_space=pltpu.SMEM)]
        + [pl.BlockSpec(memory_space=pltpu.HBM if HBM else pl.ANY)] * len(operands),
        out_specs=[pl.BlockSpec(memory_space=pltpu.VMEM)] * outputs,
        scratch_shapes=scratch + [pltpu.SemaphoreType.DMA((sum(map(len, copies)),))],
        compiler_params=pltpu.CompilerParams(vmem_limit_bytes=VMEM_LIMIT),
        cost_estimate=pl.CostEstimate(
            flops=int(COST * 4 * (2 * len(inputs) + 1) * length * width * hidden_width),
            bytes_accessed=int(COST * sum(a.size * a.dtype.itemsize for a in operands)),
            transcendentals=0,
        ),
    )(place, *operands)


def on_device(
    x_forward,
    route_forward,
    gate_forward,
    x_backward,
    route_backward,
    gate_backward,
    cotangent,
    w_gate,
    w_up,
    w_down,
):
    experts = lax.axis_size("expert")
    rows, width = x_forward.shape[1:]
    topk = route_forward.shape[2]
    me = lax.axis_index("expert").astype(jnp.int32)

    bits = []
    while 2 << len(bits) < experts:
        bits.insert(0, 2 << len(bits))
    blocks = experts // 2
    orders = {
        "P": bits,
        "Q": bits[:-2] + [bits[-1], bits[-2]],
        "R": bits[-1:] + bits[:-1],
    }
    plan = PLAN
    even = dict(zip(bits, bits))
    odd = {kind: dict(zip(bits, orders[plan["odd"][kind != "f"]])) for kind in "fbc"}
    paths = {kind: (even, odd[kind]) for kind in "fbc"}

    arrays = {"f": x_forward[0], "b": x_backward[0], "c": cotangent[0]}
    words = [route_forward[0], gate_forward[0], route_backward[0], gate_backward[0]]
    held = {}

    arrays["f"] = packed(arrays["f"], *words)
    down0 = w_down[0, 0]
    pair = [w_gate[0, 0], w_up[0, 0]]
    if GU:
        *pair, down0 = behind([*pair, down0], [arrays["f"]])
    gate_up0 = jnp.concatenate(pair, axis=1)
    chip = [{1: 1}] * 2
    gate_up1, down1 = swapped(gate_up0, chip, 1), swapped(down0, chip, 1)
    weights = [gate_up0, down0, gate_up1, down1]

    step = min(plan["step"], blocks // 2)
    place = jnp.reshape(me, (1,))

    class Far:
        came = [passed_along(x_forward[0], 1, [{}, {}]), passed_along(cotangent[0], -1, [{}, {}])]

    held["y"] = Far

    def arrived(far, kind):
        one, other = held[kind].came[-2:]
        return (far.astype(F32) + (one.astype(F32) + other.astype(F32))).astype(BF16)[None]

    outs = {}
    items = (plan["ops"] if len(bits) < 4 else IN_TURN).split(",")
    left = {name: [item[0] for item in items if item[1:2] not in ("s", "k")].count(name) for name in "fbcFB"}
    for item in items:
        name, _, after = item.partition(":")
        after = [
            outs[other] if other in outs else held[other[0]].came[int(other[1])]
            for other in after.split()
        ]
        kind = name[0].lower()
        if len(name) == 1:
            if name not in held:
                held[name] = Spread(arrays[name], paths[kind], orders[plan[name]], name in plan["cut"])
            held[name].step(after)
            left[name] -= 1
            while left[name] == 0 and not held[name].done():
                held[name].step()
            continue
        back = orders[plan["r" + kind]][::-1]
        order = halving_order(back)
        takes = [(held[other].parts, held[other].orders) for other in ("f" if kind == "f" else "bc")]
        carrier = (held["f"].parts, held["f"].orders, held["f"].held.shape[1] - width)
        each, first = (forward_rows, 0) if kind == "f" else (backward_rows, 4)
        half = len(order) // 2
        sent = name[1] == "s"
        wanted, dtype = (order[:half], BF16) if sent else (order[half:], F32)
        (place,) = behind([place], after)
        number = 2 if sent and name[0] in plan["cut"] else 1
        out = weighted(
            each, first, topk, rows, step, wanted, dtype, number, place, carrier, takes, weights
        )
        place, *out = lax.optimization_barrier((place, *out))
        outs[name] = out[0]
        if sent:
            held[name[0]] = Return(out, paths[kind], back, 1 if kind == "f" else -1)
        else:
            held[name[0]].keep = out[0]

    return arrived(held["y"].came[0], "F"), arrived(held["y"].came[1], "B")


def solution(mesh):
    in_specs = (
        P("section", "expert", None),
        P("section", "expert", None),
        P("section", "expert", None),
        P("section", "expert", None),
        P("section", "expert", None),
        P("section", "expert", None),
        P("section", "expert", None),
        P("section", "expert", None, None),
        P("section", "expert", None, None),
        P("section", "expert", None, None),
    )
    out_specs = (P("section", "expert", None), P("section", "expert", None))
    return jax.shard_map(
        on_device, mesh=mesh, in_specs=in_specs, out_specs=out_specs, check_vma=False
    )
```

time: 198 us -> 87.6 us (0.44); the launches traced: 195 us -> 87.4 us
  waiting for transfers between devices: 89.4 us -> 35.2 us
  matrix products: 27.6 us -> 0 us
  local copies, waits for them, and re-layouts: 24.4 us -> 1.55 us
  Pallas kernels: 0 us -> 21.2 us
  starting transfers between devices: 42.7 us -> 24.1 us
  other arithmetic: 10.5 us -> 4.48 us
    all_to_all x5 -> x0, waiting for transfers between devices: 84.7 us -> none  [the longest x1 25.7 us: on_device(): lax.all_to_all(send_xb, 'expert', split_axis=0, concat_axis=0, tiled=True)]
    all_to_all x5 -> x0, starting transfers between devices: 39.6 us -> none  [the longest x1 8.06 us: on_device(): lax.all_to_all(send_x, 'expert', split_axis=0, concat_axis=0, tiled=True)]
    ppermute x2 -> x21, waiting for transfers between devices: 4.65 us -> 35.2 us  [the longest x15 30.5 us: swapped(): return lax.ppermute(block, 'expert', route)]
    dot_general x11 -> x0, matrix products: 27.6 us -> none  [the longest x1 4.33 us: expert_backward(): lax.dot_general(d_gate, gate_mat, (((1,), (1,)), ((), ())), preferred_ele...]
    pallas_call x0 -> x5, Pallas kernels: none -> 21.2 us  [the longest x4 19.4 us: weighted(): pl.pallas_call(functools.partial(expert_kernel, each, topk, first, rows,...]
    ppermute x2 -> x21, starting transfers between devices: 3.1 us -> 24.1 us  [the longest x15 17.8 us: swapped(): return lax.ppermute(block, 'expert', route)]
    reshape x14 -> x0, local copies, waits for them, and re-layouts: 14.9 us -> none  [the longest x1 2.26 us: on_device(): expert_forward(received.reshape(-1, width), gate_mat, up_mat, down_mat)]
    reduce_sum x4 -> x0, other arithmetic: 4.8 us -> none  [the longest x2 3.84 us: route_tables(): picker = jnp.sum(match.astype(jnp.float32), axis=2).astype(jnp.bfloat16)]
  transfers between devices with their start and end apart: 7 -> 21, of which waited for: 6 -> 9; matrix products, arithmetic and copies ran while one was open for 27% -> 4% of each run, Pallas kernels for 0% -> 22%
where the time goes in v2:
time: 87.6 us; the launch traced here: 87.4 us
  waiting for transfers between devices  35.2 us (40%)
  starting transfers between devices  24.1 us (28%)
  Pallas kernels  21.2 us (24%)
  other arithmetic  4.48 us (5%)
  local copies, waits for them, and re-layouts  1.55 us (2%)
    ppermute x15, waiting for transfers between devices, swapped(): return lax.ppermute(block, 'expert', route)  30.5 us
    pallas_call x4, Pallas kernels, weighted(): pl.pallas_call(functools.partial(expert_kernel, each, topk, first, rows,...  19.4 us
    ppermute x15, starting transfers between devices, swapped(): return lax.ppermute(block, 'expert', route)  17.8 us
    ppermute x6, starting transfers between devices, passed_along(): return lax.ppermute(block, ('section', 'expert'), route)  6.35 us
    ppermute x6, waiting for transfers between devices, passed_along(): return lax.ppermute(block, ('section', 'expert'), route)  4.79 us
    concatenate x6, other arithmetic, step(): self.held = joined(parts, 0) if JOIN else jnp.concatenate(parts, axis=0)  2.59 us
    pallas_call x1, Pallas kernels, packed(): pl.pallas_call(packing_kernel, out_shape=jax.ShapeDtypeStruct((length, wi...  1.77 us
  transfers between devices with their start and end apart: 21, of which 9 were waited for; matrix products, arithmetic and copies ran while one was open for 4% of the time, Pallas kernels for 22%

profile of v2, /device:TPU:0, one launch (start us, length us, event | category | flops | bytes accessed | tf_op | source)
XLA Modules:
  0.0 87.4 jit_solution(6396976107733861557)
XLA Ops:
  0.6 1.8 %shard_map.113 = bf16[64,1152]{1,0:T(8,128)(2,1)} custom-call(bf16[64,1024]{1,0:T(8,128)(2,1)} %bitcast.32, s32[8,64]{1,0:T(8,128)} %bitcast.34, f32[8,64]{1,0:T(8,128)} %bitcast.35, s32[8,64]{1,0:T(8,128)} %bitcast.36, f32[8,64]{1,0:T(8,128)} %bitcast.37), custom_call_target="tpu_custom_call" | custom-call | flops 1 | bytes 1 | tf_op jit(solution)/shard_map/pallas_call | solution.py:158
  2.4 1.3 %constant_dynamic-update-slice_fusion.1 = bf16[1024,768]{1,0:T(8,128)(2,1)S(1)} fusion(bf16[1024,384]{1,0:T(8,128)(2,1)} %bitcast.23), kind=kLoop, calls=%fused_computation.19 | loop fusion | bytes 1572864
  4.4 3.7 %collective-permute-start.1 = (bf16[64,1152]{1,0:T(8,128)(2,1)S(1)}, bf16[64,1152]{1,0:T(8,128)(2,1)S(1)}, u32[]{:S(2)}, u32[]{:S(2)}) collective-permute-start(bf16[64,1152]{1,0:T(8,128)(2,1)S(1)} %copy-done.1), channel_id=1, source_target_pairs={{0,8},{1,9},{2,10},{3,11},{4,12},{5,13},{6,14},{7,15},{8,0},{9,1},... | collective-permute-start | bytes 442376 | tf_op jit(solution)/shard_map/ppermute | solution.py:35
  8.1 10.6 %collective-permute-done.1 = bf16[64,1152]{1,0:T(8,128)(2,1)S(1)} collective-permute-done((bf16[64,1152]{1,0:T(8,128)(2,1)S(1)}, bf16[64,1152]{1,0:T(8,128)(2,1)S(1)}, u32[]{:S(2)}, u32[]{:S(2)}) %collective-permute-start.1) | collective-permute-done | bytes 147488 | tf_op jit(solution)/shard_map/ppermute | solution.py:35
  19.3 3.4 %collective-permute-start.14 = (bf16[64,1024]{1,0:T(8,128)(2,1)S(1)}, bf16[64,1024]{1,0:T(8,128)(2,1)S(1)}, u32[]{:S(2)}, u32[]{:S(2)}) collective-permute-start(bf16[64,1024]{1,0:T(8,128)(2,1)S(1)} %bitcast.28), channel_id=1, source_target_pairs={{0,8},{1,9},{2,10},{3,11},{4,12},{5,13},{6,14},{7,15},{8,0},{9,1},... | collective-permute-start | bytes 393224 | tf_op jit(solution)/shard_map/ppermute | solution.py:35
  22.7 1.0 %collective-permute-start.12 = (bf16[128,1024]{1,0:T(8,128)(2,1)S(1)}, bf16[128,1024]{1,0:T(8,128)(2,1)S(1)}, u32[]{:S(2)}, u32[]{:S(2)}) collective-permute-start(bf16[128,1024]{1,0:T(8,128)(2,1)S(1)} %pad_maximum_fusion.4), channel_id=1, source_target_pairs={{0,4},{1,3},{2,6},{3,1},{4,0},{5,7},{6,2},{7,5},{8,12},{9,11},{10,... | collective-permute-start | bytes 786440 | tf_op jit(solution)/shard_map/ppermute | solution.py:35
  23.8 3.5 %collective-permute-done.14 = bf16[64,1024]{1,0:T(8,128)(2,1)S(1)} collective-permute-done((bf16[64,1024]{1,0:T(8,128)(2,1)S(1)}, bf16[64,1024]{1,0:T(8,128)(2,1)S(1)}, u32[]{:S(2)}, u32[]{:S(2)}) %collective-permute-start.14) | collective-permute-done | bytes 131104 | tf_op jit(solution)/shard_map/ppermute | solution.py:35
  27.3 3.0 %collective-permute-start.15 = (bf16[128,1024]{1,0:T(8,128)(2,1)S(1)}, bf16[128,1024]{1,0:T(8,128)(2,1)S(1)}, u32[]{:S(2)}, u32[]{:S(2)}) collective-permute-start(bf16[128,1024]{1,0:T(8,128)(2,1)S(1)} %pad_maximum_fusion.5), channel_id=1, source_target_pairs={{0,4},{1,3},{2,6},{3,1},{4,0},{5,7},{6,2},{7,5},{8,12},{9,11},{10,... | collective-permute-start | bytes 786440 | tf_op jit(solution)/shard_map/ppermute | solution.py:35
  30.3 0.9 %pad_maximum_fusion.refs_0_.refs_6_ = bf16[256,1152]{1,0:T(8,128)(2,1)} fusion(bf16[128,1152]{1,0:T(8,128)(2,1)S(1)} %collective-permute-done.2, bf16[64,1152]{1,0:T(8,128)(2,1)S(1)} %collective-permute-done.1, bf16[64,1152]{1,0:T(8,128)(2,1)S(1)} %copy-done.1), kind=kLoop, calls=%fused_computation.2 | loop fusion | flops 1769472 | bytes 1179648 | tf_op jit(solution)/shard_map/concatenate | solution.py:53
  31.2 1.1 %collective-permute-start.3 = (bf16[256,1152]{1,0:T(8,128)(2,1)}, bf16[256,1152]{1,0:T(8,128)(2,1)}, u32[]{:S(2)}, u32[]{:S(2)}) collective-permute-start(bf16[256,1152]{1,0:T(8,128)(2,1)} %pad_maximum_fusion.refs_0_.refs_6_), channel_id=1, source_target_pairs={{0,2},{1,5},{2,0},{3,7},{4,6},{5,1},{6,4},{7,3},{8,10},{9,13},{10,... | collective-permute-start | bytes 1769480 | tf_op jit(solution)/shard_map/ppermute | solution.py:35
  32.3 0.8 pad_maximum_fusion.1.refs_0_
  33.1 0.9 %collective-permute-start.13 = (bf16[256,1024]{1,0:T(8,128)(2,1)}, bf16[256,1024]{1,0:T(8,128)(2,1)}, u32[]{:S(2)}, u32[]{:S(2)}) collective-permute-start(bf16[256,1024]{1,0:T(8,128)(2,1)} %pad_maximum_fusion.1.refs_0_), channel_id=1, source_target_pairs={{0,2},{1,5},{2,0},{3,7},{4,6},{5,1},{6,4},{7,3},{8,10},{9,13},{10,... | collective-permute-start | bytes 1572872 | tf_op jit(solution)/shard_map/ppermute | solution.py:35
  34.0 3.5 %collective-permute-done.15 = bf16[128,1024]{1,0:T(8,128)(2,1)S(1)} collective-permute-done((bf16[128,1024]{1,0:T(8,128)(2,1)S(1)}, bf16[128,1024]{1,0:T(8,128)(2,1)S(1)}, u32[]{:S(2)}, u32[]{:S(2)}) %collective-permute-start.15) | collective-permute-done | bytes 262176 | tf_op jit(solution)/shard_map/ppermute | solution.py:35
  37.5 0.8 pad_maximum_fusion.2.refs_1_
  38.4 1.0 %collective-permute-start.16 = (bf16[256,1024]{1,0:T(8,128)(2,1)}, bf16[256,1024]{1,0:T(8,128)(2,1)}, u32[]{:S(2)}, u32[]{:S(2)}) collective-permute-start(bf16[256,1024]{1,0:T(8,128)(2,1)} %pad_maximum_fusion.2.refs_1_), channel_id=1, source_target_pairs={{0,2},{1,5},{2,0},{3,7},{4,6},{5,1},{6,4},{7,3},{8,10},{9,13},{10,... | collective-permute-start | bytes 1572872 | tf_op jit(solution)/shard_map/ppermute | solution.py:35
  39.4 2.0 %collective-permute-done.3.refs_0_.refs_6_ = bf16[256,1152]{1,0:T(8,128)(2,1)} collective-permute-done((bf16[256,1152]{1,0:T(8,128)(2,1)}, bf16[256,1152]{1,0:T(8,128)(2,1)}, u32[]{:S(2)}, u32[]{:S(2)}) %collective-permute-start.3) | collective-permute-done | bytes 589856 | tf_op jit(solution)/shard_map/ppermute | solution.py:35
  41.4 4.8 %shard_map.114 = bf16[256,1024]{1,0:T(8,128)(2,1)S(1)} custom-call(s32[1]{0:T(128)} %bitcast.1.me_ref, bf16[256,1152]{1,0:T(8,128)(2,1)} %collective-permute-done.3.refs_0_.refs_6_, bf16[1024,768]{1,0:T(8,128)(2,1)S(1)} %constant_dynamic-update-slice_fusion.refs_1_.refs_2_, bf16[384,1024]{1,0:T(8,128)(2,1)} %bitcast.12.refs_2_.refs_3_, ...), custom_call_target="tpu_custom_call" | custom-call | flops 120795952 | bytes 530841 | tf_op jit(solution)/shard_map/pallas_call | solution.py:275
  46.2 1.1 %collective-permute-start.6 = (bf16[256,1024]{1,0:T(8,128)(2,1)S(1)}, bf16[256,1024]{1,0:T(8,128)(2,1)S(1)}, u32[]{:S(2)}, u32[]{:S(2)}) collective-permute-start(bf16[256,1024]{1,0:T(8,128)(2,1)S(1)} %shard_map.114), channel_id=1, source_target_pairs={{0,2},{1,5},{2,0},{3,7},{4,6},{5,1},{6,4},{7,3},{8,10},{9,13},{10,... | collective-permute-start | bytes 1572872 | tf_op jit(solution)/shard_map/ppermute | solution.py:35
  47.4 4.3 %shard_map.115 = f32[256,1024]{1,0:T(8,128)S(1)} custom-call(s32[1]{0:T(128)} %bitcast.1.me_ref, bf16[256,1152]{1,0:T(8,128)(2,1)} %pad_maximum_fusion.refs_0_.refs_6_, bf16[1024,768]{1,0:T(8,128)(2,1)S(1)} %constant_dynamic-update-slice_fusion.refs_1_.refs_2_, bf16[384,1024]{1,0:T(8,128)(2,1)} %bitcast.12.refs_2_.refs_3_, bf16[1024,768]{1,0:T(8,128)(2,1)} %copy-done, ...), custom_call_target="tpu_custom_call" | custom-call | flops 120795952 | bytes 530841 | tf_op jit(solution)/shard_map/pallas_call | solution.py:275
  51.7 0.9 %collective-permute-done.16.refs_1_ = bf16[256,1024]{1,0:T(8,128)(2,1)} collective-permute-done((bf16[256,1024]{1,0:T(8,128)(2,1)}, bf16[256,1024]{1,0:T(8,128)(2,1)}, u32[]{:S(2)}, u32[]{:S(2)}) %collective-permute-start.16) | collective-permute-done | bytes 524320 | tf_op jit(solution)/shard_map/ppermute | solution.py:35
  52.6 5.2 %shard_map.116 = bf16[256,1024]{1,0:T(8,128)(2,1)S(1)} custom-call(s32[1]{0:T(128)} %bitcast.1.me_ref, bf16[256,1024]{1,0:T(8,128)(2,1)} %collective-permute-done.13.refs_0_, bf16[256,1024]{1,0:T(8,128)(2,1)} %collective-permute-done.16.refs_1_, bf16[1024,768]{1,0:T(8,128)(2,1)S(1)} %constant_dynamic-update-slice_fusion.refs_1_.refs_2_, ...), custom_call_target="tpu_custom_call" | custom-call | flops 201326592 | bytes 635699 | tf_op jit(solution)/shard_map/pallas_call | solution.py:275
  57.8 1.1 %collective-permute-start.17 = (bf16[256,1024]{1,0:T(8,128)(2,1)S(1)}, bf16[256,1024]{1,0:T(8,128)(2,1)S(1)}, u32[]{:S(2)}, u32[]{:S(2)}) collective-permute-start(bf16[256,1024]{1,0:T(8,128)(2,1)S(1)} %shard_map.116), channel_id=1, source_target_pairs={{0,2},{1,5},{2,0},{3,7},{4,6},{5,1},{6,4},{7,3},{8,10},{9,13},{10,... | collective-permute-start | bytes 1572872 | tf_op jit(solution)/shard_map/ppermute | solution.py:35
  58.9 1.5 %collective-permute-start = (bf16[64,1024]{1,0:T(8,128)(2,1)S(1)}, bf16[64,1024]{1,0:T(8,128)(2,1)S(1)}, u32[]{:S(2)}, u32[]{:S(2)}) collective-permute-start(bf16[64,1024]{1,0:T(8,128)(2,1)S(1)} %bitcast.33), channel_id=1, source_target_pairs={{0,16},{1,17},{2,18},{3,19},{4,20},{5,21},{6,22},{7,23},{8,24},{9,... | collective-permute-start | bytes 393224 | tf_op jit(solution)/shard_map/ppermute | solution.py:30
  61.3 5.1 %shard_map.117 = f32[256,1024]{1,0:T(8,128)S(1)} custom-call(s32[1]{0:T(128)} %bitcast.1.me_ref, bf16[256,1024]{1,0:T(8,128)(2,1)} %pad_maximum_fusion.1.refs_0_, bf16[256,1024]{1,0:T(8,128)(2,1)} %pad_maximum_fusion.2.refs_1_, bf16[1024,768]{1,0:T(8,128)(2,1)S(1)} %constant_dynamic-update-slice_fusion.refs_1_.refs_2_, ...), custom_call_target="tpu_custom_call" | custom-call | flops 201326592 | bytes 635699 | tf_op jit(solution)/shard_map/pallas_call | solution.py:275
  66.4 4.4 %collective-permute-done.17 = bf16[256,1024]{1,0:T(8,128)(2,1)S(1)} collective-permute-done((bf16[256,1024]{1,0:T(8,128)(2,1)S(1)}, bf16[256,1024]{1,0:T(8,128)(2,1)S(1)}, u32[]{:S(2)}, u32[]{:S(2)}) %collective-permute-start.17) | collective-permute-done | bytes 524320 | tf_op jit(solution)/shard_map/ppermute | solution.py:35
  71.3 2.0 %collective-permute-start.9 = (bf16[64,1024]{1,0:T(8,128)(2,1)S(1)}, bf16[64,1024]{1,0:T(8,128)(2,1)S(1)}, u32[]{:S(2)}, u32[]{:S(2)}) collective-permute-start(bf16[64,1024]{1,0:T(8,128)(2,1)S(1)} %get-tuple-element.27), channel_id=1, source_target_pairs={{0,24},{1,25},{2,26},{3,27},{4,28},{5,29},{6,30},{7,31},{8,16},{9,... | collective-permute-start | bytes 393224 | tf_op jit(solution)/shard_map/ppermute | solution.py:30
  73.8 5.5 %collective-permute-done.18 = bf16[128,1024]{1,0:T(8,128)(2,1)S(1)} collective-permute-done((bf16[128,1024]{1,0:T(8,128)(2,1)S(1)}, bf16[128,1024]{1,0:T(8,128)(2,1)S(1)}, u32[]{:S(2)}, u32[]{:S(2)}) %collective-permute-start.18) | collective-permute-done | bytes 262176 | tf_op jit(solution)/shard_map/ppermute | solution.py:35
  79.4 0.9 %collective-permute-start.20 = (bf16[64,1024]{1,0:T(8,128)(2,1)S(1)}, bf16[64,1024]{1,0:T(8,128)(2,1)S(1)}, u32[]{:S(2)}, u32[]{:S(2)}) collective-permute-start(bf16[64,1024]{1,0:T(8,128)(2,1)S(1)} %get-tuple-element.25), channel_id=1, source_target_pairs={{0,24},{1,25},{2,26},{3,27},{4,28},{5,29},{6,30},{7,31},{8,16},{9,... | collective-permute-start | bytes 393224 | tf_op jit(solution)/shard_map/ppermute | solution.py:30
  80.3 0.9 %collective-permute-start.19 = (bf16[64,1024]{1,0:T(8,128)(2,1)S(1)}, bf16[64,1024]{1,0:T(8,128)(2,1)S(1)}, u32[]{:S(2)}, u32[]{:S(2)}) collective-permute-start(bf16[64,1024]{1,0:T(8,128)(2,1)S(1)} %get-tuple-element.24), channel_id=1, source_target_pairs={{0,16},{1,17},{2,18},{3,19},{4,20},{5,21},{6,22},{7,23},{8,24},{9,... | collective-permute-start | bytes 393224 | tf_op jit(solution)/shard_map/ppermute | solution.py:30
  81.2 1.5 %collective-permute-done.9 = bf16[64,1024]{1,0:T(8,128)(2,1)S(1)} collective-permute-done((bf16[64,1024]{1,0:T(8,128)(2,1)S(1)}, bf16[64,1024]{1,0:T(8,128)(2,1)S(1)}, u32[]{:S(2)}, u32[]{:S(2)}) %collective-permute-start.9) | collective-permute-done | bytes 131104 | tf_op jit(solution)/shard_map/ppermute | solution.py:30
  82.7 0.7 fusion.2
  83.4 3.3 %collective-permute-done.20 = bf16[64,1024]{1,0:T(8,128)(2,1)S(1)} collective-permute-done((bf16[64,1024]{1,0:T(8,128)(2,1)S(1)}, bf16[64,1024]{1,0:T(8,128)(2,1)S(1)}, u32[]{:S(2)}, u32[]{:S(2)}) %collective-permute-start.20) | collective-permute-done | bytes 131104 | tf_op jit(solution)/shard_map/ppermute | solution.py:30
  (45 shorter events, 3.9 us)
Async XLA Ops:
  0.6 3.1 %copy-start.2 = (bf16[1,1,1024,384]{3,2,1,0:T(8,128)(2,1)S(1)}, bf16[1,1,1024,384]{3,2,1,0:T(8,128)(2,1)}, u32[]{:S(2)}) copy-start(bf16[1,1,1024,384]{3,2,1,0:T(8,128)(2,1)} %param.18) | copy-start | bytes 2359300
  2.4 2.0 %copy-start.1 = (bf16[64,1152]{1,0:T(8,128)(2,1)S(1)}, bf16[64,1152]{1,0:T(8,128)(2,1)}, u32[]{:S(2)}) copy-start(bf16[64,1152]{1,0:T(8,128)(2,1)} %shard_map.113) | copy-start | bytes 442372
  2.4 5.6 %copy-start.3 = (bf16[1,64,1024]{2,1,0:T(8,128)(2,1)S(1)}, bf16[1,64,1024]{2,1,0:T(8,128)(2,1)}, u32[]{:S(2)}) copy-start(bf16[1,64,1024]{2,1,0:T(8,128)(2,1)} %param.13) | copy-start | bytes 393220
  2.4 16.9 %copy-start.4 = (bf16[1,64,1024]{2,1,0:T(8,128)(2,1)S(1)}, bf16[1,64,1024]{2,1,0:T(8,128)(2,1)}, u32[]{:S(2)}) copy-start(bf16[1,64,1024]{2,1,0:T(8,128)(2,1)} %param.16) | copy-start | bytes 393220
  3.9 37.5 %collective-permute-start.4 = (bf16[1024,768]{1,0:T(8,128)(2,1)S(1)}, bf16[1024,768]{1,0:T(8,128)(2,1)S(1)}, u32[]{:S(2)}, u32[]{:S(2)}) collective-permute-start(bf16[1024,768]{1,0:T(8,128)(2,1)S(1)} %constant_dynamic-update-slice_fusion.refs_1_.refs_2_), channel_id=1, source_target_pairs={{0,1},{1,0},{2,3},{3,2},{4,5},{5,4},{6,7},{7,6},{8,9},{9,8},{10,11... | collective-permute-start | bytes 4718600 | tf_op jit(solution)/shard_map/ppermute | solution.py:35
  4.4 14.3 %collective-permute-start.1 = (bf16[64,1152]{1,0:T(8,128)(2,1)S(1)}, bf16[64,1152]{1,0:T(8,128)(2,1)S(1)}, u32[]{:S(2)}, u32[]{:S(2)}) collective-permute-start(bf16[64,1152]{1,0:T(8,128)(2,1)S(1)} %copy-done.1), channel_id=1, source_target_pairs={{0,8},{1,9},{2,10},{3,11},{4,12},{5,13},{6,14},{7,15},{8,0},{9,1},... | collective-permute-start | bytes 442376 | tf_op jit(solution)/shard_map/ppermute | solution.py:35
  8.1 14.7 %collective-permute-start.11 = (bf16[64,1024]{1,0:T(8,128)(2,1)S(1)}, bf16[64,1024]{1,0:T(8,128)(2,1)S(1)}, u32[]{:S(2)}, u32[]{:S(2)}) collective-permute-start(bf16[64,1024]{1,0:T(8,128)(2,1)S(1)} %bitcast.25), channel_id=1, source_target_pairs={{0,8},{1,9},{2,10},{3,11},{4,12},{5,13},{6,14},{7,15},{8,0},{9,1},... | collective-permute-start | bytes 393224 | tf_op jit(solution)/shard_map/ppermute | solution.py:35
  18.7 11.6 %collective-permute-start.2 = (bf16[128,1152]{1,0:T(8,128)(2,1)S(1)}, bf16[128,1152]{1,0:T(8,128)(2,1)S(1)}, u32[]{:S(2)}, u32[]{:S(2)}) collective-permute-start(bf16[128,1152]{1,0:T(8,128)(2,1)S(1)} %pad_maximum_fusion.3), channel_id=1, source_target_pairs={{0,4},{1,3},{2,6},{3,1},{4,0},{5,7},{6,2},{7,5},{8,12},{9,11},{10,... | collective-permute-start | bytes 884744 | tf_op jit(solution)/shard_map/ppermute | solution.py:35
  19.3 7.9 %collective-permute-start.14 = (bf16[64,1024]{1,0:T(8,128)(2,1)S(1)}, bf16[64,1024]{1,0:T(8,128)(2,1)S(1)}, u32[]{:S(2)}, u32[]{:S(2)}) collective-permute-start(bf16[64,1024]{1,0:T(8,128)(2,1)S(1)} %bitcast.28), channel_id=1, source_target_pairs={{0,8},{1,9},{2,10},{3,11},{4,12},{5,13},{6,14},{7,15},{8,0},{9,1},... | collective-permute-start | bytes 393224 | tf_op jit(solution)/shard_map/ppermute | solution.py:35
  22.7 16.7 %collective-permute-start.5 = (bf16[384,1024]{1,0:T(8,128)(2,1)}, bf16[384,1024]{1,0:T(8,128)(2,1)}, u32[]{:S(2)}, u32[]{:S(2)}) collective-permute-start(bf16[384,1024]{1,0:T(8,128)(2,1)} %bitcast.12.refs_2_.refs_3_), channel_id=1, source_target_pairs={{0,1},{1,0},{2,3},{3,2},{4,5},{5,4},{6,7},{7,6},{8,9},{9,8},{10,11... | collective-permute-start | bytes 2359304 | tf_op jit(solution)/shard_map/ppermute | solution.py:35
  22.7 9.5 %collective-permute-start.12 = (bf16[128,1024]{1,0:T(8,128)(2,1)S(1)}, bf16[128,1024]{1,0:T(8,128)(2,1)S(1)}, u32[]{:S(2)}, u32[]{:S(2)}) collective-permute-start(bf16[128,1024]{1,0:T(8,128)(2,1)S(1)} %pad_maximum_fusion.4), channel_id=1, source_target_pairs={{0,4},{1,3},{2,6},{3,1},{4,0},{5,7},{6,2},{7,5},{8,12},{9,11},{10,... | collective-permute-start | bytes 786440 | tf_op jit(solution)/shard_map/ppermute | solution.py:35
  27.3 10.2 %collective-permute-start.15 = (bf16[128,1024]{1,0:T(8,128)(2,1)S(1)}, bf16[128,1024]{1,0:T(8,128)(2,1)S(1)}, u32[]{:S(2)}, u32[]{:S(2)}) collective-permute-start(bf16[128,1024]{1,0:T(8,128)(2,1)S(1)} %pad_maximum_fusion.5), channel_id=1, source_target_pairs={{0,4},{1,3},{2,6},{3,1},{4,0},{5,7},{6,2},{7,5},{8,12},{9,11},{10,... | collective-permute-start | bytes 786440 | tf_op jit(solution)/shard_map/ppermute | solution.py:35
  31.2 10.2 %collective-permute-start.3 = (bf16[256,1152]{1,0:T(8,128)(2,1)}, bf16[256,1152]{1,0:T(8,128)(2,1)}, u32[]{:S(2)}, u32[]{:S(2)}) collective-permute-start(bf16[256,1152]{1,0:T(8,128)(2,1)} %pad_maximum_fusion.refs_0_.refs_6_), channel_id=1, source_target_pairs={{0,2},{1,5},{2,0},{3,7},{4,6},{5,1},{6,4},{7,3},{8,10},{9,13},{10,... | collective-permute-start | bytes 1769480 | tf_op jit(solution)/shard_map/ppermute | solution.py:35
  33.1 18.6 %collective-permute-start.13 = (bf16[256,1024]{1,0:T(8,128)(2,1)}, bf16[256,1024]{1,0:T(8,128)(2,1)}, u32[]{:S(2)}, u32[]{:S(2)}) collective-permute-start(bf16[256,1024]{1,0:T(8,128)(2,1)} %pad_maximum_fusion.1.refs_0_), channel_id=1, source_target_pairs={{0,2},{1,5},{2,0},{3,7},{4,6},{5,1},{6,4},{7,3},{8,10},{9,13},{10,... | collective-permute-start | bytes 1572872 | tf_op jit(solution)/shard_map/ppermute | solution.py:35
  38.4 14.3 %collective-permute-start.16 = (bf16[256,1024]{1,0:T(8,128)(2,1)}, bf16[256,1024]{1,0:T(8,128)(2,1)}, u32[]{:S(2)}, u32[]{:S(2)}) collective-permute-start(bf16[256,1024]{1,0:T(8,128)(2,1)} %pad_maximum_fusion.2.refs_1_), channel_id=1, source_target_pairs={{0,2},{1,5},{2,0},{3,7},{4,6},{5,1},{6,4},{7,3},{8,10},{9,13},{10,... | collective-permute-start | bytes 1572872 | tf_op jit(solution)/shard_map/ppermute | solution.py:35
  41.4 4.9 %copy-start = (bf16[1024,768]{1,0:T(8,128)(2,1)}, bf16[1024,768]{1,0:T(8,128)(2,1)S(1)}, u32[]{:S(2)}) copy-start(bf16[1024,768]{1,0:T(8,128)(2,1)S(1)} %collective-permute-done.4.refs_3_.refs_4_) | copy-start | bytes 4718596
  46.2 14.7 %collective-permute-start.6 = (bf16[256,1024]{1,0:T(8,128)(2,1)S(1)}, bf16[256,1024]{1,0:T(8,128)(2,1)S(1)}, u32[]{:S(2)}, u32[]{:S(2)}) collective-permute-start(bf16[256,1024]{1,0:T(8,128)(2,1)S(1)} %shard_map.114), channel_id=1, source_target_pairs={{0,2},{1,5},{2,0},{3,7},{4,6},{5,1},{6,4},{7,3},{8,10},{9,13},{10,... | collective-permute-start | bytes 1572872 | tf_op jit(solution)/shard_map/ppermute | solution.py:35
  51.7 7.2 %copy-start.5 = (bf16[1,64,1024]{2,1,0:T(8,128)(2,1)S(1)}, bf16[1,64,1024]{2,1,0:T(8,128)(2,1)}, u32[]{:S(2)}) copy-start(bf16[1,64,1024]{2,1,0:T(8,128)(2,1)} %param.10) | copy-start | bytes 393220
  57.8 13.1 %collective-permute-start.17 = (bf16[256,1024]{1,0:T(8,128)(2,1)S(1)}, bf16[256,1024]{1,0:T(8,128)(2,1)S(1)}, u32[]{:S(2)}, u32[]{:S(2)}) collective-permute-start(bf16[256,1024]{1,0:T(8,128)(2,1)S(1)} %shard_map.116), channel_id=1, source_target_pairs={{0,2},{1,5},{2,0},{3,7},{4,6},{5,1},{6,4},{7,3},{8,10},{9,13},{10,... | collective-permute-start | bytes 1572872 | tf_op jit(solution)/shard_map/ppermute | solution.py:35
  58.9 21.4 %collective-permute-start = (bf16[64,1024]{1,0:T(8,128)(2,1)S(1)}, bf16[64,1024]{1,0:T(8,128)(2,1)S(1)}, u32[]{:S(2)}, u32[]{:S(2)}) collective-permute-start(bf16[64,1024]{1,0:T(8,128)(2,1)S(1)} %bitcast.33), channel_id=1, source_target_pairs={{0,16},{1,17},{2,18},{3,19},{4,20},{5,21},{6,22},{7,23},{8,24},{9,... | collective-permute-start | bytes 393224 | tf_op jit(solution)/shard_map/ppermute | solution.py:30
  60.4 22.9 %collective-permute-start.10 = (bf16[64,1024]{1,0:T(8,128)(2,1)S(1)}, bf16[64,1024]{1,0:T(8,128)(2,1)S(1)}, u32[]{:S(2)}, u32[]{:S(2)}) collective-permute-start(bf16[64,1024]{1,0:T(8,128)(2,1)S(1)} %bitcast.31), channel_id=1, source_target_pairs={{0,16},{1,17},{2,18},{3,19},{4,20},{5,21},{6,22},{7,23},{8,24},{9,... | collective-permute-start | bytes 393224 | tf_op jit(solution)/shard_map/ppermute | solution.py:30
  61.2 10.0 %collective-permute-start.7 = (bf16[128,1024]{1,0:T(8,128)(2,1)S(1)}, bf16[128,1024]{1,0:T(8,128)(2,1)S(1)}, u32[]{:S(2)}, u32[]{:S(2)}) collective-permute-start(bf16[128,1024]{1,0:T(8,128)(2,1)S(1)} %slice.55), channel_id=1, source_target_pairs={{0,4},{1,3},{2,6},{3,1},{4,0},{5,7},{6,2},{7,5},{8,12},{9,11},{10,... | collective-permute-start | bytes 786440 | tf_op jit(solution)/shard_map/ppermute | solution.py:35
  71.1 8.2 %collective-permute-start.18 = (bf16[128,1024]{1,0:T(8,128)(2,1)S(1)}, bf16[128,1024]{1,0:T(8,128)(2,1)S(1)}, u32[]{:S(2)}, u32[]{:S(2)}) collective-permute-start(bf16[128,1024]{1,0:T(8,128)(2,1)S(1)} %slice.54), channel_id=1, source_target_pairs={{0,4},{1,3},{2,6},{3,1},{4,0},{5,7},{6,2},{7,5},{8,12},{9,11},{10,... | collective-permute-start | bytes 786440 | tf_op jit(solution)/shard_map/ppermute | solution.py:35
  71.3 11.4 %collective-permute-start.9 = (bf16[64,1024]{1,0:T(8,128)(2,1)S(1)}, bf16[64,1024]{1,0:T(8,128)(2,1)S(1)}, u32[]{:S(2)}, u32[]{:S(2)}) collective-permute-start(bf16[64,1024]{1,0:T(8,128)(2,1)S(1)} %get-tuple-element.27), channel_id=1, source_target_pairs={{0,24},{1,25},{2,26},{3,27},{4,28},{5,29},{6,30},{7,31},{8,16},{9,... | collective-permute-start | bytes 393224 | tf_op jit(solution)/shard_map/ppermute | solution.py:30
  73.3 9.4 %collective-permute-start.8 = (bf16[64,1024]{1,0:T(8,128)(2,1)S(1)}, bf16[64,1024]{1,0:T(8,128)(2,1)S(1)}, u32[]{:S(2)}, u32[]{:S(2)}) collective-permute-start(bf16[64,1024]{1,0:T(8,128)(2,1)S(1)} %get-tuple-element.26), channel_id=1, source_target_pairs={{0,16},{1,17},{2,18},{3,19},{4,20},{5,21},{6,22},{7,23},{8,24},{9,... | collective-permute-start | bytes 393224 | tf_op jit(solution)/shard_map/ppermute | solution.py:30
  79.4 7.3 %collective-permute-start.20 = (bf16[64,1024]{1,0:T(8,128)(2,1)S(1)}, bf16[64,1024]{1,0:T(8,128)(2,1)S(1)}, u32[]{:S(2)}, u32[]{:S(2)}) collective-permute-start(bf16[64,1024]{1,0:T(8,128)(2,1)S(1)} %get-tuple-element.25), channel_id=1, source_target_pairs={{0,24},{1,25},{2,26},{3,27},{4,28},{5,29},{6,30},{7,31},{8,16},{9,... | collective-permute-start | bytes 393224 | tf_op jit(solution)/shard_map/ppermute | solution.py:30
  80.3 6.4 %collective-permute-start.19 = (bf16[64,1024]{1,0:T(8,128)(2,1)S(1)}, bf16[64,1024]{1,0:T(8,128)(2,1)S(1)}, u32[]{:S(2)}, u32[]{:S(2)}) collective-permute-start(bf16[64,1024]{1,0:T(8,128)(2,1)S(1)} %get-tuple-element.24), channel_id=1, source_target_pairs={{0,16},{1,17},{2,18},{3,19},{4,20},{5,21},{6,22},{7,23},{8,24},{9,... | collective-permute-start | bytes 393224 | tf_op jit(solution)/shard_map/ppermute | solution.py:30

commit v3 on v2

--- a/solution.py
+++ b/solution.py
@@ -10,14 +10,15 @@
 F32 = jnp.float32
 BF16 = jnp.bfloat16
 LANES = 128
-VMEM_LIMIT = 48 * 1024 * 1024
-COST = 0.1
+VMEM_LIMIT = 20 * 1024 * 1024
+COST = 1.0
 IN_TURN = "f,Fs,F,Fk,F,b:Fk,c:Fk,Bs,B,Bk,B"
 JOIN = False
-HBM = True
+LOAD = True
+HBM = False
 GU = 1
 LITTLE = pl.CostEstimate(flops=1, bytes_accessed=1, transcendentals=0)
-PLAN = dict(f="P", b="P", c="P", rf="P", rb="P", odd="QQ", cut="", ops="f,c,b,f,c,b,f,c,b,Fs,F,Fk,Bs,B,F,Bk:F0,B,F,B", step=4)
+PLAN = dict(f="P", b="P", c="P", rf="P", rb="P", odd="QQ", cut="FB", ops="f,c,b,f,c,b,f,c:W,b,Fs,F,F,Fk,Bs,B,B,F,Bk:F0,B,F,B", step=4)
 
 
 def passed_along(block, distance, paths, bit=0):
@@ -198,23 +199,49 @@
     return times_transposed(both, gate_up[...])
 
 
+def loading_kernel(*refs):
+    sems = refs[-1]
+    count = len(refs) // 2
+    copies = [pltpu.make_async_copy(refs[n], refs[count + n], sems.at[n]) for n in range(count)]
+    for copy in copies:
+        copy.start()
+    for copy in copies:
+        copy.wait()
+
+
+def loaded(arrays):
+    return pl.pallas_call(
+        loading_kernel,
+        out_shape=[jax.ShapeDtypeStruct(array.shape, array.dtype) for array in arrays],
+        in_specs=[pl.BlockSpec(memory_space=pl.ANY)] * len(arrays),
+        out_specs=[pl.BlockSpec(memory_space=pltpu.VMEM)] * len(arrays),
+        scratch_shapes=[pltpu.SemaphoreType.DMA((len(arrays),))],
+        compiler_params=pltpu.CompilerParams(vmem_limit_bytes=VMEM_LIMIT),
+        cost_estimate=LITTLE,
+    )(*arrays)
+
+
 def expert_kernel(each, topk, first, rows, step, copies, me_ref, *refs):
     count = 1 + max(operand for each_copy in copies for operand, *_ in each_copy)
     buffers, sems = refs[-1 - len(copies) : -1], refs[-1]
-    out_refs = refs[count : -1 - len(copies)]
-    started = []
-    for buffer, pieces in zip(buffers, copies, strict=True):
-        row, group = 0, []
-        for operand, at, length, column in pieces:
+    weights, out_refs = refs[count : count + 4], refs[count + 4 : -1 - len(copies)]
+    begins = [0]
+    for pieces in copies:
+        begins.append(begins[-1] + len(pieces))
+    started = {}
+
+    def start_copies(number):
+        buffer, row = buffers[number], 0
+        started[number] = []
+        for piece, (operand, at, length, column) in enumerate(copies[number]):
             copy = pltpu.make_async_copy(
                 refs[operand].at[pl.ds(at, length), pl.ds(column, buffer.shape[1])],
                 buffer.at[pl.ds(row, length), :],
-                sems.at[sum(map(len, started)) + len(group)],
+                sems.at[begins[number] + piece],
             )
             copy.start()
-            group.append(copy)
+            started[number].append(copy)
             row += length
-        started.append(group)
 
     def ready(number):
         for copy in started[number]:
@@ -222,27 +249,29 @@
         started[number] = []
         return buffers[number]
 
-    inputs = len(copies) - 5
-    length = out_refs[0].shape[0]
+    inputs = len(copies) - 1
+    for number in range(len(copies)):
+        start_copies(number)
     total_rows = buffers[0].shape[0]
+    places = [(out_ref, row) for out_ref in out_refs for row in range(0, out_ref.shape[0], rows)]
     totals = {}
     for flip in range(2):
         for start in range(0, total_rows, step * rows):
             tile = pl.ds(start, min(step * rows, total_rows - start))
             taken = [ready(number)[tile, :] for number in range(inputs)]
-            gate_up, down = ready(inputs + 2 * flip), ready(inputs + 2 * flip + 1)
+            gate_up, down = weights[2 * flip : 2 * flip + 2]
             out = each(*taken, gate_up, down).astype(BF16).astype(F32)
             out = out * gate_of(ready(len(copies) - 1)[tile, :], topk, first, me_ref[0] ^ flip)
             if flip == 0:
                 totals[start] = out
                 continue
-            out = (totals[start] + out).astype(out_refs[0].dtype)
+            out = totals[start] + out
             for at in range(0, out.shape[0], rows):
-                number, row = divmod(start + at, length)
-                out_refs[number][pl.ds(row, rows), :] = out[at : at + rows]
-
-
-def weighted(each, first, topk, rows, step, wanted, dtype, outputs, place, words, inputs, weights):
+                out_ref, row = places[(start + at) // rows]
+                out_ref[pl.ds(row, rows), :] = out[at : at + rows].astype(out_ref.dtype)
+
+
+def weighted(each, first, topk, rows, step, wanted, outputs, place, words, inputs, weights):
     width, hidden_width = weights[1].shape[1], weights[1].shape[0]
     operands, copies, scratch = [], [], []
     length = len(wanted) * rows
@@ -268,16 +297,14 @@
 
     for parts, orders in inputs:
         rows_from(parts, orders, width, 0)
-    for array in weights:
-        copies.append([(operand(array), 0, array.shape[0], 0)])
-        scratch.append(pltpu.VMEM(array.shape, BF16))
     rows_from(*words, width)
     return pl.pallas_call(
         functools.partial(expert_kernel, each, topk, first, rows, step, copies),
-        out_shape=[jax.ShapeDtypeStruct((length // outputs, width), dtype)] * outputs,
+        out_shape=[jax.ShapeDtypeStruct((number * rows, width), dtype) for number, dtype in outputs],
         in_specs=[pl.BlockSpec(memory_space=pltpu.SMEM)]
-        + [pl.BlockSpec(memory_space=pltpu.HBM if HBM else pl.ANY)] * len(operands),
-        out_specs=[pl.BlockSpec(memory_space=pltpu.VMEM)] * outputs,
+        + [pl.BlockSpec(memory_space=pltpu.HBM if HBM else pl.ANY)] * len(operands)
+        + [pl.BlockSpec(memory_space=pltpu.VMEM)] * len(weights),
+        out_specs=[pl.BlockSpec(memory_space=pltpu.VMEM)] * len(outputs),
         scratch_shapes=scratch + [pltpu.SemaphoreType.DMA((sum(map(len, copies)),))],
         compiler_params=pltpu.CompilerParams(vmem_limit_bytes=VMEM_LIMIT),
         cost_estimate=pl.CostEstimate(
@@ -285,7 +312,7 @@
             bytes_accessed=int(COST * sum(a.size * a.dtype.itemsize for a in operands)),
             transcendentals=0,
         ),
-    )(place, *operands)
+    )(place, *operands, *weights)
 
 
 def on_device(
@@ -326,12 +353,18 @@
     arrays["f"] = packed(arrays["f"], *words)
     down0 = w_down[0, 0]
     pair = [w_gate[0, 0], w_up[0, 0]]
-    if GU:
+    if GU == 1:
         *pair, down0 = behind([*pair, down0], [arrays["f"]])
+    if GU in ("f", "b", "c"):
+        held[GU] = Spread(arrays[GU], paths[GU], orders[plan[GU]], GU in plan["cut"])
+        held[GU].step()
+        *pair, down0 = behind([*pair, down0], held[GU].came)
     gate_up0 = jnp.concatenate(pair, axis=1)
     chip = [{1: 1}] * 2
     gate_up1, down1 = swapped(gate_up0, chip, 1), swapped(down0, chip, 1)
     weights = [gate_up0, down0, gate_up1, down1]
+    if LOAD:
+        weights = loaded(weights)
 
     step = min(plan["step"], blocks // 2)
     place = jnp.reshape(me, (1,))
@@ -345,9 +378,10 @@
         one, other = held[kind].came[-2:]
         return (far.astype(F32) + (one.astype(F32) + other.astype(F32))).astype(BF16)[None]
 
-    outs = {}
+    outs, keeps = {"W": weights[0]}, {}
     items = (plan["ops"] if len(bits) < 4 else IN_TURN).split(",")
-    left = {name: [item[0] for item in items if item[1:2] not in ("s", "k")].count(name) for name in "fbcFB"}
+    left = {name: [item[0] for item in items if item[1:2] not in ("s", "k", "a")].count(name) for name in "fbcFB"}
+    first_left = dict(left)
     for item in items:
         name, _, after = item.partition(":")
         after = [
@@ -358,7 +392,8 @@
         if len(name) == 1:
             if name not in held:
                 held[name] = Spread(arrays[name], paths[kind], orders[plan[name]], name in plan["cut"])
-            held[name].step(after)
+            if name != GU or left[name] < first_left[name]:
+                held[name].step(after)
             left[name] -= 1
             while left[name] == 0 and not held[name].done():
                 held[name].step()
@@ -369,19 +404,21 @@
         carrier = (held["f"].parts, held["f"].orders, held["f"].held.shape[1] - width)
         each, first = (forward_rows, 0) if kind == "f" else (backward_rows, 4)
         half = len(order) // 2
-        sent = name[1] == "s"
-        wanted, dtype = (order[:half], BF16) if sent else (order[half:], F32)
+        sends = [(half // 2, BF16)] * 2 if name[0] in plan["cut"] else [(half, BF16)]
+        wanted, results = {
+            "s": (order[:half], sends),
+            "k": (order[half:], [(half, F32)]),
+            "a": (order, sends + [(half, F32)]),
+        }[name[1]]
         (place,) = behind([place], after)
-        number = 2 if sent and name[0] in plan["cut"] else 1
-        out = weighted(
-            each, first, topk, rows, step, wanted, dtype, number, place, carrier, takes, weights
-        )
+        out = weighted(each, first, topk, rows, step, wanted, results, place, carrier, takes, weights)
         place, *out = lax.optimization_barrier((place, *out))
         outs[name] = out[0]
-        if sent:
+        keeps[name[0]] = keeps.get(name[0]) if name[1] == "s" else out.pop()
+        if name[1] != "k":
             held[name[0]] = Return(out, paths[kind], back, 1 if kind == "f" else -1)
-        else:
-            held[name[0]].keep = out[0]
+        if name[0] in held:
+            held[name[0]].keep = keeps[name[0]]
 
     return arrived(held["y"].came[0], "F"), arrived(held["y"].came[1], "B")
 

time: 87.6 us -> 84.3 us (0.962)
  waiting for transfers between devices: 35.2 us -> 19.8 us
  starting transfers between devices: 24.1 us -> 33.6 us
  local copies, waits for them, and re-layouts: 1.55 us -> 7.06 us
  Pallas kernels: 21.2 us -> 18.2 us
    ppermute x15 -> x17, waiting for transfers between devices: 30.5 us -> 16.2 us  [swapped(): return lax.ppermute(block, 'expert', route)]
    unnamed x13 -> x26, local copies, waits for them, and re-layouts: 1.29 us -> 6.13 us
    ppermute x15 -> x17, starting transfers between devices: 17.8 us -> 22.6 us  [swapped(): return lax.ppermute(block, 'expert', route)]
    ppermute x6, starting transfers between devices: 6.35 us -> 11.1 us  [passed_along(): return lax.ppermute(block, ('section', 'expert'), route)]
    pallas_call x4, Pallas kernels: 19.4 us -> 16.1 us  [weighted(): pl.pallas_call(functools.partial(expert_kernel, each, topk, first, rows,...]
    ppermute x6, waiting for transfers between devices: 4.79 us -> 3.59 us  [passed_along(): return lax.ppermute(block, ('section', 'expert'), route)]
    broadcast_in_dim x2, other arithmetic: 1.42 us -> 2.32 us  [arrived(): (far.astype(F32) + (one.astype(F32) + other.astype(F32))).astype(BF16)[None]]
    concatenate x6 -> x5, other arithmetic: 2.59 us -> 1.76 us  [step(): self.held = joined(parts, 0) if JOIN else jnp.concatenate(parts, axis=0)]
  transfers between devices with their start and end apart: 21 -> 23, of which waited for: 9 -> 6; matrix products, arithmetic and copies ran while one was open for 4% -> 6% of each run, Pallas kernels for 22% -> 20%
where the time goes in v3:
time: 84.3 us; the launch traced here: 83.9 us
  starting transfers between devices  33.6 us (40%)
  waiting for transfers between devices  19.8 us (23%)
  Pallas kernels  18.2 us (22%)
  local copies, waits for them, and re-layouts  7.06 us (8%)
  other arithmetic  4.39 us (5%)
    ppermute x17, starting transfers between devices, swapped(): return lax.ppermute(block, 'expert', route)  22.6 us
    ppermute x17, waiting for transfers between devices, swapped(): return lax.ppermute(block, 'expert', route)  16.2 us
    pallas_call x4, Pallas kernels, weighted(): pl.pallas_call(functools.partial(expert_kernel, each, topk, first, rows,...  16.1 us
    ppermute x6, starting transfers between devices, passed_along(): return lax.ppermute(block, ('section', 'expert'), route)  11.1 us
    unnamed x26, local copies, waits for them, and re-layouts  6.13 us
    ppermute x6, waiting for transfers between devices, passed_along(): return lax.ppermute(block, ('section', 'expert'), route)  3.59 us
    broadcast_in_dim x2, other arithmetic, arrived(): (far.astype(F32) + (one.astype(F32) + other.astype(F32))).astype(BF16)[None]  2.32 us
    concatenate x5, other arithmetic, step(): self.held = joined(parts, 0) if JOIN else jnp.concatenate(parts, axis=0)  1.76 us
  transfers between devices with their start and end apart: 23, of which 6 were waited for; matrix products, arithmetic and copies ran while one was open for 6% of the time, Pallas kernels for 20%

profile of v3, /device:TPU:0, one launch (start us, length us, event | category | flops | bytes accessed | tf_op | source)
XLA Modules:
  0.0 83.9 jit_solution(5466217196135925837)
XLA Ops:
  0.6 1.8 %shard_map.113 = bf16[64,1152]{1,0:T(8,128)(2,1)} custom-call(bf16[64,1024]{1,0:T(8,128)(2,1)} %bitcast.30, s32[8,64]{1,0:T(8,128)} %bitcast.35, f32[8,64]{1,0:T(8,128)} %bitcast.36, s32[8,64]{1,0:T(8,128)} %bitcast.37, f32[8,64]{1,0:T(8,128)} %bitcast.38), custom_call_target="tpu_custom_call" | custom-call | flops 1 | bytes 1 | tf_op jit(solution)/shard_map/pallas_call | solution.py:159
  2.4 1.3 %constant_dynamic-update-slice_fusion.1 = bf16[1024,768]{1,0:T(8,128)(2,1)S(1)} fusion(bf16[1024,384]{1,0:T(8,128)(2,1)} %bitcast.25), kind=kLoop, calls=%fused_computation.14 | loop fusion | bytes 1572864
  4.4 3.7 %collective-permute-start.1 = (bf16[64,1152]{1,0:T(8,128)(2,1)S(1)}, bf16[64,1152]{1,0:T(8,128)(2,1)S(1)}, u32[]{:S(2)}, u32[]{:S(2)}) collective-permute-start(bf16[64,1152]{1,0:T(8,128)(2,1)S(1)} %copy-done.7), channel_id=1, source_target_pairs={{0,8},{1,9},{2,10},{3,11},{4,12},{5,13},{6,14},{7,15},{8,0},{9,1},... | collective-permute-start | bytes 442376 | tf_op jit(solution)/shard_map/ppermute | solution.py:36
  8.6 10.2 %collective-permute-done.1 = bf16[64,1152]{1,0:T(8,128)(2,1)S(1)} collective-permute-done((bf16[64,1152]{1,0:T(8,128)(2,1)S(1)}, bf16[64,1152]{1,0:T(8,128)(2,1)S(1)}, u32[]{:S(2)}, u32[]{:S(2)}) %collective-permute-start.1) | collective-permute-done | bytes 147488 | tf_op jit(solution)/shard_map/ppermute | solution.py:36
  19.4 3.4 %collective-permute-start.15 = (bf16[64,1024]{1,0:T(8,128)(2,1)S(1)}, bf16[64,1024]{1,0:T(8,128)(2,1)S(1)}, u32[]{:S(2)}, u32[]{:S(2)}) collective-permute-start(bf16[64,1024]{1,0:T(8,128)(2,1)S(1)} %bitcast.32), channel_id=1, source_target_pairs={{0,8},{1,9},{2,10},{3,11},{4,12},{5,13},{6,14},{7,15},{8,0},{9,1},... | collective-permute-start | bytes 393224 | tf_op jit(solution)/shard_map/ppermute | solution.py:36
  23.1 4.2 %collective-permute-done.15 = bf16[64,1024]{1,0:T(8,128)(2,1)S(1)} collective-permute-done((bf16[64,1024]{1,0:T(8,128)(2,1)S(1)}, bf16[64,1024]{1,0:T(8,128)(2,1)S(1)}, u32[]{:S(2)}, u32[]{:S(2)}) %collective-permute-start.15) | collective-permute-done | bytes 131104 | tf_op jit(solution)/shard_map/ppermute | solution.py:36
  27.3 3.0 %collective-permute-start.16 = (bf16[128,1024]{1,0:T(8,128)(2,1)S(1)}, bf16[128,1024]{1,0:T(8,128)(2,1)S(1)}, u32[]{:S(2)}, u32[]{:S(2)}) collective-permute-start(bf16[128,1024]{1,0:T(8,128)(2,1)S(1)} %pad_maximum_fusion.4), channel_id=1, source_target_pairs={{0,4},{1,3},{2,6},{3,1},{4,0},{5,7},{6,2},{7,5},{8,12},{9,11},{10,... | collective-permute-start | bytes 786440 | tf_op jit(solution)/shard_map/ppermute | solution.py:36
  31.2 1.1 %collective-permute-start.3 = (bf16[256,1152]{1,0:T(8,128)(2,1)}, bf16[256,1152]{1,0:T(8,128)(2,1)}, u32[]{:S(2)}, u32[]{:S(2)}) collective-permute-start(bf16[256,1152]{1,0:T(8,128)(2,1)} %pad_maximum_fusion.refs_0_.refs_2_), channel_id=1, source_target_pairs={{0,2},{1,5},{2,0},{3,7},{4,6},{5,1},{6,4},{7,3},{8,10},{9,13},{10,... | collective-permute-start | bytes 1769480 | tf_op jit(solution)/shard_map/ppermute | solution.py:36
  33.1 0.9 %collective-permute-start.14 = (bf16[256,1024]{1,0:T(8,128)(2,1)}, bf16[256,1024]{1,0:T(8,128)(2,1)}, u32[]{:S(2)}, u32[]{:S(2)}) collective-permute-start(bf16[256,1024]{1,0:T(8,128)(2,1)} %pad_maximum_fusion.1.refs_0_), channel_id=1, source_target_pairs={{0,2},{1,5},{2,0},{3,7},{4,6},{5,1},{6,4},{7,3},{8,10},{9,13},{10,... | collective-permute-start | bytes 1572872 | tf_op jit(solution)/shard_map/ppermute | solution.py:36
  34.5 0.9 %copy-done = bf16[384,1024]{1,0:T(8,128)(2,1)} copy-done((bf16[384,1024]{1,0:T(8,128)(2,1)}, bf16[384,1024]{1,0:T(8,128)(2,1)S(1)}, u32[]{:S(2)}) %copy-start) | copy-done | bytes 786456
  35.3 0.9 %copy-done.3 = bf16[384,1024]{1,0:T(8,128)(2,1)} copy-done((bf16[384,1024]{1,0:T(8,128)(2,1)}, bf16[384,1024]{1,0:T(8,128)(2,1)S(1)}, u32[]{:S(2)}) %copy-start.3) | copy-done | bytes 786456
  36.3 1.3 %collective-permute-done.16 = bf16[128,1024]{1,0:T(8,128)(2,1)S(1)} collective-permute-done((bf16[128,1024]{1,0:T(8,128)(2,1)S(1)}, bf16[128,1024]{1,0:T(8,128)(2,1)S(1)}, u32[]{:S(2)}, u32[]{:S(2)}) %collective-permute-start.16) | collective-permute-done | bytes 262176 | tf_op jit(solution)/shard_map/ppermute | solution.py:36
  39.0 1.0 %collective-permute-start.17 = (bf16[256,1024]{1,0:T(8,128)(2,1)}, bf16[256,1024]{1,0:T(8,128)(2,1)}, u32[]{:S(2)}, u32[]{:S(2)}) collective-permute-start(bf16[256,1024]{1,0:T(8,128)(2,1)} %constant_dynamic-update-slice_fusion.2.refs_1_), channel_id=1, source_target_pairs={{0,2},{1,5},{2,0},{3,7},{4,6},{5,1},{6,4},{7,3},{8,10},{9,13},{10,... | collective-permute-start | bytes 1572872 | tf_op jit(solution)/shard_map/ppermute | solution.py:36
  40.0 1.5 %collective-permute-start = (bf16[64,1024]{1,0:T(8,128)(2,1)S(1)}, bf16[64,1024]{1,0:T(8,128)(2,1)}, u32[]{:S(2)}, u32[]{:S(2)}) collective-permute-start(bf16[64,1024]{1,0:T(8,128)(2,1)S(1)} %bitcast.31), channel_id=1, source_target_pairs={{0,16},{1,17},{2,18},{3,19},{4,20},{5,21},{6,22},{7,23},{8,24},{9,... | collective-permute-start | bytes 393224 | tf_op jit(solution)/shard_map/ppermute | solution.py:31
  42.1 1.1 %copy-done.1 = bf16[384,1024]{1,0:T(8,128)(2,1)S(1)} copy-done((bf16[384,1024]{1,0:T(8,128)(2,1)S(1)}, bf16[384,1024]{1,0:T(8,128)(2,1)}, u32[]{:S(2)}) %copy-start.1) | copy-done | bytes 786456
  43.2 1.1 %copy-done.4 = bf16[384,1024]{1,0:T(8,128)(2,1)S(1)} copy-done((bf16[384,1024]{1,0:T(8,128)(2,1)S(1)}, bf16[384,1024]{1,0:T(8,128)(2,1)}, u32[]{:S(2)}) %copy-start.4) | copy-done | bytes 786456
  44.3 3.7 %shard_map.115 = (bf16[128,1024]{1,0:T(8,128)(2,1)S(1)}, bf16[128,1024]{1,0:T(8,128)(2,1)S(1)}) custom-call(s32[1]{0:T(128)} %bitcast.1.me_ref, bf16[256,1152]{1,0:T(8,128)(2,1)} %collective-permute-done.3.refs_0_.refs_2_, bf16[1024,768]{1,0:T(8,128)(2,1)S(1)} %get-tuple-element.28.refs_1_.refs_3_, bf16[384,1024]{1,0:T(8,128)(2,1)S(1)} %copy-done.1, ...), custom_call_target="tpu_custom_call" | custom-call | flops 1207959552 | bytes 589824 | tf_op jit(solution)/shard_map/pallas_call | solution.py:301
  48.1 1.1 %collective-permute-start.6 = (bf16[128,1024]{1,0:T(8,128)(2,1)S(1)}, bf16[128,1024]{1,0:T(8,128)(2,1)S(1)}, u32[]{:S(2)}, u32[]{:S(2)}) collective-permute-start(bf16[128,1024]{1,0:T(8,128)(2,1)S(1)} %get-tuple-element.36), channel_id=1, source_target_pairs={{0,2},{1,5},{2,0},{3,7},{4,6},{5,1},{6,4},{7,3},{8,10},{9,13},{10,... | collective-permute-start | bytes 786440 | tf_op jit(solution)/shard_map/ppermute | solution.py:36
  49.2 3.6 %shard_map.116 = f32[256,1024]{1,0:T(8,128)S(1)} custom-call(s32[1]{0:T(128)} %bitcast.1.me_ref, bf16[256,1152]{1,0:T(8,128)(2,1)} %pad_maximum_fusion.refs_0_.refs_2_, bf16[1024,768]{1,0:T(8,128)(2,1)S(1)} %get-tuple-element.28.refs_1_.refs_3_, bf16[384,1024]{1,0:T(8,128)(2,1)S(1)} %copy-done.2, bf16[1024,768]{1,0:T(8,128)(2,1)S(1)} %get-tuple-element.30.refs_3_.refs_5_, ...), custom_call_target="tpu_custom_call" | custom-call | flops 1207959552 | bytes 589824 | tf_op jit(solution)/shard_map/pallas_call | solution.py:301
  52.8 1.0 %collective-permute-start.8 = (bf16[128,1024]{1,0:T(8,128)(2,1)S(1)}, bf16[128,1024]{1,0:T(8,128)(2,1)S(1)}, u32[]{:S(2)}, u32[]{:S(2)}) collective-permute-start(bf16[128,1024]{1,0:T(8,128)(2,1)S(1)} %get-tuple-element.37), channel_id=1, source_target_pairs={{0,2},{1,5},{2,0},{3,7},{4,6},{5,1},{6,4},{7,3},{8,10},{9,13},{10,... | collective-permute-start | bytes 786440 | tf_op jit(solution)/shard_map/ppermute | solution.py:36
  53.9 4.4 %shard_map.117 = (bf16[128,1024]{1,0:T(8,128)(2,1)S(1)}, bf16[128,1024]{1,0:T(8,128)(2,1)S(1)}) custom-call(s32[1]{0:T(128)} %bitcast.1.me_ref, bf16[256,1024]{1,0:T(8,128)(2,1)} %collective-permute-done.14.refs_0_, bf16[256,1024]{1,0:T(8,128)(2,1)} %collective-permute-done.17.refs_1_, bf16[256,1152]{1,0:T(8,128)(2,1)} %collective-permute-done.3.refs_0_.refs_2_, ...), custom_call_target="tpu_custom_call" | custom-call | flops 2013265920 | bytes 1638400 | tf_op jit(solution)/shard_map/pallas_call | solution.py:301
  58.3 1.1 %collective-permute-start.18 = (bf16[128,1024]{1,0:T(8,128)(2,1)S(1)}, bf16[128,1024]{1,0:T(8,128)(2,1)S(1)}, u32[]{:S(2)}, u32[]{:S(2)}) collective-permute-start(bf16[128,1024]{1,0:T(8,128)(2,1)S(1)} %get-tuple-element.46), channel_id=1, source_target_pairs={{0,2},{1,5},{2,0},{3,7},{4,6},{5,1},{6,4},{7,3},{8,10},{9,13},{10,... | collective-permute-start | bytes 786440 | tf_op jit(solution)/shard_map/ppermute | solution.py:36
  59.5 2.0 %collective-permute-start.7 = (bf16[128,1024]{1,0:T(8,128)(2,1)S(1)}, bf16[128,1024]{1,0:T(8,128)(2,1)S(1)}, u32[]{:S(2)}, u32[]{:S(2)}) collective-permute-start(bf16[128,1024]{1,0:T(8,128)(2,1)S(1)} %add_convert_fusion.3), channel_id=1, source_target_pairs={{0,4},{1,3},{2,6},{3,1},{4,0},{5,7},{6,2},{7,5},{8,12},{9,11},{10,... | collective-permute-start | bytes 786440 | tf_op jit(solution)/shard_map/ppermute | solution.py:36
  61.5 4.4 %shard_map.118 = f32[256,1024]{1,0:T(8,128)S(1)} custom-call(s32[1]{0:T(128)} %bitcast.1.me_ref, bf16[256,1024]{1,0:T(8,128)(2,1)} %pad_maximum_fusion.1.refs_0_, bf16[256,1024]{1,0:T(8,128)(2,1)} %constant_dynamic-update-slice_fusion.2.refs_1_, bf16[256,1152]{1,0:T(8,128)(2,1)} %pad_maximum_fusion.refs_0_.refs_2_, ...), custom_call_target="tpu_custom_call" | custom-call | flops 2013265920 | bytes 1638400 | tf_op jit(solution)/shard_map/pallas_call | solution.py:301
  65.9 1.1 %collective-permute-start.20 = (bf16[128,1024]{1,0:T(8,128)(2,1)S(1)}, bf16[128,1024]{1,0:T(8,128)(2,1)S(1)}, u32[]{:S(2)}, u32[]{:S(2)}) collective-permute-start(bf16[128,1024]{1,0:T(8,128)(2,1)S(1)} %get-tuple-element.47), channel_id=1, source_target_pairs={{0,2},{1,5},{2,0},{3,7},{4,6},{5,1},{6,4},{7,3},{8,10},{9,13},{10,... | collective-permute-start | bytes 786440 | tf_op jit(solution)/shard_map/ppermute | solution.py:36
  67.1 1.1 %collective-permute-start.19 = (bf16[128,1024]{1,0:T(8,128)(2,1)S(1)}, bf16[128,1024]{1,0:T(8,128)(2,1)S(1)}, u32[]{:S(2)}, u32[]{:S(2)}) collective-permute-start(bf16[128,1024]{1,0:T(8,128)(2,1)S(1)} %add_convert_fusion.1), channel_id=1, source_target_pairs={{0,4},{1,3},{2,6},{3,1},{4,0},{5,7},{6,2},{7,5},{8,12},{9,11},{10,... | collective-permute-start | bytes 786440 | tf_op jit(solution)/shard_map/ppermute | solution.py:36
  68.3 3.5 %collective-permute-start.10 = (bf16[64,1024]{1,0:T(8,128)(2,1)S(1)}, bf16[64,1024]{1,0:T(8,128)(2,1)S(1)}, u32[]{:S(2)}, u32[]{:S(2)}) collective-permute-start(bf16[64,1024]{1,0:T(8,128)(2,1)S(1)} %get-tuple-element.51), channel_id=1, source_target_pairs={{0,24},{1,25},{2,26},{3,27},{4,28},{5,29},{6,30},{7,31},{8,16},{9,... | collective-permute-start | bytes 393224 | tf_op jit(solution)/shard_map/ppermute | solution.py:31
  72.4 1.5 %collective-permute-start.9 = (bf16[64,1024]{1,0:T(8,128)(2,1)S(1)}, bf16[64,1024]{1,0:T(8,128)(2,1)S(1)}, u32[]{:S(2)}, u32[]{:S(2)}) collective-permute-start(bf16[64,1024]{1,0:T(8,128)(2,1)S(1)} %get-tuple-element.50), channel_id=1, source_target_pairs={{0,16},{1,17},{2,18},{3,19},{4,20},{5,21},{6,22},{7,23},{8,24},{9,... | collective-permute-start | bytes 393224 | tf_op jit(solution)/shard_map/ppermute | solution.py:31
  74.0 3.2 %collective-permute-start.22 = (bf16[64,1024]{1,0:T(8,128)(2,1)S(1)}, bf16[64,1024]{1,0:T(8,128)(2,1)S(1)}, u32[]{:S(2)}, u32[]{:S(2)}) collective-permute-start(bf16[64,1024]{1,0:T(8,128)(2,1)S(1)} %get-tuple-element.49), channel_id=1, source_target_pairs={{0,24},{1,25},{2,26},{3,27},{4,28},{5,29},{6,30},{7,31},{8,16},{9,... | collective-permute-start | bytes 393224 | tf_op jit(solution)/shard_map/ppermute | solution.py:31
  78.0 1.0 %collective-permute-done.9 = bf16[64,1024]{1,0:T(8,128)(2,1)S(1)} collective-permute-done((bf16[64,1024]{1,0:T(8,128)(2,1)S(1)}, bf16[64,1024]{1,0:T(8,128)(2,1)S(1)}, u32[]{:S(2)}, u32[]{:S(2)}) %collective-permute-start.9) | collective-permute-done | bytes 131104 | tf_op jit(solution)/shard_map/ppermute | solution.py:31
  79.0 1.6 %fusion = bf16[1,64,1024]{2,1,0:T(8,128)(2,1)} fusion(bf16[64,1024]{1,0:T(8,128)(2,1)S(1)} %collective-permute-done.10, bf16[64,1024]{1,0:T(8,128)(2,1)S(1)} %collective-permute-done.9, bf16[64,1024]{1,0:T(8,128)(2,1)} %collective-permute-done), kind=kLoop, calls=%fused_computation.11 | loop fusion | flops 393216 | bytes 524288 | tf_op jit(solution)/shard_map/broadcast_in_dim | solution.py:379
  80.7 2.6 %collective-permute-done.22 = bf16[64,1024]{1,0:T(8,128)(2,1)S(1)} collective-permute-done((bf16[64,1024]{1,0:T(8,128)(2,1)S(1)}, bf16[64,1024]{1,0:T(8,128)(2,1)S(1)}, u32[]{:S(2)}, u32[]{:S(2)}) %collective-permute-start.22) | collective-permute-done | bytes 131104 | tf_op jit(solution)/shard_map/ppermute | solution.py:31
  (61 shorter events, 8.7 us)
Async XLA Ops:
  0.6 3.1 %copy-start.8 = (bf16[1,1,1024,384]{3,2,1,0:T(8,128)(2,1)S(1)}, bf16[1,1,1024,384]{3,2,1,0:T(8,128)(2,1)}, u32[]{:S(2)}) copy-start(bf16[1,1,1024,384]{3,2,1,0:T(8,128)(2,1)} %param.18) | copy-start | bytes 2359300
  2.4 2.0 %copy-start.7 = (bf16[64,1152]{1,0:T(8,128)(2,1)S(1)}, bf16[64,1152]{1,0:T(8,128)(2,1)}, u32[]{:S(2)}) copy-start(bf16[64,1152]{1,0:T(8,128)(2,1)} %shard_map.113) | copy-start | bytes 442372
  2.4 5.7 %copy-start.6 = (bf16[1,1,384,1024]{3,2,1,0:T(8,128)(2,1)S(1)}, bf16[1,1,384,1024]{3,2,1,0:T(8,128)(2,1)}, u32[]{:S(2)}) copy-start(bf16[1,1,384,1024]{3,2,1,0:T(8,128)(2,1)} %param.19) | copy-start | bytes 2359300
  2.4 5.9 %copy-start.9 = (bf16[1,64,1024]{2,1,0:T(8,128)(2,1)S(1)}, bf16[1,64,1024]{2,1,0:T(8,128)(2,1)}, u32[]{:S(2)}) copy-start(bf16[1,64,1024]{2,1,0:T(8,128)(2,1)} %param.13) | copy-start | bytes 393220
  2.4 17.0 %copy-start.11 = (bf16[1,64,1024]{2,1,0:T(8,128)(2,1)S(1)}, bf16[1,64,1024]{2,1,0:T(8,128)(2,1)}, u32[]{:S(2)}) copy-start(bf16[1,64,1024]{2,1,0:T(8,128)(2,1)} %param.16) | copy-start | bytes 393220
  3.9 30.2 %collective-permute-start.4 = (bf16[1024,768]{1,0:T(8,128)(2,1)S(1)}, bf16[1024,768]{1,0:T(8,128)(2,1)S(1)}, u32[]{:S(2)}, u32[]{:S(2)}) collective-permute-start(bf16[1024,768]{1,0:T(8,128)(2,1)S(1)} %constant_dynamic-update-slice_fusion.refs_0_), channel_id=1, source_target_pairs={{0,1},{1,0},{2,3},{3,2},{4,5},{5,4},{6,7},{7,6},{8,9},{9,8},{10,11... | collective-permute-start | bytes 4718600 | tf_op jit(solution)/shard_map/ppermute | solution.py:36
  4.4 14.3 %collective-permute-start.1 = (bf16[64,1152]{1,0:T(8,128)(2,1)S(1)}, bf16[64,1152]{1,0:T(8,128)(2,1)S(1)}, u32[]{:S(2)}, u32[]{:S(2)}) collective-permute-start(bf16[64,1152]{1,0:T(8,128)(2,1)S(1)} %copy-done.7), channel_id=1, source_target_pairs={{0,8},{1,9},{2,10},{3,11},{4,12},{5,13},{6,14},{7,15},{8,0},{9,1},... | collective-permute-start | bytes 442376 | tf_op jit(solution)/shard_map/ppermute | solution.py:36
  8.1 26.0 %collective-permute-start.5 = (bf16[384,1024]{1,0:T(8,128)(2,1)S(1)}, bf16[384,1024]{1,0:T(8,128)(2,1)S(1)}, u32[]{:S(2)}, u32[]{:S(2)}) collective-permute-start(bf16[384,1024]{1,0:T(8,128)(2,1)S(1)} %bitcast.23), channel_id=1, source_target_pairs={{0,1},{1,0},{2,3},{3,2},{4,5},{5,4},{6,7},{7,6},{8,9},{9,8},{10,11... | collective-permute-start | bytes 2359304 | tf_op jit(solution)/shard_map/ppermute | solution.py:36
  8.3 14.5 %collective-permute-start.12 = (bf16[64,1024]{1,0:T(8,128)(2,1)S(1)}, bf16[64,1024]{1,0:T(8,128)(2,1)S(1)}, u32[]{:S(2)}, u32[]{:S(2)}) collective-permute-start(bf16[64,1024]{1,0:T(8,128)(2,1)S(1)} %bitcast.27), channel_id=1, source_target_pairs={{0,8},{1,9},{2,10},{3,11},{4,12},{5,13},{6,14},{7,15},{8,0},{9,1},... | collective-permute-start | bytes 393224 | tf_op jit(solution)/shard_map/ppermute | solution.py:36
  18.8 11.6 %collective-permute-start.2 = (bf16[128,1152]{1,0:T(8,128)(2,1)S(1)}, bf16[128,1152]{1,0:T(8,128)(2,1)S(1)}, u32[]{:S(2)}, u32[]{:S(2)}) collective-permute-start(bf16[128,1152]{1,0:T(8,128)(2,1)S(1)} %pad_maximum_fusion.2), channel_id=1, source_target_pairs={{0,4},{1,3},{2,6},{3,1},{4,0},{5,7},{6,2},{7,5},{8,12},{9,11},{10,... | collective-permute-start | bytes 884744 | tf_op jit(solution)/shard_map/ppermute | solution.py:36
  19.4 7.9 %collective-permute-start.15 = (bf16[64,1024]{1,0:T(8,128)(2,1)S(1)}, bf16[64,1024]{1,0:T(8,128)(2,1)S(1)}, u32[]{:S(2)}, u32[]{:S(2)}) collective-permute-start(bf16[64,1024]{1,0:T(8,128)(2,1)S(1)} %bitcast.32), channel_id=1, source_target_pairs={{0,8},{1,9},{2,10},{3,11},{4,12},{5,13},{6,14},{7,15},{8,0},{9,1},... | collective-permute-start | bytes 393224 | tf_op jit(solution)/shard_map/ppermute | solution.py:36
  22.8 9.5 %collective-permute-start.13 = (bf16[128,1024]{1,0:T(8,128)(2,1)S(1)}, bf16[128,1024]{1,0:T(8,128)(2,1)S(1)}, u32[]{:S(2)}, u32[]{:S(2)}) collective-permute-start(bf16[128,1024]{1,0:T(8,128)(2,1)S(1)} %pad_maximum_fusion.3), channel_id=1, source_target_pairs={{0,4},{1,3},{2,6},{3,1},{4,0},{5,7},{6,2},{7,5},{8,12},{9,11},{10,... | collective-permute-start | bytes 786440 | tf_op jit(solution)/shard_map/ppermute | solution.py:36
  27.3 10.3 %collective-permute-start.16 = (bf16[128,1024]{1,0:T(8,128)(2,1)S(1)}, bf16[128,1024]{1,0:T(8,128)(2,1)S(1)}, u32[]{:S(2)}, u32[]{:S(2)}) collective-permute-start(bf16[128,1024]{1,0:T(8,128)(2,1)S(1)} %pad_maximum_fusion.4), channel_id=1, source_target_pairs={{0,4},{1,3},{2,6},{3,1},{4,0},{5,7},{6,2},{7,5},{8,12},{9,11},{10,... | collective-permute-start | bytes 786440 | tf_op jit(solution)/shard_map/ppermute | solution.py:36
  31.2 10.8 %collective-permute-start.3 = (bf16[256,1152]{1,0:T(8,128)(2,1)}, bf16[256,1152]{1,0:T(8,128)(2,1)}, u32[]{:S(2)}, u32[]{:S(2)}) collective-permute-start(bf16[256,1152]{1,0:T(8,128)(2,1)} %pad_maximum_fusion.refs_0_.refs_2_), channel_id=1, source_target_pairs={{0,2},{1,5},{2,0},{3,7},{4,6},{5,1},{6,4},{7,3},{8,10},{9,13},{10,... | collective-permute-start | bytes 1769480 | tf_op jit(solution)/shard_map/ppermute | solution.py:36
  33.1 6.9 %copy-start.10 = (bf16[1,64,1024]{2,1,0:T(8,128)(2,1)S(1)}, bf16[1,64,1024]{2,1,0:T(8,128)(2,1)}, u32[]{:S(2)}) copy-start(bf16[1,64,1024]{2,1,0:T(8,128)(2,1)} %param.10) | copy-start | bytes 393220
  33.1 19.7 %collective-permute-start.14 = (bf16[256,1024]{1,0:T(8,128)(2,1)}, bf16[256,1024]{1,0:T(8,128)(2,1)}, u32[]{:S(2)}, u32[]{:S(2)}) collective-permute-start(bf16[256,1024]{1,0:T(8,128)(2,1)} %pad_maximum_fusion.1.refs_0_), channel_id=1, source_target_pairs={{0,2},{1,5},{2,0},{3,7},{4,6},{5,1},{6,4},{7,3},{8,10},{9,13},{10,... | collective-permute-start | bytes 1572872 | tf_op jit(solution)/shard_map/ppermute | solution.py:36
  39.0 14.8 %collective-permute-start.17 = (bf16[256,1024]{1,0:T(8,128)(2,1)}, bf16[256,1024]{1,0:T(8,128)(2,1)}, u32[]{:S(2)}, u32[]{:S(2)}) collective-permute-start(bf16[256,1024]{1,0:T(8,128)(2,1)} %constant_dynamic-update-slice_fusion.2.refs_1_), channel_id=1, source_target_pairs={{0,2},{1,5},{2,0},{3,7},{4,6},{5,1},{6,4},{7,3},{8,10},{9,13},{10,... | collective-permute-start | bytes 1572872 | tf_op jit(solution)/shard_map/ppermute | solution.py:36
  40.0 37.2 %collective-permute-start = (bf16[64,1024]{1,0:T(8,128)(2,1)S(1)}, bf16[64,1024]{1,0:T(8,128)(2,1)}, u32[]{:S(2)}, u32[]{:S(2)}) collective-permute-start(bf16[64,1024]{1,0:T(8,128)(2,1)S(1)} %bitcast.31), channel_id=1, source_target_pairs={{0,16},{1,17},{2,18},{3,19},{4,20},{5,21},{6,22},{7,23},{8,24},{9,... | collective-permute-start | bytes 393224 | tf_op jit(solution)/shard_map/ppermute | solution.py:31
  41.6 39.1 %collective-permute-start.11 = (bf16[64,1024]{1,0:T(8,128)(2,1)S(1)}, bf16[64,1024]{1,0:T(8,128)(2,1)S(1)}, u32[]{:S(2)}, u32[]{:S(2)}) collective-permute-start(bf16[64,1024]{1,0:T(8,128)(2,1)S(1)} %bitcast.34), channel_id=1, source_target_pairs={{0,16},{1,17},{2,18},{3,19},{4,20},{5,21},{6,22},{7,23},{8,24},{9,... | collective-permute-start | bytes 393224 | tf_op jit(solution)/shard_map/ppermute | solution.py:31
  42.1 1.1 %copy-start.1 = (bf16[384,1024]{1,0:T(8,128)(2,1)S(1)}, bf16[384,1024]{1,0:T(8,128)(2,1)}, u32[]{:S(2)}) copy-start(bf16[384,1024]{1,0:T(8,128)(2,1)} %copy-done) | copy-start | bytes 2359300
  44.3 4.9 %copy-start.2 = (bf16[384,1024]{1,0:T(8,128)(2,1)S(1)}, bf16[384,1024]{1,0:T(8,128)(2,1)}, u32[]{:S(2)}) copy-start(bf16[384,1024]{1,0:T(8,128)(2,1)} %copy-done) | copy-start | bytes 2359300
  44.3 4.9 %copy-start.5 = (bf16[384,1024]{1,0:T(8,128)(2,1)S(1)}, bf16[384,1024]{1,0:T(8,128)(2,1)}, u32[]{:S(2)}) copy-start(bf16[384,1024]{1,0:T(8,128)(2,1)} %copy-done.3) | copy-start | bytes 2359300
  48.1 11.3 %collective-permute-start.6 = (bf16[128,1024]{1,0:T(8,128)(2,1)S(1)}, bf16[128,1024]{1,0:T(8,128)(2,1)S(1)}, u32[]{:S(2)}, u32[]{:S(2)}) collective-permute-start(bf16[128,1024]{1,0:T(8,128)(2,1)S(1)} %get-tuple-element.36), channel_id=1, source_target_pairs={{0,2},{1,5},{2,0},{3,7},{4,6},{5,1},{6,4},{7,3},{8,10},{9,13},{10,... | collective-permute-start | bytes 786440 | tf_op jit(solution)/shard_map/ppermute | solution.py:36
  52.8 14.2 %collective-permute-start.8 = (bf16[128,1024]{1,0:T(8,128)(2,1)S(1)}, bf16[128,1024]{1,0:T(8,128)(2,1)S(1)}, u32[]{:S(2)}, u32[]{:S(2)}) collective-permute-start(bf16[128,1024]{1,0:T(8,128)(2,1)S(1)} %get-tuple-element.37), channel_id=1, source_target_pairs={{0,2},{1,5},{2,0},{3,7},{4,6},{5,1},{6,4},{7,3},{8,10},{9,13},{10,... | collective-permute-start | bytes 786440 | tf_op jit(solution)/shard_map/ppermute | solution.py:36
  58.3 7.6 %collective-permute-start.18 = (bf16[128,1024]{1,0:T(8,128)(2,1)S(1)}, bf16[128,1024]{1,0:T(8,128)(2,1)S(1)}, u32[]{:S(2)}, u32[]{:S(2)}) collective-permute-start(bf16[128,1024]{1,0:T(8,128)(2,1)S(1)} %get-tuple-element.46), channel_id=1, source_target_pairs={{0,2},{1,5},{2,0},{3,7},{4,6},{5,1},{6,4},{7,3},{8,10},{9,13},{10,... | collective-permute-start | bytes 786440 | tf_op jit(solution)/shard_map/ppermute | solution.py:36
  59.5 8.7 %collective-permute-start.7 = (bf16[128,1024]{1,0:T(8,128)(2,1)S(1)}, bf16[128,1024]{1,0:T(8,128)(2,1)S(1)}, u32[]{:S(2)}, u32[]{:S(2)}) collective-permute-start(bf16[128,1024]{1,0:T(8,128)(2,1)S(1)} %add_convert_fusion.3), channel_id=1, source_target_pairs={{0,4},{1,3},{2,6},{3,1},{4,0},{5,7},{6,2},{7,5},{8,12},{9,11},{10,... | collective-permute-start | bytes 786440 | tf_op jit(solution)/shard_map/ppermute | solution.py:36
  65.9 6.4 %collective-permute-start.20 = (bf16[128,1024]{1,0:T(8,128)(2,1)S(1)}, bf16[128,1024]{1,0:T(8,128)(2,1)S(1)}, u32[]{:S(2)}, u32[]{:S(2)}) collective-permute-start(bf16[128,1024]{1,0:T(8,128)(2,1)S(1)} %get-tuple-element.47), channel_id=1, source_target_pairs={{0,2},{1,5},{2,0},{3,7},{4,6},{5,1},{6,4},{7,3},{8,10},{9,13},{10,... | collective-permute-start | bytes 786440 | tf_op jit(solution)/shard_map/ppermute | solution.py:36
  67.1 6.8 %collective-permute-start.19 = (bf16[128,1024]{1,0:T(8,128)(2,1)S(1)}, bf16[128,1024]{1,0:T(8,128)(2,1)S(1)}, u32[]{:S(2)}, u32[]{:S(2)}) collective-permute-start(bf16[128,1024]{1,0:T(8,128)(2,1)S(1)} %add_convert_fusion.1), channel_id=1, source_target_pairs={{0,4},{1,3},{2,6},{3,1},{4,0},{5,7},{6,2},{7,5},{8,12},{9,11},{10,... | collective-permute-start | bytes 786440 | tf_op jit(solution)/shard_map/ppermute | solution.py:36
  68.3 9.7 %collective-permute-start.10 = (bf16[64,1024]{1,0:T(8,128)(2,1)S(1)}, bf16[64,1024]{1,0:T(8,128)(2,1)S(1)}, u32[]{:S(2)}, u32[]{:S(2)}) collective-permute-start(bf16[64,1024]{1,0:T(8,128)(2,1)S(1)} %get-tuple-element.51), channel_id=1, source_target_pairs={{0,24},{1,25},{2,26},{3,27},{4,28},{5,29},{6,30},{7,31},{8,16},{9,... | collective-permute-start | bytes 393224 | tf_op jit(solution)/shard_map/ppermute | solution.py:31
  72.4 6.7 %collective-permute-start.9 = (bf16[64,1024]{1,0:T(8,128)(2,1)S(1)}, bf16[64,1024]{1,0:T(8,128)(2,1)S(1)}, u32[]{:S(2)}, u32[]{:S(2)}) collective-permute-start(bf16[64,1024]{1,0:T(8,128)(2,1)S(1)} %get-tuple-element.50), channel_id=1, source_target_pairs={{0,16},{1,17},{2,18},{3,19},{4,20},{5,21},{6,22},{7,23},{8,24},{9,... | collective-permute-start | bytes 393224 | tf_op jit(solution)/shard_map/ppermute | solution.py:31
  74.0 9.2 %collective-permute-start.22 = (bf16[64,1024]{1,0:T(8,128)(2,1)S(1)}, bf16[64,1024]{1,0:T(8,128)(2,1)S(1)}, u32[]{:S(2)}, u32[]{:S(2)}) collective-permute-start(bf16[64,1024]{1,0:T(8,128)(2,1)S(1)} %get-tuple-element.49), channel_id=1, source_target_pairs={{0,24},{1,25},{2,26},{3,27},{4,28},{5,29},{6,30},{7,31},{8,16},{9,... | collective-permute-start | bytes 393224 | tf_op jit(solution)/shard_map/ppermute | solution.py:31
  77.2 6.0 %collective-permute-start.21 = (bf16[64,1024]{1,0:T(8,128)(2,1)S(1)}, bf16[64,1024]{1,0:T(8,128)(2,1)S(1)}, u32[]{:S(2)}, u32[]{:S(2)}) collective-permute-start(bf16[64,1024]{1,0:T(8,128)(2,1)S(1)} %get-tuple-element.48), channel_id=1, source_target_pairs={{0,16},{1,17},{2,18},{3,19},{4,20},{5,21},{6,22},{7,23},{8,24},{9,... | collective-permute-start | bytes 393224 | tf_op jit(solution)/shard_map/ppermute | solution.py:31
  (3 other events, 2.9 us)

commit v4 on v3

--- a/solution.py
+++ b/solution.py
@@ -11,14 +11,9 @@
 BF16 = jnp.bfloat16
 LANES = 128
 VMEM_LIMIT = 20 * 1024 * 1024
-COST = 1.0
+TOGETHER = "f,c,b,f,c,b,f,c,b,Fs,F,F,Fk,Bs,B,B,F,Bk,B,F,B"
 IN_TURN = "f,Fs,F,Fk,F,b:Fk,c:Fk,Bs,B,Bk,B"
-JOIN = False
-LOAD = True
-HBM = False
-GU = 1
 LITTLE = pl.CostEstimate(flops=1, bytes_accessed=1, transcendentals=0)
-PLAN = dict(f="P", b="P", c="P", rf="P", rb="P", odd="QQ", cut="FB", ops="f,c,b,f,c,b,f,c:W,b,Fs,F,F,Fk,Bs,B,B,F,Bk:F0,B,F,B", step=4)
 
 
 def passed_along(block, distance, paths, bit=0):
@@ -37,64 +32,28 @@
 
 
 class Spread:
-    def __init__(self, block, paths, bits, cut):
-        self.paths, self.bits, self.cut, self.came, self.held, self.order = paths, bits, cut, [], block, [0]
-        self.parts, self.orders = [], []
+    def __init__(self, block, paths, bits):
+        self.paths, self.bits = paths, bits
+        self.came, self.held, self.order = [], block, [0]
 
     def done(self):
-        return len(self.came) == len(self.bits) + self.cut
+        return len(self.came) == len(self.bits)
 
     def step(self, after=()):
-        at, last = len(self.came), len(self.bits) - 1
-        bit = self.bits[min(at, last)]
-        if at <= last:
-            parts = [self.held] + ([self.came[-1]] if 0 < at and (at < last or not self.cut) else [])
-            parts = behind(parts, after)
-            if len(parts) > 1:
-                self.held = joined(parts, 0) if JOIN else jnp.concatenate(parts, axis=0)
-                self.order = self.order + [r | self.bits[at - 1] for r in self.order]
-            else:
-                self.held = parts[0]
-            payload, order = self.held, self.order
-        else:
-            (payload,) = behind([self.came[last - 1]], after)
-            order = [r | self.bits[last - 1] for r in self.order]
-        self.came.append(swapped(payload, self.paths, bit))
-        if at >= last:
-            self.parts += [payload, self.came[-1]]
-            self.orders += [order, [r | bit for r in order]]
+        at = len(self.came)
+        parts = behind([self.held] + self.came[-1:], after)
+        self.held = parts[0] if at == 0 else jnp.concatenate(parts, axis=0)
+        if at:
+            self.order = self.order + [r | self.bits[at - 1] for r in self.order]
+        self.came.append(swapped(self.held, self.paths, self.bits[at]))
+        self.parts = [self.held, self.came[-1]]
+        self.orders = [self.order, [r | self.bits[at] for r in self.order]]
 
 
 def behind(arrays, others):
     if not others:
         return list(arrays)
     return list(lax.optimization_barrier((*arrays, *others))[: len(arrays)])
-
-
-def joining_kernel(axis, *refs):
-    *parts, out_ref, sems = refs
-    at, copies = 0, []
-    for number, part in enumerate(parts):
-        here = [slice(None)] * 2
-        here[axis] = pl.ds(at, part.shape[axis])
-        copies.append(pltpu.make_async_copy(part, out_ref.at[tuple(here)], sems.at[number]))
-        copies[-1].start()
-        at += part.shape[axis]
-    for copy in copies:
-        copy.wait()
-
-
-def joined(parts, axis):
-    shape = list(parts[0].shape)
-    shape[axis] = sum(part.shape[axis] for part in parts)
-    return pl.pallas_call(
-        functools.partial(joining_kernel, axis),
-        out_shape=jax.ShapeDtypeStruct(tuple(shape), parts[0].dtype),
-        in_specs=[pl.BlockSpec(memory_space=pl.ANY)] * len(parts),
-        out_specs=pl.BlockSpec(memory_space=pltpu.VMEM),
-        scratch_shapes=[pltpu.SemaphoreType.DMA((len(parts),))],
-        cost_estimate=LITTLE,
-    )(*parts)
 
 
 def halving_order(bits):
@@ -110,24 +69,24 @@
         self.paths, self.bits, self.distance = paths, bits, distance
 
     def done(self):
-        return len(self.came) == len(self.bits) + len(self.sends)
+        return len(self.came) == len(self.bits) + 2
 
     def step(self, after=()):
-        at, first = len(self.came), len(self.sends)
-        if at < first:
+        at = len(self.came)
+        if at < 2:
             (send,) = behind([self.sends[at]], after)
             self.came.append(swapped(send, self.paths, self.bits[0]))
             return
-        if at == first and first == 2:
-            half = self.keep.shape[0] // 2
+        half = self.keep.shape[0] // 2
+        if at == 2:
             send, self.keep = self.keep[:half] + self.came[0].astype(F32), self.keep[half:]
         else:
             total = self.keep + self.came[-1].astype(F32)
-            if at == 3 and first == 2:
+            if at == 3:
                 total = total + self.came[1].astype(F32)
             half = total.shape[0] // 2
             send, self.keep = total[:half], total[half:]
-        bit = self.bits[at - first + 1]
+        bit = self.bits[at - 1]
         if bit != self.bits[-1]:
             (send,) = behind([send.astype(BF16)], after)
             self.came.append(swapped(send, self.paths, bit))
@@ -199,32 +158,37 @@
     return times_transposed(both, gate_up[...])
 
 
-def loading_kernel(*refs):
-    sems = refs[-1]
-    count = len(refs) // 2
-    copies = [pltpu.make_async_copy(refs[n], refs[count + n], sems.at[n]) for n in range(count)]
-    for copy in copies:
-        copy.start()
+def loading_kernel(places, *refs):
+    *parts, out_ref, sems = refs
+    copies = []
+    for number, (part, row) in enumerate(zip(parts, places, strict=True)):
+        there = out_ref.at[pl.ds(row, part.shape[0]), pl.ds(0, part.shape[1])]
+        copies.append(pltpu.make_async_copy(part, there, sems.at[number]))
+        copies[-1].start()
     for copy in copies:
         copy.wait()
 
 
 def loaded(arrays):
-    return pl.pallas_call(
-        loading_kernel,
-        out_shape=[jax.ShapeDtypeStruct(array.shape, array.dtype) for array in arrays],
+    places = [sum(array.shape[0] for array in arrays[:number]) for number in range(len(arrays))]
+    shape = (sum(array.shape[0] for array in arrays), max(array.shape[1] for array in arrays))
+    array = pl.pallas_call(
+        functools.partial(loading_kernel, places),
+        out_shape=jax.ShapeDtypeStruct(shape, arrays[0].dtype),
         in_specs=[pl.BlockSpec(memory_space=pl.ANY)] * len(arrays),
-        out_specs=[pl.BlockSpec(memory_space=pltpu.VMEM)] * len(arrays),
+        out_specs=pl.BlockSpec(memory_space=pltpu.VMEM),
         scratch_shapes=[pltpu.SemaphoreType.DMA((len(arrays),))],
         compiler_params=pltpu.CompilerParams(vmem_limit_bytes=VMEM_LIMIT),
         cost_estimate=LITTLE,
     )(*arrays)
-
-
-def expert_kernel(each, topk, first, rows, step, copies, me_ref, *refs):
+    return array, [(row, *part.shape) for row, part in zip(places, arrays, strict=True)]
+
+
+def expert_kernel(each, topk, first, rows, step, copies, matrices, me_ref, *refs):
     count = 1 + max(operand for each_copy in copies for operand, *_ in each_copy)
     buffers, sems = refs[-1 - len(copies) : -1], refs[-1]
-    weights, out_refs = refs[count : count + 4], refs[count + 4 : -1 - len(copies)]
+    out_refs = refs[count + 1 : -1 - len(copies)]
+    weights = [refs[count].at[pl.ds(row, depth), pl.ds(0, across)] for row, depth, across in matrices]
     begins = [0]
     for pieces in copies:
         begins.append(begins[-1] + len(pieces))
@@ -272,7 +236,8 @@
 
 
 def weighted(each, first, topk, rows, step, wanted, outputs, place, words, inputs, weights):
-    width, hidden_width = weights[1].shape[1], weights[1].shape[0]
+    weights, matrices = weights
+    hidden_width, width = matrices[1][1:]
     operands, copies, scratch = [], [], []
     length = len(wanted) * rows
 
@@ -299,20 +264,20 @@
         rows_from(parts, orders, width, 0)
     rows_from(*words, width)
     return pl.pallas_call(
-        functools.partial(expert_kernel, each, topk, first, rows, step, copies),
+        functools.partial(expert_kernel, each, topk, first, rows, step, copies, matrices),
         out_shape=[jax.ShapeDtypeStruct((number * rows, width), dtype) for number, dtype in outputs],
         in_specs=[pl.BlockSpec(memory_space=pltpu.SMEM)]
-        + [pl.BlockSpec(memory_space=pltpu.HBM if HBM else pl.ANY)] * len(operands)
-        + [pl.BlockSpec(memory_space=pltpu.VMEM)] * len(weights),
+        + [pl.BlockSpec(memory_space=pl.ANY)] * len(operands)
+        + [pl.BlockSpec(memory_space=pltpu.VMEM)],
         out_specs=[pl.BlockSpec(memory_space=pltpu.VMEM)] * len(outputs),
         scratch_shapes=scratch + [pltpu.SemaphoreType.DMA((sum(map(len, copies)),))],
         compiler_params=pltpu.CompilerParams(vmem_limit_bytes=VMEM_LIMIT),
         cost_estimate=pl.CostEstimate(
-            flops=int(COST * 4 * (2 * len(inputs) + 1) * length * width * hidden_width),
-            bytes_accessed=int(COST * sum(a.size * a.dtype.itemsize for a in operands)),
+            flops=4 * (2 * len(inputs) + 1) * length * width * hidden_width,
+            bytes_accessed=sum(a.size * a.dtype.itemsize for a in operands),
             transcendentals=0,
         ),
-    )(place, *operands, *weights)
+    )(place, *operands, weights)
 
 
 def on_device(
@@ -336,15 +301,9 @@
     while 2 << len(bits) < experts:
         bits.insert(0, 2 << len(bits))
     blocks = experts // 2
-    orders = {
-        "P": bits,
-        "Q": bits[:-2] + [bits[-1], bits[-2]],
-        "R": bits[-1:] + bits[:-1],
-    }
-    plan = PLAN
-    even = dict(zip(bits, bits))
-    odd = {kind: dict(zip(bits, orders[plan["odd"][kind != "f"]])) for kind in "fbc"}
-    paths = {kind: (even, odd[kind]) for kind in "fbc"}
+    paths = (dict(zip(bits, bits)), dict(zip(bits, bits[:-2] + [bits[-1], bits[-2]])))
+    back = bits[::-1]
+    order = halving_order(back)
 
     arrays = {"f": x_forward[0], "b": x_backward[0], "c": cotangent[0]}
     words = [route_forward[0], gate_forward[0], route_backward[0], gate_backward[0]]
@@ -353,74 +312,54 @@
     arrays["f"] = packed(arrays["f"], *words)
     down0 = w_down[0, 0]
     pair = [w_gate[0, 0], w_up[0, 0]]
-    if GU == 1:
-        *pair, down0 = behind([*pair, down0], [arrays["f"]])
-    if GU in ("f", "b", "c"):
-        held[GU] = Spread(arrays[GU], paths[GU], orders[plan[GU]], GU in plan["cut"])
-        held[GU].step()
-        *pair, down0 = behind([*pair, down0], held[GU].came)
+    *pair, down0 = behind([*pair, down0], [arrays["f"]])
     gate_up0 = jnp.concatenate(pair, axis=1)
     chip = [{1: 1}] * 2
     gate_up1, down1 = swapped(gate_up0, chip, 1), swapped(down0, chip, 1)
-    weights = [gate_up0, down0, gate_up1, down1]
-    if LOAD:
-        weights = loaded(weights)
-
-    step = min(plan["step"], blocks // 2)
+    weights = loaded([gate_up0, down0, gate_up1, down1])
+
+    step = min(4, blocks // 2)
     place = jnp.reshape(me, (1,))
 
-    class Far:
-        came = [passed_along(x_forward[0], 1, [{}, {}]), passed_along(cotangent[0], -1, [{}, {}])]
-
-    held["y"] = Far
-
-    def arrived(far, kind):
+    far = passed_along(x_forward[0], 1, [{}, {}]), passed_along(cotangent[0], -1, [{}, {}])
+
+    def arrived(rows_far, kind):
         one, other = held[kind].came[-2:]
-        return (far.astype(F32) + (one.astype(F32) + other.astype(F32))).astype(BF16)[None]
-
-    outs, keeps = {"W": weights[0]}, {}
-    items = (plan["ops"] if len(bits) < 4 else IN_TURN).split(",")
-    left = {name: [item[0] for item in items if item[1:2] not in ("s", "k", "a")].count(name) for name in "fbcFB"}
-    first_left = dict(left)
+        return (rows_far.astype(F32) + (one.astype(F32) + other.astype(F32))).astype(BF16)[None]
+
+    outs = {}
+    items = (TOGETHER if len(bits) < 4 else IN_TURN).split(",")
+    left = {name: [item.split(":")[0] for item in items].count(name) for name in "fbcFB"}
     for item in items:
         name, _, after = item.partition(":")
-        after = [
-            outs[other] if other in outs else held[other[0]].came[int(other[1])]
-            for other in after.split()
-        ]
+        after = [outs[other] for other in after.split()]
         kind = name[0].lower()
         if len(name) == 1:
             if name not in held:
-                held[name] = Spread(arrays[name], paths[kind], orders[plan[name]], name in plan["cut"])
-            if name != GU or left[name] < first_left[name]:
-                held[name].step(after)
+                held[name] = Spread(arrays[name], paths, bits)
+            held[name].step(after)
             left[name] -= 1
             while left[name] == 0 and not held[name].done():
                 held[name].step()
             continue
-        back = orders[plan["r" + kind]][::-1]
-        order = halving_order(back)
         takes = [(held[other].parts, held[other].orders) for other in ("f" if kind == "f" else "bc")]
         carrier = (held["f"].parts, held["f"].orders, held["f"].held.shape[1] - width)
         each, first = (forward_rows, 0) if kind == "f" else (backward_rows, 4)
         half = len(order) // 2
-        sends = [(half // 2, BF16)] * 2 if name[0] in plan["cut"] else [(half, BF16)]
         wanted, results = {
-            "s": (order[:half], sends),
+            "s": (order[:half], [(half // 2, BF16)] * 2),
             "k": (order[half:], [(half, F32)]),
-            "a": (order, sends + [(half, F32)]),
         }[name[1]]
         (place,) = behind([place], after)
         out = weighted(each, first, topk, rows, step, wanted, results, place, carrier, takes, weights)
         place, *out = lax.optimization_barrier((place, *out))
         outs[name] = out[0]
-        keeps[name[0]] = keeps.get(name[0]) if name[1] == "s" else out.pop()
-        if name[1] != "k":
-            held[name[0]] = Return(out, paths[kind], back, 1 if kind == "f" else -1)
-        if name[0] in held:
-            held[name[0]].keep = keeps[name[0]]
-
-    return arrived(held["y"].came[0], "F"), arrived(held["y"].came[1], "B")
+        if name[1] == "s":
+            held[name[0]] = Return(out, paths, back, 1 if kind == "f" else -1)
+        else:
+            held[name[0]].keep = out[0]
+
+    return arrived(far[0], "F"), arrived(far[1], "B")
 
 
 def solution(mesh):

time: 84.3 us -> 83.9 us (level)
  waiting for transfers between devices: 19.8 us -> 25.8 us
  local copies, waits for them, and re-layouts: 7.06 us -> 1.48 us
  other arithmetic: 4.39 us -> 1.91 us
  Pallas kernels: 18.2 us -> 19.1 us
    ppermute x17, waiting for transfers between devices: 16.2 us -> 21.7 us  [swapped(): return lax.ppermute(block, 'expert', route)]
    unnamed x26 -> x11, local copies, waits for them, and re-layouts: 6.13 us -> 1.28 us
    pallas_call x1, Pallas kernels: 0.36 us -> 2.1 us  [loaded(): pl.pallas_call(functools.partial(loading_kernel, places), out_shape=jax.S...]
    concatenate x5 -> x6, other arithmetic: 1.76 us -> 0.17 us  [step(): self.held = parts[0] if at == 0 else jnp.concatenate(parts, axis=0)]
    broadcast_in_dim x2, other arithmetic: 2.32 us -> 1.42 us  [arrived(): (rows_far.astype(F32) + (one.astype(F32) + other.astype(F32))).astype(BF16)]
    pallas_call x4, Pallas kernels: 16.1 us -> 15.2 us  [weighted(): pl.pallas_call(functools.partial(expert_kernel, each, topk, first, rows,...]
  transfers between devices with their start and end apart: 23 -> 23, of which waited for: 6 -> 7; matrix products, arithmetic and copies ran while one was open for 6% -> 1% of each run, Pallas kernels for 20% -> 21%
where the time goes in v4:
time: 83.9 us; the launch traced here: 83.4 us
  starting transfers between devices  34.3 us (41%)
  waiting for transfers between devices  25.8 us (31%)
  Pallas kernels  19.1 us (23%)
  other arithmetic  1.91 us (2%)
  local copies, waits for them, and re-layouts  1.48 us (2%)
    ppermute x17, starting transfers between devices, swapped(): return lax.ppermute(block, 'expert', route)  22.7 us
    ppermute x17, waiting for transfers between devices, swapped(): return lax.ppermute(block, 'expert', route)  21.7 us
    pallas_call x4, Pallas kernels, weighted(): pl.pallas_call(functools.partial(expert_kernel, each, topk, first, rows,...  15.2 us
    ppermute x6, starting transfers between devices, passed_along(): return lax.ppermute(block, ('section', 'expert'), route)  11.6 us
    ppermute x6, waiting for transfers between devices, passed_along(): return lax.ppermute(block, ('section', 'expert'), route)  4.1 us
    pallas_call x1, Pallas kernels, loaded(): pl.pallas_call(functools.partial(loading_kernel, places), out_shape=jax.S...  2.1 us
    pallas_call x1, Pallas kernels, packed(): pl.pallas_call(packing_kernel, out_shape=jax.ShapeDtypeStruct((length, wi...  1.77 us
  transfers between devices with their start and end apart: 23, of which 7 were waited for; matrix products, arithmetic and copies ran while one was open for 1% of the time, Pallas kernels for 21%

profile of v4, /device:TPU:0, one launch (start us, length us, event | category | flops | bytes accessed | tf_op | source)
XLA Modules:
  0.0 83.4 jit_solution(6977827431556514313)
XLA Ops:
  0.6 1.8 %shard_map.113 = bf16[64,1152]{1,0:T(8,128)(2,1)} custom-call(bf16[64,1024]{1,0:T(8,128)(2,1)} %bitcast.32, s32[8,64]{1,0:T(8,128)} %bitcast.34, f32[8,64]{1,0:T(8,128)} %bitcast.35, s32[8,64]{1,0:T(8,128)} %bitcast.36, f32[8,64]{1,0:T(8,128)} %bitcast.37), custom_call_target="tpu_custom_call" | custom-call | flops 1 | bytes 1 | tf_op jit(solution)/shard_map/pallas_call | solution.py:118
  2.4 1.3 %constant_dynamic-update-slice_fusion.1 = bf16[1024,768]{1,0:T(8,128)(2,1)S(1)} fusion(bf16[1024,384]{1,0:T(8,128)(2,1)} %bitcast.23), kind=kLoop, calls=%fused_computation.15 | loop fusion | bytes 1572864
  4.4 3.7 %collective-permute-start.1 = (bf16[64,1152]{1,0:T(8,128)(2,1)S(1)}, bf16[64,1152]{1,0:T(8,128)(2,1)S(1)}, u32[]{:S(2)}, u32[]{:S(2)}) collective-permute-start(bf16[64,1152]{1,0:T(8,128)(2,1)S(1)} %copy-done), channel_id=1, source_target_pairs={{0,8},{1,9},{2,10},{3,11},{4,12},{5,13},{6,14},{7,15},{8,0},{9,1},... | collective-permute-start | bytes 442376 | tf_op jit(solution)/shard_map/ppermute | solution.py:31
  8.1 10.6 %collective-permute-done.1 = bf16[64,1152]{1,0:T(8,128)(2,1)S(1)} collective-permute-done((bf16[64,1152]{1,0:T(8,128)(2,1)S(1)}, bf16[64,1152]{1,0:T(8,128)(2,1)S(1)}, u32[]{:S(2)}, u32[]{:S(2)}) %collective-permute-start.1) | collective-permute-done | bytes 147488 | tf_op jit(solution)/shard_map/ppermute | solution.py:31
  19.3 3.4 %collective-permute-start.15 = (bf16[64,1024]{1,0:T(8,128)(2,1)S(1)}, bf16[64,1024]{1,0:T(8,128)(2,1)S(1)}, u32[]{:S(2)}, u32[]{:S(2)}) collective-permute-start(bf16[64,1024]{1,0:T(8,128)(2,1)S(1)} %bitcast.28), channel_id=1, source_target_pairs={{0,8},{1,9},{2,10},{3,11},{4,12},{5,13},{6,14},{7,15},{8,0},{9,1},... | collective-permute-start | bytes 393224 | tf_op jit(solution)/shard_map/ppermute | solution.py:31
  22.7 1.0 %collective-permute-start.13 = (bf16[128,1024]{1,0:T(8,128)(2,1)S(1)}, bf16[128,1024]{1,0:T(8,128)(2,1)S(1)}, u32[]{:S(2)}, u32[]{:S(2)}) collective-permute-start(bf16[128,1024]{1,0:T(8,128)(2,1)S(1)} %pad_maximum_fusion.4), channel_id=1, source_target_pairs={{0,4},{1,3},{2,6},{3,1},{4,0},{5,7},{6,2},{7,5},{8,12},{9,11},{10,... | collective-permute-start | bytes 786440 | tf_op jit(solution)/shard_map/ppermute | solution.py:31
  23.8 3.5 %collective-permute-done.15 = bf16[64,1024]{1,0:T(8,128)(2,1)S(1)} collective-permute-done((bf16[64,1024]{1,0:T(8,128)(2,1)S(1)}, bf16[64,1024]{1,0:T(8,128)(2,1)S(1)}, u32[]{:S(2)}, u32[]{:S(2)}) %collective-permute-start.15) | collective-permute-done | bytes 131104 | tf_op jit(solution)/shard_map/ppermute | solution.py:31
  27.3 3.0 %collective-permute-start.16 = (bf16[128,1024]{1,0:T(8,128)(2,1)S(1)}, bf16[128,1024]{1,0:T(8,128)(2,1)S(1)}, u32[]{:S(2)}, u32[]{:S(2)}) collective-permute-start(bf16[128,1024]{1,0:T(8,128)(2,1)S(1)} %pad_maximum_fusion.5), channel_id=1, source_target_pairs={{0,4},{1,3},{2,6},{3,1},{4,0},{5,7},{6,2},{7,5},{8,12},{9,11},{10,... | collective-permute-start | bytes 786440 | tf_op jit(solution)/shard_map/ppermute | solution.py:31
  30.4 1.1 %collective-permute-start.3 = (bf16[256,1152]{1,0:T(8,128)(2,1)S(1)}, bf16[256,1152]{1,0:T(8,128)(2,1)}, u32[]{:S(2)}, u32[]{:S(2)}) collective-permute-start(bf16[256,1152]{1,0:T(8,128)(2,1)S(1)} %pad_maximum_fusion.refs_0_.refs_2_), channel_id=1, source_target_pairs={{0,2},{1,5},{2,0},{3,7},{4,6},{5,1},{6,4},{7,3},{8,10},{9,13},{10,... | collective-permute-start | bytes 1769480 | tf_op jit(solution)/shard_map/ppermute | solution.py:31
  31.5 1.4 %collective-permute-done.13 = bf16[128,1024]{1,0:T(8,128)(2,1)S(1)} collective-permute-done((bf16[128,1024]{1,0:T(8,128)(2,1)S(1)}, bf16[128,1024]{1,0:T(8,128)(2,1)S(1)}, u32[]{:S(2)}, u32[]{:S(2)}) %collective-permute-start.13) | collective-permute-done | bytes 262176 | tf_op jit(solution)/shard_map/ppermute | solution.py:31
  32.9 0.9 %collective-permute-start.14 = (bf16[256,1024]{1,0:T(8,128)(2,1)S(1)}, bf16[256,1024]{1,0:T(8,128)(2,1)}, u32[]{:S(2)}, u32[]{:S(2)}) collective-permute-start(bf16[256,1024]{1,0:T(8,128)(2,1)S(1)} %pad_maximum_fusion.1.refs_0_), channel_id=1, source_target_pairs={{0,2},{1,5},{2,0},{3,7},{4,6},{5,1},{6,4},{7,3},{8,10},{9,13},{10,... | collective-permute-start | bytes 1572872 | tf_op jit(solution)/shard_map/ppermute | solution.py:31
  33.8 4.7 %collective-permute-done.16 = bf16[128,1024]{1,0:T(8,128)(2,1)S(1)} collective-permute-done((bf16[128,1024]{1,0:T(8,128)(2,1)S(1)}, bf16[128,1024]{1,0:T(8,128)(2,1)S(1)}, u32[]{:S(2)}, u32[]{:S(2)}) %collective-permute-start.16) | collective-permute-done | bytes 262176 | tf_op jit(solution)/shard_map/ppermute | solution.py:31
  38.5 0.9 %collective-permute-start.17 = (bf16[256,1024]{1,0:T(8,128)(2,1)S(1)}, bf16[256,1024]{1,0:T(8,128)(2,1)}, u32[]{:S(2)}, u32[]{:S(2)}) collective-permute-start(bf16[256,1024]{1,0:T(8,128)(2,1)S(1)} %pad_maximum_fusion.2.refs_1_), channel_id=1, source_target_pairs={{0,2},{1,5},{2,0},{3,7},{4,6},{5,1},{6,4},{7,3},{8,10},{9,13},{10,... | collective-permute-start | bytes 1572872 | tf_op jit(solution)/shard_map/ppermute | solution.py:31
  39.4 1.3 %collective-permute-start = (bf16[64,1024]{1,0:T(8,128)(2,1)S(1)}, bf16[64,1024]{1,0:T(8,128)(2,1)S(1)}, u32[]{:S(2)}, u32[]{:S(2)}) collective-permute-start(bf16[64,1024]{1,0:T(8,128)(2,1)S(1)} %bitcast.33), channel_id=1, source_target_pairs={{0,16},{1,17},{2,18},{3,19},{4,20},{5,21},{6,22},{7,23},{8,24},{9,... | collective-permute-start | bytes 393224 | tf_op jit(solution)/shard_map/ppermute | solution.py:26
  41.4 2.1 %shard_map.114.refs_1_.refs_3_ = bf16[2816,1024]{1,0:T(8,128)(2,1)S(1)} custom-call(bf16[1024,768]{1,0:T(8,128)(2,1)S(1)} %constant_dynamic-update-slice_fusion.refs_0_, bf16[384,1024]{1,0:T(8,128)(2,1)} %bitcast.12.refs_1_, bf16[1024,768]{1,0:T(8,128)(2,1)} %collective-permute-done.4.refs_2_, bf16[384,1024]{1,0:T(8,128)(2,1)} %collective-permute-done.5.refs_3_), custom_call_target="tpu_custom_call" | custom-call | flops 1 | bytes 1 | tf_op jit(solution)/shard_map/pallas_call | solution.py:175
  43.5 3.7 %shard_map.115 = (bf16[128,1024]{1,0:T(8,128)(2,1)S(1)}, bf16[128,1024]{1,0:T(8,128)(2,1)S(1)}) custom-call(s32[1]{0:T(128)} %bitcast.1.me_ref, bf16[256,1152]{1,0:T(8,128)(2,1)} %collective-permute-done.3.refs_0_.refs_2_, bf16[2816,1024]{1,0:T(8,128)(2,1)S(1)} %shard_map.114.refs_1_.refs_3_), custom_call_target="tpu_custom_call" | custom-call | flops 1207959552 | bytes 589824 | tf_op jit(solution)/shard_map/pallas_call | solution.py:266
  47.2 1.4 %collective-permute-start.6 = (bf16[128,1024]{1,0:T(8,128)(2,1)S(1)}, bf16[128,1024]{1,0:T(8,128)(2,1)S(1)}, u32[]{:S(2)}, u32[]{:S(2)}) collective-permute-start(bf16[128,1024]{1,0:T(8,128)(2,1)S(1)} %get-tuple-element.25), channel_id=1, source_target_pairs={{0,2},{1,5},{2,0},{3,7},{4,6},{5,1},{6,4},{7,3},{8,10},{9,13},{10,... | collective-permute-start | bytes 786440 | tf_op jit(solution)/shard_map/ppermute | solution.py:31
  48.6 2.6 %shard_map.116 = f32[256,1024]{1,0:T(8,128)S(1)} custom-call(s32[1]{0:T(128)} %bitcast.1.me_ref, bf16[256,1152]{1,0:T(8,128)(2,1)S(1)} %pad_maximum_fusion.refs_0_.refs_2_, bf16[2816,1024]{1,0:T(8,128)(2,1)S(1)} %shard_map.114.refs_1_.refs_3_), custom_call_target="tpu_custom_call" | custom-call | flops 1207959552 | bytes 589824 | tf_op jit(solution)/shard_map/pallas_call | solution.py:266
  51.3 0.8 collective-permute-start.8
  52.0 4.4 %shard_map.117 = (bf16[128,1024]{1,0:T(8,128)(2,1)S(1)}, bf16[128,1024]{1,0:T(8,128)(2,1)S(1)}) custom-call(s32[1]{0:T(128)} %bitcast.1.me_ref, bf16[256,1024]{1,0:T(8,128)(2,1)} %collective-permute-done.14.refs_0_, bf16[256,1024]{1,0:T(8,128)(2,1)} %collective-permute-done.17.refs_1_, bf16[256,1152]{1,0:T(8,128)(2,1)} %collective-permute-done.3.refs_0_.refs_2_, ...), custom_call_target="tpu_custom_call" | custom-call | flops 2013265920 | bytes 1638400 | tf_op jit(solution)/shard_map/pallas_call | solution.py:266
  56.5 1.4 %collective-permute-start.18 = (bf16[128,1024]{1,0:T(8,128)(2,1)S(1)}, bf16[128,1024]{1,0:T(8,128)(2,1)S(1)}, u32[]{:S(2)}, u32[]{:S(2)}) collective-permute-start(bf16[128,1024]{1,0:T(8,128)(2,1)S(1)} %get-tuple-element.32), channel_id=1, source_target_pairs={{0,2},{1,5},{2,0},{3,7},{4,6},{5,1},{6,4},{7,3},{8,10},{9,13},{10,... | collective-permute-start | bytes 786440 | tf_op jit(solution)/shard_map/ppermute | solution.py:31
  57.9 1.0 %collective-permute-start.7 = (bf16[128,1024]{1,0:T(8,128)(2,1)S(1)}, bf16[128,1024]{1,0:T(8,128)(2,1)S(1)}, u32[]{:S(2)}, u32[]{:S(2)}) collective-permute-start(bf16[128,1024]{1,0:T(8,128)(2,1)S(1)} %add_convert_fusion.3), channel_id=1, source_target_pairs={{0,4},{1,3},{2,6},{3,1},{4,0},{5,7},{6,2},{7,5},{8,12},{9,11},{10,... | collective-permute-start | bytes 786440 | tf_op jit(solution)/shard_map/ppermute | solution.py:31
  59.0 4.5 %shard_map.118 = f32[256,1024]{1,0:T(8,128)S(1)} custom-call(s32[1]{0:T(128)} %bitcast.1.me_ref, bf16[256,1024]{1,0:T(8,128)(2,1)S(1)} %pad_maximum_fusion.1.refs_0_, bf16[256,1024]{1,0:T(8,128)(2,1)S(1)} %pad_maximum_fusion.2.refs_1_, bf16[256,1152]{1,0:T(8,128)(2,1)S(1)} %pad_maximum_fusion.refs_0_.refs_2_, bf16[2816,1024]{1,0:T(8,128)(2,1)S(1)} %shard_map.114.refs_1_.refs_3_), custom_call_target="tpu_custom_call" | custom-call | flops 2013265920 | bytes 1638400 | tf_op jit(solution)/shard_map/pallas_call | solution.py:266
  63.5 1.1 %collective-permute-done.18 = bf16[128,1024]{1,0:T(8,128)(2,1)S(1)} collective-permute-done((bf16[128,1024]{1,0:T(8,128)(2,1)S(1)}, bf16[128,1024]{1,0:T(8,128)(2,1)S(1)}, u32[]{:S(2)}, u32[]{:S(2)}) %collective-permute-start.18) | collective-permute-done | bytes 262176 | tf_op jit(solution)/shard_map/ppermute | solution.py:31
  64.6 1.2 %collective-permute-start.20 = (bf16[128,1024]{1,0:T(8,128)(2,1)S(1)}, bf16[128,1024]{1,0:T(8,128)(2,1)S(1)}, u32[]{:S(2)}, u32[]{:S(2)}) collective-permute-start(bf16[128,1024]{1,0:T(8,128)(2,1)S(1)} %get-tuple-element.33), channel_id=1, source_target_pairs={{0,2},{1,5},{2,0},{3,7},{4,6},{5,1},{6,4},{7,3},{8,10},{9,13},{10,... | collective-permute-start | bytes 786440 | tf_op jit(solution)/shard_map/ppermute | solution.py:31
  65.9 1.7 %collective-permute-start.19 = (bf16[128,1024]{1,0:T(8,128)(2,1)S(1)}, bf16[128,1024]{1,0:T(8,128)(2,1)S(1)}, u32[]{:S(2)}, u32[]{:S(2)}) collective-permute-start(bf16[128,1024]{1,0:T(8,128)(2,1)S(1)} %add_convert_fusion.1), channel_id=1, source_target_pairs={{0,4},{1,3},{2,6},{3,1},{4,0},{5,7},{6,2},{7,5},{8,12},{9,11},{10,... | collective-permute-start | bytes 786440 | tf_op jit(solution)/shard_map/ppermute | solution.py:31
  67.8 3.4 %collective-permute-start.10 = (bf16[64,1024]{1,0:T(8,128)(2,1)S(1)}, bf16[64,1024]{1,0:T(8,128)(2,1)S(1)}, u32[]{:S(2)}, u32[]{:S(2)}) collective-permute-start(bf16[64,1024]{1,0:T(8,128)(2,1)S(1)} %get-tuple-element.37), channel_id=1, source_target_pairs={{0,24},{1,25},{2,26},{3,27},{4,28},{5,29},{6,30},{7,31},{8,16},{9,... | collective-permute-start | bytes 393224 | tf_op jit(solution)/shard_map/ppermute | solution.py:26
  71.7 1.5 %collective-permute-start.9 = (bf16[64,1024]{1,0:T(8,128)(2,1)S(1)}, bf16[64,1024]{1,0:T(8,128)(2,1)S(1)}, u32[]{:S(2)}, u32[]{:S(2)}) collective-permute-start(bf16[64,1024]{1,0:T(8,128)(2,1)S(1)} %get-tuple-element.36), channel_id=1, source_target_pairs={{0,16},{1,17},{2,18},{3,19},{4,20},{5,21},{6,22},{7,23},{8,24},{9,... | collective-permute-start | bytes 393224 | tf_op jit(solution)/shard_map/ppermute | solution.py:26
  73.3 3.7 %collective-permute-start.22 = (bf16[64,1024]{1,0:T(8,128)(2,1)S(1)}, bf16[64,1024]{1,0:T(8,128)(2,1)S(1)}, u32[]{:S(2)}, u32[]{:S(2)}) collective-permute-start(bf16[64,1024]{1,0:T(8,128)(2,1)S(1)} %get-tuple-element.35), channel_id=1, source_target_pairs={{0,24},{1,25},{2,26},{3,27},{4,28},{5,29},{6,30},{7,31},{8,16},{9,... | collective-permute-start | bytes 393224 | tf_op jit(solution)/shard_map/ppermute | solution.py:26
  77.0 0.9 %collective-permute-start.21 = (bf16[64,1024]{1,0:T(8,128)(2,1)S(1)}, bf16[64,1024]{1,0:T(8,128)(2,1)S(1)}, u32[]{:S(2)}, u32[]{:S(2)}) collective-permute-start(bf16[64,1024]{1,0:T(8,128)(2,1)S(1)} %get-tuple-element.34), channel_id=1, source_target_pairs={{0,16},{1,17},{2,18},{3,19},{4,20},{5,21},{6,22},{7,23},{8,24},{9,... | collective-permute-start | bytes 393224 | tf_op jit(solution)/shard_map/ppermute | solution.py:26
  77.9 0.7 fusion
  78.6 4.1 %collective-permute-done.22 = bf16[64,1024]{1,0:T(8,128)(2,1)S(1)} collective-permute-done((bf16[64,1024]{1,0:T(8,128)(2,1)S(1)}, bf16[64,1024]{1,0:T(8,128)(2,1)S(1)}, u32[]{:S(2)}, u32[]{:S(2)}) %collective-permute-start.22) | collective-permute-done | bytes 131104 | tf_op jit(solution)/shard_map/ppermute | solution.py:26
  (46 shorter events, 3.8 us)
Async XLA Ops:
  0.6 3.1 %copy-start.1 = (bf16[1,1,1024,384]{3,2,1,0:T(8,128)(2,1)S(1)}, bf16[1,1,1024,384]{3,2,1,0:T(8,128)(2,1)}, u32[]{:S(2)}) copy-start(bf16[1,1,1024,384]{3,2,1,0:T(8,128)(2,1)} %param.18) | copy-start | bytes 2359300
  2.4 2.0 %copy-start = (bf16[64,1152]{1,0:T(8,128)(2,1)S(1)}, bf16[64,1152]{1,0:T(8,128)(2,1)}, u32[]{:S(2)}) copy-start(bf16[64,1152]{1,0:T(8,128)(2,1)} %shard_map.113) | copy-start | bytes 442372
  2.4 5.6 %copy-start.2 = (bf16[1,64,1024]{2,1,0:T(8,128)(2,1)S(1)}, bf16[1,64,1024]{2,1,0:T(8,128)(2,1)}, u32[]{:S(2)}) copy-start(bf16[1,64,1024]{2,1,0:T(8,128)(2,1)} %param.13) | copy-start | bytes 393220
  2.4 16.9 %copy-start.3 = (bf16[1,64,1024]{2,1,0:T(8,128)(2,1)S(1)}, bf16[1,64,1024]{2,1,0:T(8,128)(2,1)}, u32[]{:S(2)}) copy-start(bf16[1,64,1024]{2,1,0:T(8,128)(2,1)} %param.16) | copy-start | bytes 393220
  3.9 36.9 %collective-permute-start.4 = (bf16[1024,768]{1,0:T(8,128)(2,1)S(1)}, bf16[1024,768]{1,0:T(8,128)(2,1)}, u32[]{:S(2)}, u32[]{:S(2)}) collective-permute-start(bf16[1024,768]{1,0:T(8,128)(2,1)S(1)} %constant_dynamic-update-slice_fusion.refs_0_), channel_id=1, source_target_pairs={{0,1},{1,0},{2,3},{3,2},{4,5},{5,4},{6,7},{7,6},{8,9},{9,8},{10,11... | collective-permute-start | bytes 4718600 | tf_op jit(solution)/shard_map/ppermute | solution.py:31
  4.4 14.3 %collective-permute-start.1 = (bf16[64,1152]{1,0:T(8,128)(2,1)S(1)}, bf16[64,1152]{1,0:T(8,128)(2,1)S(1)}, u32[]{:S(2)}, u32[]{:S(2)}) collective-permute-start(bf16[64,1152]{1,0:T(8,128)(2,1)S(1)} %copy-done), channel_id=1, source_target_pairs={{0,8},{1,9},{2,10},{3,11},{4,12},{5,13},{6,14},{7,15},{8,0},{9,1},... | collective-permute-start | bytes 442376 | tf_op jit(solution)/shard_map/ppermute | solution.py:31
  8.1 14.7 %collective-permute-start.12 = (bf16[64,1024]{1,0:T(8,128)(2,1)S(1)}, bf16[64,1024]{1,0:T(8,128)(2,1)S(1)}, u32[]{:S(2)}, u32[]{:S(2)}) collective-permute-start(bf16[64,1024]{1,0:T(8,128)(2,1)S(1)} %bitcast.25), channel_id=1, source_target_pairs={{0,8},{1,9},{2,10},{3,11},{4,12},{5,13},{6,14},{7,15},{8,0},{9,1},... | collective-permute-start | bytes 393224 | tf_op jit(solution)/shard_map/ppermute | solution.py:31
  18.8 11.6 %collective-permute-start.2 = (bf16[128,1152]{1,0:T(8,128)(2,1)S(1)}, bf16[128,1152]{1,0:T(8,128)(2,1)S(1)}, u32[]{:S(2)}, u32[]{:S(2)}) collective-permute-start(bf16[128,1152]{1,0:T(8,128)(2,1)S(1)} %pad_maximum_fusion.3), channel_id=1, source_target_pairs={{0,4},{1,3},{2,6},{3,1},{4,0},{5,7},{6,2},{7,5},{8,12},{9,11},{10,... | collective-permute-start | bytes 884744 | tf_op jit(solution)/shard_map/ppermute | solution.py:31
  19.3 7.9 %collective-permute-start.15 = (bf16[64,1024]{1,0:T(8,128)(2,1)S(1)}, bf16[64,1024]{1,0:T(8,128)(2,1)S(1)}, u32[]{:S(2)}, u32[]{:S(2)}) collective-permute-start(bf16[64,1024]{1,0:T(8,128)(2,1)S(1)} %bitcast.28), channel_id=1, source_target_pairs={{0,8},{1,9},{2,10},{3,11},{4,12},{5,13},{6,14},{7,15},{8,0},{9,1},... | collective-permute-start | bytes 393224 | tf_op jit(solution)/shard_map/ppermute | solution.py:31
  22.7 16.7 %collective-permute-start.5 = (bf16[384,1024]{1,0:T(8,128)(2,1)}, bf16[384,1024]{1,0:T(8,128)(2,1)}, u32[]{:S(2)}, u32[]{:S(2)}) collective-permute-start(bf16[384,1024]{1,0:T(8,128)(2,1)} %bitcast.12.refs_1_), channel_id=1, source_target_pairs={{0,1},{1,0},{2,3},{3,2},{4,5},{5,4},{6,7},{7,6},{8,9},{9,8},{10,11... | collective-permute-start | bytes 2359304 | tf_op jit(solution)/shard_map/ppermute | solution.py:31
  22.7 10.1 %collective-permute-start.13 = (bf16[128,1024]{1,0:T(8,128)(2,1)S(1)}, bf16[128,1024]{1,0:T(8,128)(2,1)S(1)}, u32[]{:S(2)}, u32[]{:S(2)}) collective-permute-start(bf16[128,1024]{1,0:T(8,128)(2,1)S(1)} %pad_maximum_fusion.4), channel_id=1, source_target_pairs={{0,4},{1,3},{2,6},{3,1},{4,0},{5,7},{6,2},{7,5},{8,12},{9,11},{10,... | collective-permute-start | bytes 786440 | tf_op jit(solution)/shard_map/ppermute | solution.py:31
  27.3 12.1 %copy-start.4 = (bf16[1,64,1024]{2,1,0:T(8,128)(2,1)S(1)}, bf16[1,64,1024]{2,1,0:T(8,128)(2,1)}, u32[]{:S(2)}) copy-start(bf16[1,64,1024]{2,1,0:T(8,128)(2,1)} %param.10) | copy-start | bytes 393220
  27.3 11.2 %collective-permute-start.16 = (bf16[128,1024]{1,0:T(8,128)(2,1)S(1)}, bf16[128,1024]{1,0:T(8,128)(2,1)S(1)}, u32[]{:S(2)}, u32[]{:S(2)}) collective-permute-start(bf16[128,1024]{1,0:T(8,128)(2,1)S(1)} %pad_maximum_fusion.5), channel_id=1, source_target_pairs={{0,4},{1,3},{2,6},{3,1},{4,0},{5,7},{6,2},{7,5},{8,12},{9,11},{10,... | collective-permute-start | bytes 786440 | tf_op jit(solution)/shard_map/ppermute | solution.py:31
  30.4 13.2 %collective-permute-start.3 = (bf16[256,1152]{1,0:T(8,128)(2,1)S(1)}, bf16[256,1152]{1,0:T(8,128)(2,1)}, u32[]{:S(2)}, u32[]{:S(2)}) collective-permute-start(bf16[256,1152]{1,0:T(8,128)(2,1)S(1)} %pad_maximum_fusion.refs_0_.refs_2_), channel_id=1, source_target_pairs={{0,2},{1,5},{2,0},{3,7},{4,6},{5,1},{6,4},{7,3},{8,10},{9,13},{10,... | collective-permute-start | bytes 1769480 | tf_op jit(solution)/shard_map/ppermute | solution.py:31
  32.9 18.3 %collective-permute-start.14 = (bf16[256,1024]{1,0:T(8,128)(2,1)S(1)}, bf16[256,1024]{1,0:T(8,128)(2,1)}, u32[]{:S(2)}, u32[]{:S(2)}) collective-permute-start(bf16[256,1024]{1,0:T(8,128)(2,1)S(1)} %pad_maximum_fusion.1.refs_0_), channel_id=1, source_target_pairs={{0,2},{1,5},{2,0},{3,7},{4,6},{5,1},{6,4},{7,3},{8,10},{9,13},{10,... | collective-permute-start | bytes 1572872 | tf_op jit(solution)/shard_map/ppermute | solution.py:31
  38.5 13.5 %collective-permute-start.17 = (bf16[256,1024]{1,0:T(8,128)(2,1)S(1)}, bf16[256,1024]{1,0:T(8,128)(2,1)}, u32[]{:S(2)}, u32[]{:S(2)}) collective-permute-start(bf16[256,1024]{1,0:T(8,128)(2,1)S(1)} %pad_maximum_fusion.2.refs_1_), channel_id=1, source_target_pairs={{0,2},{1,5},{2,0},{3,7},{4,6},{5,1},{6,4},{7,3},{8,10},{9,13},{10,... | collective-permute-start | bytes 1572872 | tf_op jit(solution)/shard_map/ppermute | solution.py:31
  39.4 37.6 %collective-permute-start = (bf16[64,1024]{1,0:T(8,128)(2,1)S(1)}, bf16[64,1024]{1,0:T(8,128)(2,1)S(1)}, u32[]{:S(2)}, u32[]{:S(2)}) collective-permute-start(bf16[64,1024]{1,0:T(8,128)(2,1)S(1)} %bitcast.33), channel_id=1, source_target_pairs={{0,16},{1,17},{2,18},{3,19},{4,20},{5,21},{6,22},{7,23},{8,24},{9,... | collective-permute-start | bytes 393224 | tf_op jit(solution)/shard_map/ppermute | solution.py:26
  40.7 37.9 %collective-permute-start.11 = (bf16[64,1024]{1,0:T(8,128)(2,1)S(1)}, bf16[64,1024]{1,0:T(8,128)(2,1)S(1)}, u32[]{:S(2)}, u32[]{:S(2)}) collective-permute-start(bf16[64,1024]{1,0:T(8,128)(2,1)S(1)} %bitcast.31), channel_id=1, source_target_pairs={{0,16},{1,17},{2,18},{3,19},{4,20},{5,21},{6,22},{7,23},{8,24},{9,... | collective-permute-start | bytes 393224 | tf_op jit(solution)/shard_map/ppermute | solution.py:26
  47.2 10.6 %collective-permute-start.6 = (bf16[128,1024]{1,0:T(8,128)(2,1)S(1)}, bf16[128,1024]{1,0:T(8,128)(2,1)S(1)}, u32[]{:S(2)}, u32[]{:S(2)}) collective-permute-start(bf16[128,1024]{1,0:T(8,128)(2,1)S(1)} %get-tuple-element.25), channel_id=1, source_target_pairs={{0,2},{1,5},{2,0},{3,7},{4,6},{5,1},{6,4},{7,3},{8,10},{9,13},{10,... | collective-permute-start | bytes 786440 | tf_op jit(solution)/shard_map/ppermute | solution.py:31
  51.3 14.7 %collective-permute-start.8 = (bf16[128,1024]{1,0:T(8,128)(2,1)S(1)}, bf16[128,1024]{1,0:T(8,128)(2,1)S(1)}, u32[]{:S(2)}, u32[]{:S(2)}) collective-permute-start(bf16[128,1024]{1,0:T(8,128)(2,1)S(1)} %get-tuple-element.26), channel_id=1, source_target_pairs={{0,2},{1,5},{2,0},{3,7},{4,6},{5,1},{6,4},{7,3},{8,10},{9,13},{10,... | collective-permute-start | bytes 786440 | tf_op jit(solution)/shard_map/ppermute | solution.py:31
  56.5 8.1 %collective-permute-start.18 = (bf16[128,1024]{1,0:T(8,128)(2,1)S(1)}, bf16[128,1024]{1,0:T(8,128)(2,1)S(1)}, u32[]{:S(2)}, u32[]{:S(2)}) collective-permute-start(bf16[128,1024]{1,0:T(8,128)(2,1)S(1)} %get-tuple-element.32), channel_id=1, source_target_pairs={{0,2},{1,5},{2,0},{3,7},{4,6},{5,1},{6,4},{7,3},{8,10},{9,13},{10,... | collective-permute-start | bytes 786440 | tf_op jit(solution)/shard_map/ppermute | solution.py:31
  57.9 9.7 %collective-permute-start.7 = (bf16[128,1024]{1,0:T(8,128)(2,1)S(1)}, bf16[128,1024]{1,0:T(8,128)(2,1)S(1)}, u32[]{:S(2)}, u32[]{:S(2)}) collective-permute-start(bf16[128,1024]{1,0:T(8,128)(2,1)S(1)} %add_convert_fusion.3), channel_id=1, source_target_pairs={{0,4},{1,3},{2,6},{3,1},{4,0},{5,7},{6,2},{7,5},{8,12},{9,11},{10,... | collective-permute-start | bytes 786440 | tf_op jit(solution)/shard_map/ppermute | solution.py:31
  64.6 7.0 %collective-permute-start.20 = (bf16[128,1024]{1,0:T(8,128)(2,1)S(1)}, bf16[128,1024]{1,0:T(8,128)(2,1)S(1)}, u32[]{:S(2)}, u32[]{:S(2)}) collective-permute-start(bf16[128,1024]{1,0:T(8,128)(2,1)S(1)} %get-tuple-element.33), channel_id=1, source_target_pairs={{0,2},{1,5},{2,0},{3,7},{4,6},{5,1},{6,4},{7,3},{8,10},{9,13},{10,... | collective-permute-start | bytes 786440 | tf_op jit(solution)/shard_map/ppermute | solution.py:31
  65.9 7.2 %collective-permute-start.19 = (bf16[128,1024]{1,0:T(8,128)(2,1)S(1)}, bf16[128,1024]{1,0:T(8,128)(2,1)S(1)}, u32[]{:S(2)}, u32[]{:S(2)}) collective-permute-start(bf16[128,1024]{1,0:T(8,128)(2,1)S(1)} %add_convert_fusion.1), channel_id=1, source_target_pairs={{0,4},{1,3},{2,6},{3,1},{4,0},{5,7},{6,2},{7,5},{8,12},{9,11},{10,... | collective-permute-start | bytes 786440 | tf_op jit(solution)/shard_map/ppermute | solution.py:31
  67.8 10.2 %collective-permute-start.10 = (bf16[64,1024]{1,0:T(8,128)(2,1)S(1)}, bf16[64,1024]{1,0:T(8,128)(2,1)S(1)}, u32[]{:S(2)}, u32[]{:S(2)}) collective-permute-start(bf16[64,1024]{1,0:T(8,128)(2,1)S(1)} %get-tuple-element.37), channel_id=1, source_target_pairs={{0,24},{1,25},{2,26},{3,27},{4,28},{5,29},{6,30},{7,31},{8,16},{9,... | collective-permute-start | bytes 393224 | tf_op jit(solution)/shard_map/ppermute | solution.py:26
  71.7 6.3 %collective-permute-start.9 = (bf16[64,1024]{1,0:T(8,128)(2,1)S(1)}, bf16[64,1024]{1,0:T(8,128)(2,1)S(1)}, u32[]{:S(2)}, u32[]{:S(2)}) collective-permute-start(bf16[64,1024]{1,0:T(8,128)(2,1)S(1)} %get-tuple-element.36), channel_id=1, source_target_pairs={{0,16},{1,17},{2,18},{3,19},{4,20},{5,21},{6,22},{7,23},{8,24},{9,... | collective-permute-start | bytes 393224 | tf_op jit(solution)/shard_map/ppermute | solution.py:26
  73.3 9.4 %collective-permute-start.22 = (bf16[64,1024]{1,0:T(8,128)(2,1)S(1)}, bf16[64,1024]{1,0:T(8,128)(2,1)S(1)}, u32[]{:S(2)}, u32[]{:S(2)}) collective-permute-start(bf16[64,1024]{1,0:T(8,128)(2,1)S(1)} %get-tuple-element.35), channel_id=1, source_target_pairs={{0,24},{1,25},{2,26},{3,27},{4,28},{5,29},{6,30},{7,31},{8,16},{9,... | collective-permute-start | bytes 393224 | tf_op jit(solution)/shard_map/ppermute | solution.py:26
  77.0 5.7 %collective-permute-start.21 = (bf16[64,1024]{1,0:T(8,128)(2,1)S(1)}, bf16[64,1024]{1,0:T(8,128)(2,1)S(1)}, u32[]{:S(2)}, u32[]{:S(2)}) collective-permute-start(bf16[64,1024]{1,0:T(8,128)(2,1)S(1)} %get-tuple-element.34), channel_id=1, source_target_pairs={{0,16},{1,17},{2,18},{3,19},{4,20},{5,21},{6,22},{7,23},{8,24},{9,... | collective-permute-start | bytes 393224 | tf_op jit(solution)/shard_map/ppermute | solution.py:26

commit v5 on v4

--- a/solution.py
+++ b/solution.py
@@ -139,7 +139,7 @@
 
 
 def forward_rows(x, gate_up, down):
-    pre = times(x, gate_up[...])
+    pre = times(x(), gate_up[...])
     width = pre.shape[1] // 2
     gate, up = pre[:, :width], pre[:, width:]
     hidden = (gate * jax.nn.sigmoid(gate) * up).astype(BF16)
@@ -147,11 +147,11 @@
 
 
 def backward_rows(x, cot, gate_up, down):
-    pre = times(x, gate_up[...])
+    pre = times(x(), gate_up[...])
     width = pre.shape[1] // 2
     gate, up = pre[:, :width], pre[:, width:]
     sig = jax.nn.sigmoid(gate)
-    d_hidden = times_transposed(cot, down[...])
+    d_hidden = times_transposed(cot(), down[...])
     d_gate = d_hidden * up * sig * (1.0 + gate * (1.0 - sig))
     d_up = d_hidden * gate * sig
     both = jnp.concatenate([d_gate.astype(BF16), d_up.astype(BF16)], axis=1)
@@ -213,6 +213,9 @@
         started[number] = []
         return buffers[number]
 
+    def taken_rows(number, tile):
+        return ready(number)[tile, :]
+
     inputs = len(copies) - 1
     for number in range(len(copies)):
         start_copies(number)
@@ -222,7 +225,7 @@
     for flip in range(2):
         for start in range(0, total_rows, step * rows):
             tile = pl.ds(start, min(step * rows, total_rows - start))
-            taken = [ready(number)[tile, :] for number in range(inputs)]
+            taken = [functools.partial(taken_rows, number, tile) for number in range(inputs)]
             gate_up, down = weights[2 * flip : 2 * flip + 2]
             out = each(*taken, gate_up, down).astype(BF16).astype(F32)
             out = out * gate_of(ready(len(copies) - 1)[tile, :], topk, first, me_ref[0] ^ flip)

time: 83.9 us -> 84.3 us (level)
  transfers between devices with their start and end apart: 23 -> 23, of which waited for: 7 -> 10; matrix products, arithmetic and copies ran while one was open for 1% -> 1% of each run, Pallas kernels for 21% -> 21%
where the time goes in v5:
time: 84.3 us; the launch traced here: 84 us
  starting transfers between devices  34.1 us (40%)
  waiting for transfers between devices  26.2 us (31%)
  Pallas kernels  19.5 us (23%)
  other arithmetic  1.91 us (2%)
  local copies, waits for them, and re-layouts  1.48 us (2%)
    ppermute x17, starting transfers between devices, swapped(): return lax.ppermute(block, 'expert', route)  22.7 us
    ppermute x17, waiting for transfers between devices, swapped(): return lax.ppermute(block, 'expert', route)  21.8 us
    pallas_call x4, Pallas kernels, weighted(): pl.pallas_call(functools.partial(expert_kernel, each, topk, first, rows,...  15.7 us
    ppermute x6, starting transfers between devices, passed_along(): return lax.ppermute(block, ('section', 'expert'), route)  11.4 us
    ppermute x6, waiting for transfers between devices, passed_along(): return lax.ppermute(block, ('section', 'expert'), route)  4.41 us
    pallas_call x1, Pallas kernels, loaded(): pl.pallas_call(functools.partial(loading_kernel, places), out_shape=jax.S...  2.1 us
    pallas_call x1, Pallas kernels, packed(): pl.pallas_call(packing_kernel, out_shape=jax.ShapeDtypeStruct((length, wi...  1.77 us
  transfers between devices with their start and end apart: 23, of which 10 were waited for; matrix products, arithmetic and copies ran while one was open for 1% of the time, Pallas kernels for 21%

profile of v5, /device:TPU:0, one launch (start us, length us, event | category | flops | bytes accessed | tf_op | source)
XLA Modules:
  0.0 84.0 jit_solution(7785987172365371772)
XLA Ops:
  0.6 1.8 %shard_map.113 = bf16[64,1152]{1,0:T(8,128)(2,1)} custom-call(bf16[64,1024]{1,0:T(8,128)(2,1)} %bitcast.32, s32[8,64]{1,0:T(8,128)} %bitcast.34, f32[8,64]{1,0:T(8,128)} %bitcast.35, s32[8,64]{1,0:T(8,128)} %bitcast.36, f32[8,64]{1,0:T(8,128)} %bitcast.37), custom_call_target="tpu_custom_call" | custom-call | flops 1 | bytes 1 | tf_op jit(solution)/shard_map/pallas_call | solution.py:118
  2.4 1.3 %constant_dynamic-update-slice_fusion.1 = bf16[1024,768]{1,0:T(8,128)(2,1)S(1)} fusion(bf16[1024,384]{1,0:T(8,128)(2,1)} %bitcast.23), kind=kLoop, calls=%fused_computation.15 | loop fusion | bytes 1572864
  4.4 3.7 %collective-permute-start.1 = (bf16[64,1152]{1,0:T(8,128)(2,1)S(1)}, bf16[64,1152]{1,0:T(8,128)(2,1)S(1)}, u32[]{:S(2)}, u32[]{:S(2)}) collective-permute-start(bf16[64,1152]{1,0:T(8,128)(2,1)S(1)} %copy-done), channel_id=1, source_target_pairs={{0,8},{1,9},{2,10},{3,11},{4,12},{5,13},{6,14},{7,15},{8,0},{9,1},... | collective-permute-start | bytes 442376 | tf_op jit(solution)/shard_map/ppermute | solution.py:31
  8.1 10.6 %collective-permute-done.1 = bf16[64,1152]{1,0:T(8,128)(2,1)S(1)} collective-permute-done((bf16[64,1152]{1,0:T(8,128)(2,1)S(1)}, bf16[64,1152]{1,0:T(8,128)(2,1)S(1)}, u32[]{:S(2)}, u32[]{:S(2)}) %collective-permute-start.1) | collective-permute-done | bytes 147488 | tf_op jit(solution)/shard_map/ppermute | solution.py:31
  19.3 3.4 %collective-permute-start.15 = (bf16[64,1024]{1,0:T(8,128)(2,1)S(1)}, bf16[64,1024]{1,0:T(8,128)(2,1)S(1)}, u32[]{:S(2)}, u32[]{:S(2)}) collective-permute-start(bf16[64,1024]{1,0:T(8,128)(2,1)S(1)} %bitcast.28), channel_id=1, source_target_pairs={{0,8},{1,9},{2,10},{3,11},{4,12},{5,13},{6,14},{7,15},{8,0},{9,1},... | collective-permute-start | bytes 393224 | tf_op jit(solution)/shard_map/ppermute | solution.py:31
  22.7 1.0 %collective-permute-start.13 = (bf16[128,1024]{1,0:T(8,128)(2,1)S(1)}, bf16[128,1024]{1,0:T(8,128)(2,1)S(1)}, u32[]{:S(2)}, u32[]{:S(2)}) collective-permute-start(bf16[128,1024]{1,0:T(8,128)(2,1)S(1)} %pad_maximum_fusion.4), channel_id=1, source_target_pairs={{0,4},{1,3},{2,6},{3,1},{4,0},{5,7},{6,2},{7,5},{8,12},{9,11},{10,... | collective-permute-start | bytes 786440 | tf_op jit(solution)/shard_map/ppermute | solution.py:31
  23.8 3.5 %collective-permute-done.15 = bf16[64,1024]{1,0:T(8,128)(2,1)S(1)} collective-permute-done((bf16[64,1024]{1,0:T(8,128)(2,1)S(1)}, bf16[64,1024]{1,0:T(8,128)(2,1)S(1)}, u32[]{:S(2)}, u32[]{:S(2)}) %collective-permute-start.15) | collective-permute-done | bytes 131104 | tf_op jit(solution)/shard_map/ppermute | solution.py:31
  27.3 3.0 %collective-permute-start.16 = (bf16[128,1024]{1,0:T(8,128)(2,1)S(1)}, bf16[128,1024]{1,0:T(8,128)(2,1)S(1)}, u32[]{:S(2)}, u32[]{:S(2)}) collective-permute-start(bf16[128,1024]{1,0:T(8,128)(2,1)S(1)} %pad_maximum_fusion.5), channel_id=1, source_target_pairs={{0,4},{1,3},{2,6},{3,1},{4,0},{5,7},{6,2},{7,5},{8,12},{9,11},{10,... | collective-permute-start | bytes 786440 | tf_op jit(solution)/shard_map/ppermute | solution.py:31
  30.4 1.1 %collective-permute-start.3 = (bf16[256,1152]{1,0:T(8,128)(2,1)S(1)}, bf16[256,1152]{1,0:T(8,128)(2,1)}, u32[]{:S(2)}, u32[]{:S(2)}) collective-permute-start(bf16[256,1152]{1,0:T(8,128)(2,1)S(1)} %pad_maximum_fusion.refs_0_.refs_2_), channel_id=1, source_target_pairs={{0,2},{1,5},{2,0},{3,7},{4,6},{5,1},{6,4},{7,3},{8,10},{9,13},{10,... | collective-permute-start | bytes 1769480 | tf_op jit(solution)/shard_map/ppermute | solution.py:31
  31.5 1.4 %collective-permute-done.13 = bf16[128,1024]{1,0:T(8,128)(2,1)S(1)} collective-permute-done((bf16[128,1024]{1,0:T(8,128)(2,1)S(1)}, bf16[128,1024]{1,0:T(8,128)(2,1)S(1)}, u32[]{:S(2)}, u32[]{:S(2)}) %collective-permute-start.13) | collective-permute-done | bytes 262176 | tf_op jit(solution)/shard_map/ppermute | solution.py:31
  32.9 0.9 %collective-permute-start.14 = (bf16[256,1024]{1,0:T(8,128)(2,1)S(1)}, bf16[256,1024]{1,0:T(8,128)(2,1)}, u32[]{:S(2)}, u32[]{:S(2)}) collective-permute-start(bf16[256,1024]{1,0:T(8,128)(2,1)S(1)} %pad_maximum_fusion.1.refs_0_), channel_id=1, source_target_pairs={{0,2},{1,5},{2,0},{3,7},{4,6},{5,1},{6,4},{7,3},{8,10},{9,13},{10,... | collective-permute-start | bytes 1572872 | tf_op jit(solution)/shard_map/ppermute | solution.py:31
  33.8 4.7 %collective-permute-done.16 = bf16[128,1024]{1,0:T(8,128)(2,1)S(1)} collective-permute-done((bf16[128,1024]{1,0:T(8,128)(2,1)S(1)}, bf16[128,1024]{1,0:T(8,128)(2,1)S(1)}, u32[]{:S(2)}, u32[]{:S(2)}) %collective-permute-start.16) | collective-permute-done | bytes 262176 | tf_op jit(solution)/shard_map/ppermute | solution.py:31
  38.5 0.9 %collective-permute-start.17 = (bf16[256,1024]{1,0:T(8,128)(2,1)S(1)}, bf16[256,1024]{1,0:T(8,128)(2,1)}, u32[]{:S(2)}, u32[]{:S(2)}) collective-permute-start(bf16[256,1024]{1,0:T(8,128)(2,1)S(1)} %pad_maximum_fusion.2.refs_1_), channel_id=1, source_target_pairs={{0,2},{1,5},{2,0},{3,7},{4,6},{5,1},{6,4},{7,3},{8,10},{9,13},{10,... | collective-permute-start | bytes 1572872 | tf_op jit(solution)/shard_map/ppermute | solution.py:31
  39.4 1.3 %collective-permute-start = (bf16[64,1024]{1,0:T(8,128)(2,1)S(1)}, bf16[64,1024]{1,0:T(8,128)(2,1)S(1)}, u32[]{:S(2)}, u32[]{:S(2)}) collective-permute-start(bf16[64,1024]{1,0:T(8,128)(2,1)S(1)} %bitcast.33), channel_id=1, source_target_pairs={{0,16},{1,17},{2,18},{3,19},{4,20},{5,21},{6,22},{7,23},{8,24},{9,... | collective-permute-start | bytes 393224 | tf_op jit(solution)/shard_map/ppermute | solution.py:26
  41.4 2.1 %shard_map.114.refs_1_.refs_3_ = bf16[2816,1024]{1,0:T(8,128)(2,1)S(1)} custom-call(bf16[1024,768]{1,0:T(8,128)(2,1)S(1)} %constant_dynamic-update-slice_fusion.refs_0_, bf16[384,1024]{1,0:T(8,128)(2,1)} %bitcast.12.refs_1_, bf16[1024,768]{1,0:T(8,128)(2,1)} %collective-permute-done.4.refs_2_, bf16[384,1024]{1,0:T(8,128)(2,1)} %collective-permute-done.5.refs_3_), custom_call_target="tpu_custom_call" | custom-call | flops 1 | bytes 1 | tf_op jit(solution)/shard_map/pallas_call | solution.py:175
  43.5 3.7 %shard_map.115 = (bf16[128,1024]{1,0:T(8,128)(2,1)S(1)}, bf16[128,1024]{1,0:T(8,128)(2,1)S(1)}) custom-call(s32[1]{0:T(128)} %bitcast.1.me_ref, bf16[256,1152]{1,0:T(8,128)(2,1)} %collective-permute-done.3.refs_0_.refs_2_, bf16[2816,1024]{1,0:T(8,128)(2,1)S(1)} %shard_map.114.refs_1_.refs_3_), custom_call_target="tpu_custom_call" | custom-call | flops 1207959552 | bytes 589824 | tf_op jit(solution)/shard_map/pallas_call | solution.py:269
  47.2 1.4 %collective-permute-start.6 = (bf16[128,1024]{1,0:T(8,128)(2,1)S(1)}, bf16[128,1024]{1,0:T(8,128)(2,1)S(1)}, u32[]{:S(2)}, u32[]{:S(2)}) collective-permute-start(bf16[128,1024]{1,0:T(8,128)(2,1)S(1)} %get-tuple-element.25), channel_id=1, source_target_pairs={{0,2},{1,5},{2,0},{3,7},{4,6},{5,1},{6,4},{7,3},{8,10},{9,13},{10,... | collective-permute-start | bytes 786440 | tf_op jit(solution)/shard_map/ppermute | solution.py:31
  48.6 2.6 %shard_map.116 = f32[256,1024]{1,0:T(8,128)S(1)} custom-call(s32[1]{0:T(128)} %bitcast.1.me_ref, bf16[256,1152]{1,0:T(8,128)(2,1)S(1)} %pad_maximum_fusion.refs_0_.refs_2_, bf16[2816,1024]{1,0:T(8,128)(2,1)S(1)} %shard_map.114.refs_1_.refs_3_), custom_call_target="tpu_custom_call" | custom-call | flops 1207959552 | bytes 589824 | tf_op jit(solution)/shard_map/pallas_call | solution.py:269
  51.3 0.8 collective-permute-start.8
  52.0 4.6 %shard_map.117 = (bf16[128,1024]{1,0:T(8,128)(2,1)S(1)}, bf16[128,1024]{1,0:T(8,128)(2,1)S(1)}) custom-call(s32[1]{0:T(128)} %bitcast.1.me_ref, bf16[256,1024]{1,0:T(8,128)(2,1)} %collective-permute-done.14.refs_0_, bf16[256,1024]{1,0:T(8,128)(2,1)} %collective-permute-done.17.refs_1_, bf16[256,1152]{1,0:T(8,128)(2,1)} %collective-permute-done.3.refs_0_.refs_2_, ...), custom_call_target="tpu_custom_call" | custom-call | flops 2013265920 | bytes 1638400 | tf_op jit(solution)/shard_map/pallas_call | solution.py:269
  56.6 1.4 %collective-permute-start.18 = (bf16[128,1024]{1,0:T(8,128)(2,1)S(1)}, bf16[128,1024]{1,0:T(8,128)(2,1)S(1)}, u32[]{:S(2)}, u32[]{:S(2)}) collective-permute-start(bf16[128,1024]{1,0:T(8,128)(2,1)S(1)} %get-tuple-element.32), channel_id=1, source_target_pairs={{0,2},{1,5},{2,0},{3,7},{4,6},{5,1},{6,4},{7,3},{8,10},{9,13},{10,... | collective-permute-start | bytes 786440 | tf_op jit(solution)/shard_map/ppermute | solution.py:31
  58.1 1.0 %collective-permute-start.7 = (bf16[128,1024]{1,0:T(8,128)(2,1)S(1)}, bf16[128,1024]{1,0:T(8,128)(2,1)S(1)}, u32[]{:S(2)}, u32[]{:S(2)}) collective-permute-start(bf16[128,1024]{1,0:T(8,128)(2,1)S(1)} %add_convert_fusion.3), channel_id=1, source_target_pairs={{0,4},{1,3},{2,6},{3,1},{4,0},{5,7},{6,2},{7,5},{8,12},{9,11},{10,... | collective-permute-start | bytes 786440 | tf_op jit(solution)/shard_map/ppermute | solution.py:31
  59.1 4.8 %shard_map.118 = f32[256,1024]{1,0:T(8,128)S(1)} custom-call(s32[1]{0:T(128)} %bitcast.1.me_ref, bf16[256,1024]{1,0:T(8,128)(2,1)S(1)} %pad_maximum_fusion.1.refs_0_, bf16[256,1024]{1,0:T(8,128)(2,1)S(1)} %pad_maximum_fusion.2.refs_1_, bf16[256,1152]{1,0:T(8,128)(2,1)S(1)} %pad_maximum_fusion.refs_0_.refs_2_, bf16[2816,1024]{1,0:T(8,128)(2,1)S(1)} %shard_map.114.refs_1_.refs_3_), custom_call_target="tpu_custom_call" | custom-call | flops 2013265920 | bytes 1638400 | tf_op jit(solution)/shard_map/pallas_call | solution.py:269
  63.9 0.8 collective-permute-done.18
  64.8 1.2 %collective-permute-start.20 = (bf16[128,1024]{1,0:T(8,128)(2,1)S(1)}, bf16[128,1024]{1,0:T(8,128)(2,1)S(1)}, u32[]{:S(2)}, u32[]{:S(2)}) collective-permute-start(bf16[128,1024]{1,0:T(8,128)(2,1)S(1)} %get-tuple-element.33), channel_id=1, source_target_pairs={{0,2},{1,5},{2,0},{3,7},{4,6},{5,1},{6,4},{7,3},{8,10},{9,13},{10,... | collective-permute-start | bytes 786440 | tf_op jit(solution)/shard_map/ppermute | solution.py:31
  66.1 1.7 %collective-permute-start.19 = (bf16[128,1024]{1,0:T(8,128)(2,1)S(1)}, bf16[128,1024]{1,0:T(8,128)(2,1)S(1)}, u32[]{:S(2)}, u32[]{:S(2)}) collective-permute-start(bf16[128,1024]{1,0:T(8,128)(2,1)S(1)} %add_convert_fusion.1), channel_id=1, source_target_pairs={{0,4},{1,3},{2,6},{3,1},{4,0},{5,7},{6,2},{7,5},{8,12},{9,11},{10,... | collective-permute-start | bytes 786440 | tf_op jit(solution)/shard_map/ppermute | solution.py:31
  67.9 3.4 %collective-permute-start.10 = (bf16[64,1024]{1,0:T(8,128)(2,1)S(1)}, bf16[64,1024]{1,0:T(8,128)(2,1)S(1)}, u32[]{:S(2)}, u32[]{:S(2)}) collective-permute-start(bf16[64,1024]{1,0:T(8,128)(2,1)S(1)} %get-tuple-element.37), channel_id=1, source_target_pairs={{0,24},{1,25},{2,26},{3,27},{4,28},{5,29},{6,30},{7,31},{8,16},{9,... | collective-permute-start | bytes 393224 | tf_op jit(solution)/shard_map/ppermute | solution.py:26
  71.3 0.7 collective-permute-done.20
  72.1 1.5 %collective-permute-start.9 = (bf16[64,1024]{1,0:T(8,128)(2,1)S(1)}, bf16[64,1024]{1,0:T(8,128)(2,1)S(1)}, u32[]{:S(2)}, u32[]{:S(2)}) collective-permute-start(bf16[64,1024]{1,0:T(8,128)(2,1)S(1)} %get-tuple-element.36), channel_id=1, source_target_pairs={{0,16},{1,17},{2,18},{3,19},{4,20},{5,21},{6,22},{7,23},{8,24},{9,... | collective-permute-start | bytes 393224 | tf_op jit(solution)/shard_map/ppermute | solution.py:26
  73.8 3.6 %collective-permute-start.22 = (bf16[64,1024]{1,0:T(8,128)(2,1)S(1)}, bf16[64,1024]{1,0:T(8,128)(2,1)S(1)}, u32[]{:S(2)}, u32[]{:S(2)}) collective-permute-start(bf16[64,1024]{1,0:T(8,128)(2,1)S(1)} %get-tuple-element.35), channel_id=1, source_target_pairs={{0,24},{1,25},{2,26},{3,27},{4,28},{5,29},{6,30},{7,31},{8,16},{9,... | collective-permute-start | bytes 393224 | tf_op jit(solution)/shard_map/ppermute | solution.py:26
  77.4 0.8 collective-permute-start.21
  79.2 3.9 %collective-permute-done.22 = bf16[64,1024]{1,0:T(8,128)(2,1)S(1)} collective-permute-done((bf16[64,1024]{1,0:T(8,128)(2,1)S(1)}, bf16[64,1024]{1,0:T(8,128)(2,1)S(1)}, u32[]{:S(2)}, u32[]{:S(2)}) %collective-permute-start.22) | collective-permute-done | bytes 131104 | tf_op jit(solution)/shard_map/ppermute | solution.py:26
  (46 shorter events, 4.6 us)
Async XLA Ops:
  0.6 3.1 %copy-start.1 = (bf16[1,1,1024,384]{3,2,1,0:T(8,128)(2,1)S(1)}, bf16[1,1,1024,384]{3,2,1,0:T(8,128)(2,1)}, u32[]{:S(2)}) copy-start(bf16[1,1,1024,384]{3,2,1,0:T(8,128)(2,1)} %param.18) | copy-start | bytes 2359300
  2.4 2.0 %copy-start = (bf16[64,1152]{1,0:T(8,128)(2,1)S(1)}, bf16[64,1152]{1,0:T(8,128)(2,1)}, u32[]{:S(2)}) copy-start(bf16[64,1152]{1,0:T(8,128)(2,1)} %shard_map.113) | copy-start | bytes 442372
  2.4 5.6 %copy-start.2 = (bf16[1,64,1024]{2,1,0:T(8,128)(2,1)S(1)}, bf16[1,64,1024]{2,1,0:T(8,128)(2,1)}, u32[]{:S(2)}) copy-start(bf16[1,64,1024]{2,1,0:T(8,128)(2,1)} %param.13) | copy-start | bytes 393220
  2.4 16.9 %copy-start.3 = (bf16[1,64,1024]{2,1,0:T(8,128)(2,1)S(1)}, bf16[1,64,1024]{2,1,0:T(8,128)(2,1)}, u32[]{:S(2)}) copy-start(bf16[1,64,1024]{2,1,0:T(8,128)(2,1)} %param.16) | copy-start | bytes 393220
  3.9 36.9 %collective-permute-start.4 = (bf16[1024,768]{1,0:T(8,128)(2,1)S(1)}, bf16[1024,768]{1,0:T(8,128)(2,1)}, u32[]{:S(2)}, u32[]{:S(2)}) collective-permute-start(bf16[1024,768]{1,0:T(8,128)(2,1)S(1)} %constant_dynamic-update-slice_fusion.refs_0_), channel_id=1, source_target_pairs={{0,1},{1,0},{2,3},{3,2},{4,5},{5,4},{6,7},{7,6},{8,9},{9,8},{10,11... | collective-permute-start | bytes 4718600 | tf_op jit(solution)/shard_map/ppermute | solution.py:31
  4.4 14.3 %collective-permute-start.1 = (bf16[64,1152]{1,0:T(8,128)(2,1)S(1)}, bf16[64,1152]{1,0:T(8,128)(2,1)S(1)}, u32[]{:S(2)}, u32[]{:S(2)}) collective-permute-start(bf16[64,1152]{1,0:T(8,128)(2,1)S(1)} %copy-done), channel_id=1, source_target_pairs={{0,8},{1,9},{2,10},{3,11},{4,12},{5,13},{6,14},{7,15},{8,0},{9,1},... | collective-permute-start | bytes 442376 | tf_op jit(solution)/shard_map/ppermute | solution.py:31
  8.1 14.7 %collective-permute-start.12 = (bf16[64,1024]{1,0:T(8,128)(2,1)S(1)}, bf16[64,1024]{1,0:T(8,128)(2,1)S(1)}, u32[]{:S(2)}, u32[]{:S(2)}) collective-permute-start(bf16[64,1024]{1,0:T(8,128)(2,1)S(1)} %bitcast.25), channel_id=1, source_target_pairs={{0,8},{1,9},{2,10},{3,11},{4,12},{5,13},{6,14},{7,15},{8,0},{9,1},... | collective-permute-start | bytes 393224 | tf_op jit(solution)/shard_map/ppermute | solution.py:31
  18.8 11.6 %collective-permute-start.2 = (bf16[128,1152]{1,0:T(8,128)(2,1)S(1)}, bf16[128,1152]{1,0:T(8,128)(2,1)S(1)}, u32[]{:S(2)}, u32[]{:S(2)}) collective-permute-start(bf16[128,1152]{1,0:T(8,128)(2,1)S(1)} %pad_maximum_fusion.3), channel_id=1, source_target_pairs={{0,4},{1,3},{2,6},{3,1},{4,0},{5,7},{6,2},{7,5},{8,12},{9,11},{10,... | collective-permute-start | bytes 884744 | tf_op jit(solution)/shard_map/ppermute | solution.py:31
  19.3 7.9 %collective-permute-start.15 = (bf16[64,1024]{1,0:T(8,128)(2,1)S(1)}, bf16[64,1024]{1,0:T(8,128)(2,1)S(1)}, u32[]{:S(2)}, u32[]{:S(2)}) collective-permute-start(bf16[64,1024]{1,0:T(8,128)(2,1)S(1)} %bitcast.28), channel_id=1, source_target_pairs={{0,8},{1,9},{2,10},{3,11},{4,12},{5,13},{6,14},{7,15},{8,0},{9,1},... | collective-permute-start | bytes 393224 | tf_op jit(solution)/shard_map/ppermute | solution.py:31
  22.7 16.7 %collective-permute-start.5 = (bf16[384,1024]{1,0:T(8,128)(2,1)}, bf16[384,1024]{1,0:T(8,128)(2,1)}, u32[]{:S(2)}, u32[]{:S(2)}) collective-permute-start(bf16[384,1024]{1,0:T(8,128)(2,1)} %bitcast.12.refs_1_), channel_id=1, source_target_pairs={{0,1},{1,0},{2,3},{3,2},{4,5},{5,4},{6,7},{7,6},{8,9},{9,8},{10,11... | collective-permute-start | bytes 2359304 | tf_op jit(solution)/shard_map/ppermute | solution.py:31
  22.7 10.1 %collective-permute-start.13 = (bf16[128,1024]{1,0:T(8,128)(2,1)S(1)}, bf16[128,1024]{1,0:T(8,128)(2,1)S(1)}, u32[]{:S(2)}, u32[]{:S(2)}) collective-permute-start(bf16[128,1024]{1,0:T(8,128)(2,1)S(1)} %pad_maximum_fusion.4), channel_id=1, source_target_pairs={{0,4},{1,3},{2,6},{3,1},{4,0},{5,7},{6,2},{7,5},{8,12},{9,11},{10,... | collective-permute-start | bytes 786440 | tf_op jit(solution)/shard_map/ppermute | solution.py:31
  27.3 12.1 %copy-start.4 = (bf16[1,64,1024]{2,1,0:T(8,128)(2,1)S(1)}, bf16[1,64,1024]{2,1,0:T(8,128)(2,1)}, u32[]{:S(2)}) copy-start(bf16[1,64,1024]{2,1,0:T(8,128)(2,1)} %param.10) | copy-start | bytes 393220
  27.3 11.2 %collective-permute-start.16 = (bf16[128,1024]{1,0:T(8,128)(2,1)S(1)}, bf16[128,1024]{1,0:T(8,128)(2,1)S(1)}, u32[]{:S(2)}, u32[]{:S(2)}) collective-permute-start(bf16[128,1024]{1,0:T(8,128)(2,1)S(1)} %pad_maximum_fusion.5), channel_id=1, source_target_pairs={{0,4},{1,3},{2,6},{3,1},{4,0},{5,7},{6,2},{7,5},{8,12},{9,11},{10,... | collective-permute-start | bytes 786440 | tf_op jit(solution)/shard_map/ppermute | solution.py:31
  30.4 13.2 %collective-permute-start.3 = (bf16[256,1152]{1,0:T(8,128)(2,1)S(1)}, bf16[256,1152]{1,0:T(8,128)(2,1)}, u32[]{:S(2)}, u32[]{:S(2)}) collective-permute-start(bf16[256,1152]{1,0:T(8,128)(2,1)S(1)} %pad_maximum_fusion.refs_0_.refs_2_), channel_id=1, source_target_pairs={{0,2},{1,5},{2,0},{3,7},{4,6},{5,1},{6,4},{7,3},{8,10},{9,13},{10,... | collective-permute-start | bytes 1769480 | tf_op jit(solution)/shard_map/ppermute | solution.py:31
  32.9 18.3 %collective-permute-start.14 = (bf16[256,1024]{1,0:T(8,128)(2,1)S(1)}, bf16[256,1024]{1,0:T(8,128)(2,1)}, u32[]{:S(2)}, u32[]{:S(2)}) collective-permute-start(bf16[256,1024]{1,0:T(8,128)(2,1)S(1)} %pad_maximum_fusion.1.refs_0_), channel_id=1, source_target_pairs={{0,2},{1,5},{2,0},{3,7},{4,6},{5,1},{6,4},{7,3},{8,10},{9,13},{10,... | collective-permute-start | bytes 1572872 | tf_op jit(solution)/shard_map/ppermute | solution.py:31
  38.5 13.5 %collective-permute-start.17 = (bf16[256,1024]{1,0:T(8,128)(2,1)S(1)}, bf16[256,1024]{1,0:T(8,128)(2,1)}, u32[]{:S(2)}, u32[]{:S(2)}) collective-permute-start(bf16[256,1024]{1,0:T(8,128)(2,1)S(1)} %pad_maximum_fusion.2.refs_1_), channel_id=1, source_target_pairs={{0,2},{1,5},{2,0},{3,7},{4,6},{5,1},{6,4},{7,3},{8,10},{9,13},{10,... | collective-permute-start | bytes 1572872 | tf_op jit(solution)/shard_map/ppermute | solution.py:31
  39.4 38.0 %collective-permute-start = (bf16[64,1024]{1,0:T(8,128)(2,1)S(1)}, bf16[64,1024]{1,0:T(8,128)(2,1)S(1)}, u32[]{:S(2)}, u32[]{:S(2)}) collective-permute-start(bf16[64,1024]{1,0:T(8,128)(2,1)S(1)} %bitcast.33), channel_id=1, source_target_pairs={{0,16},{1,17},{2,18},{3,19},{4,20},{5,21},{6,22},{7,23},{8,24},{9,... | collective-permute-start | bytes 393224 | tf_op jit(solution)/shard_map/ppermute | solution.py:26
  40.7 38.5 %collective-permute-start.11 = (bf16[64,1024]{1,0:T(8,128)(2,1)S(1)}, bf16[64,1024]{1,0:T(8,128)(2,1)S(1)}, u32[]{:S(2)}, u32[]{:S(2)}) collective-permute-start(bf16[64,1024]{1,0:T(8,128)(2,1)S(1)} %bitcast.31), channel_id=1, source_target_pairs={{0,16},{1,17},{2,18},{3,19},{4,20},{5,21},{6,22},{7,23},{8,24},{9,... | collective-permute-start | bytes 393224 | tf_op jit(solution)/shard_map/ppermute | solution.py:26
  47.2 10.8 %collective-permute-start.6 = (bf16[128,1024]{1,0:T(8,128)(2,1)S(1)}, bf16[128,1024]{1,0:T(8,128)(2,1)S(1)}, u32[]{:S(2)}, u32[]{:S(2)}) collective-permute-start(bf16[128,1024]{1,0:T(8,128)(2,1)S(1)} %get-tuple-element.25), channel_id=1, source_target_pairs={{0,2},{1,5},{2,0},{3,7},{4,6},{5,1},{6,4},{7,3},{8,10},{9,13},{10,... | collective-permute-start | bytes 786440 | tf_op jit(solution)/shard_map/ppermute | solution.py:31
  51.3 14.8 %collective-permute-start.8 = (bf16[128,1024]{1,0:T(8,128)(2,1)S(1)}, bf16[128,1024]{1,0:T(8,128)(2,1)S(1)}, u32[]{:S(2)}, u32[]{:S(2)}) collective-permute-start(bf16[128,1024]{1,0:T(8,128)(2,1)S(1)} %get-tuple-element.26), channel_id=1, source_target_pairs={{0,2},{1,5},{2,0},{3,7},{4,6},{5,1},{6,4},{7,3},{8,10},{9,13},{10,... | collective-permute-start | bytes 786440 | tf_op jit(solution)/shard_map/ppermute | solution.py:31
  56.6 8.2 %collective-permute-start.18 = (bf16[128,1024]{1,0:T(8,128)(2,1)S(1)}, bf16[128,1024]{1,0:T(8,128)(2,1)S(1)}, u32[]{:S(2)}, u32[]{:S(2)}) collective-permute-start(bf16[128,1024]{1,0:T(8,128)(2,1)S(1)} %get-tuple-element.32), channel_id=1, source_target_pairs={{0,2},{1,5},{2,0},{3,7},{4,6},{5,1},{6,4},{7,3},{8,10},{9,13},{10,... | collective-permute-start | bytes 786440 | tf_op jit(solution)/shard_map/ppermute | solution.py:31
  58.1 9.7 %collective-permute-start.7 = (bf16[128,1024]{1,0:T(8,128)(2,1)S(1)}, bf16[128,1024]{1,0:T(8,128)(2,1)S(1)}, u32[]{:S(2)}, u32[]{:S(2)}) collective-permute-start(bf16[128,1024]{1,0:T(8,128)(2,1)S(1)} %add_convert_fusion.3), channel_id=1, source_target_pairs={{0,4},{1,3},{2,6},{3,1},{4,0},{5,7},{6,2},{7,5},{8,12},{9,11},{10,... | collective-permute-start | bytes 786440 | tf_op jit(solution)/shard_map/ppermute | solution.py:31
  64.8 7.3 %collective-permute-start.20 = (bf16[128,1024]{1,0:T(8,128)(2,1)S(1)}, bf16[128,1024]{1,0:T(8,128)(2,1)S(1)}, u32[]{:S(2)}, u32[]{:S(2)}) collective-permute-start(bf16[128,1024]{1,0:T(8,128)(2,1)S(1)} %get-tuple-element.33), channel_id=1, source_target_pairs={{0,2},{1,5},{2,0},{3,7},{4,6},{5,1},{6,4},{7,3},{8,10},{9,13},{10,... | collective-permute-start | bytes 786440 | tf_op jit(solution)/shard_map/ppermute | solution.py:31
  66.1 7.6 %collective-permute-start.19 = (bf16[128,1024]{1,0:T(8,128)(2,1)S(1)}, bf16[128,1024]{1,0:T(8,128)(2,1)S(1)}, u32[]{:S(2)}, u32[]{:S(2)}) collective-permute-start(bf16[128,1024]{1,0:T(8,128)(2,1)S(1)} %add_convert_fusion.1), channel_id=1, source_target_pairs={{0,4},{1,3},{2,6},{3,1},{4,0},{5,7},{6,2},{7,5},{8,12},{9,11},{10,... | collective-permute-start | bytes 786440 | tf_op jit(solution)/shard_map/ppermute | solution.py:31
  67.9 10.3 %collective-permute-start.10 = (bf16[64,1024]{1,0:T(8,128)(2,1)S(1)}, bf16[64,1024]{1,0:T(8,128)(2,1)S(1)}, u32[]{:S(2)}, u32[]{:S(2)}) collective-permute-start(bf16[64,1024]{1,0:T(8,128)(2,1)S(1)} %get-tuple-element.37), channel_id=1, source_target_pairs={{0,24},{1,25},{2,26},{3,27},{4,28},{5,29},{6,30},{7,31},{8,16},{9,... | collective-permute-start | bytes 393224 | tf_op jit(solution)/shard_map/ppermute | solution.py:26
  72.1 6.4 %collective-permute-start.9 = (bf16[64,1024]{1,0:T(8,128)(2,1)S(1)}, bf16[64,1024]{1,0:T(8,128)(2,1)S(1)}, u32[]{:S(2)}, u32[]{:S(2)}) collective-permute-start(bf16[64,1024]{1,0:T(8,128)(2,1)S(1)} %get-tuple-element.36), channel_id=1, source_target_pairs={{0,16},{1,17},{2,18},{3,19},{4,20},{5,21},{6,22},{7,23},{8,24},{9,... | collective-permute-start | bytes 393224 | tf_op jit(solution)/shard_map/ppermute | solution.py:26
  73.8 9.3 %collective-permute-start.22 = (bf16[64,1024]{1,0:T(8,128)(2,1)S(1)}, bf16[64,1024]{1,0:T(8,128)(2,1)S(1)}, u32[]{:S(2)}, u32[]{:S(2)}) collective-permute-start(bf16[64,1024]{1,0:T(8,128)(2,1)S(1)} %get-tuple-element.35), channel_id=1, source_target_pairs={{0,24},{1,25},{2,26},{3,27},{4,28},{5,29},{6,30},{7,31},{8,16},{9,... | collective-permute-start | bytes 393224 | tf_op jit(solution)/shard_map/ppermute | solution.py:26
  77.4 5.9 %collective-permute-start.21 = (bf16[64,1024]{1,0:T(8,128)(2,1)S(1)}, bf16[64,1024]{1,0:T(8,128)(2,1)S(1)}, u32[]{:S(2)}, u32[]{:S(2)}) collective-permute-start(bf16[64,1024]{1,0:T(8,128)(2,1)S(1)} %get-tuple-element.34), channel_id=1, source_target_pairs={{0,16},{1,17},{2,18},{3,19},{4,20},{5,21},{6,22},{7,23},{8,24},{9,... | collective-permute-start | bytes 393224 | tf_op jit(solution)/shard_map/ppermute | solution.py:26

commit v6 on v4

--- a/solution.py
+++ b/solution.py
@@ -312,7 +312,7 @@
     arrays["f"] = packed(arrays["f"], *words)
     down0 = w_down[0, 0]
     pair = [w_gate[0, 0], w_up[0, 0]]
-    *pair, down0 = behind([*pair, down0], [arrays["f"]])
+    pair = behind(pair, [arrays["f"]])
     gate_up0 = jnp.concatenate(pair, axis=1)
     chip = [{1: 1}] * 2
     gate_up1, down1 = swapped(gate_up0, chip, 1), swapped(down0, chip, 1)

time: 83.9 us -> 83.9 us (level)
  no operation moved by 1% of the time
where the time goes in v6:
time: 83.9 us; the launch traced here: 83.4 us
  starting transfers between devices  34.3 us (41%)
  waiting for transfers between devices  25.8 us (31%)
  Pallas kernels  19.1 us (23%)
  other arithmetic  1.91 us (2%)
  local copies, waits for them, and re-layouts  1.48 us (2%)
    ppermute x17, starting transfers between devices, swapped(): return lax.ppermute(block, 'expert', route)  22.7 us
    ppermute x17, waiting for transfers between devices, swapped(): return lax.ppermute(block, 'expert', route)  21.7 us
    pallas_call x4, Pallas kernels, weighted(): pl.pallas_call(functools.partial(expert_kernel, each, topk, first, rows,...  15.2 us
    ppermute x6, starting transfers between devices, passed_along(): return lax.ppermute(block, ('section', 'expert'), route)  11.6 us
    ppermute x6, waiting for transfers between devices, passed_along(): return lax.ppermute(block, ('section', 'expert'), route)  4.1 us
    pallas_call x1, Pallas kernels, loaded(): pl.pallas_call(functools.partial(loading_kernel, places), out_shape=jax.S...  2.1 us
    pallas_call x1, Pallas kernels, packed(): pl.pallas_call(packing_kernel, out_shape=jax.ShapeDtypeStruct((length, wi...  1.77 us
  transfers between devices with their start and end apart: 23, of which 7 were waited for; matrix products, arithmetic and copies ran while one was open for 1% of the time, Pallas kernels for 21%

profile of v6, /device:TPU:0, one launch (start us, length us, event | category | flops | bytes accessed | tf_op | source)
XLA Modules:
  0.0 83.4 jit_solution(6977827431556514313)
XLA Ops:
  0.6 1.8 %shard_map.113 = bf16[64,1152]{1,0:T(8,128)(2,1)} custom-call(bf16[64,1024]{1,0:T(8,128)(2,1)} %bitcast.32, s32[8,64]{1,0:T(8,128)} %bitcast.34, f32[8,64]{1,0:T(8,128)} %bitcast.35, s32[8,64]{1,0:T(8,128)} %bitcast.36, f32[8,64]{1,0:T(8,128)} %bitcast.37), custom_call_target="tpu_custom_call" | custom-call | flops 1 | bytes 1 | tf_op jit(solution)/shard_map/pallas_call | solution.py:118
  2.4 1.3 %constant_dynamic-update-slice_fusion.1 = bf16[1024,768]{1,0:T(8,128)(2,1)S(1)} fusion(bf16[1024,384]{1,0:T(8,128)(2,1)} %bitcast.23), kind=kLoop, calls=%fused_computation.15 | loop fusion | bytes 1572864
  4.4 3.7 %collective-permute-start.1 = (bf16[64,1152]{1,0:T(8,128)(2,1)S(1)}, bf16[64,1152]{1,0:T(8,128)(2,1)S(1)}, u32[]{:S(2)}, u32[]{:S(2)}) collective-permute-start(bf16[64,1152]{1,0:T(8,128)(2,1)S(1)} %copy-done), channel_id=1, source_target_pairs={{0,8},{1,9},{2,10},{3,11},{4,12},{5,13},{6,14},{7,15},{8,0},{9,1},... | collective-permute-start | bytes 442376 | tf_op jit(solution)/shard_map/ppermute | solution.py:31
  8.1 10.6 %collective-permute-done.1 = bf16[64,1152]{1,0:T(8,128)(2,1)S(1)} collective-permute-done((bf16[64,1152]{1,0:T(8,128)(2,1)S(1)}, bf16[64,1152]{1,0:T(8,128)(2,1)S(1)}, u32[]{:S(2)}, u32[]{:S(2)}) %collective-permute-start.1) | collective-permute-done | bytes 147488 | tf_op jit(solution)/shard_map/ppermute | solution.py:31
  19.3 3.4 %collective-permute-start.15 = (bf16[64,1024]{1,0:T(8,128)(2,1)S(1)}, bf16[64,1024]{1,0:T(8,128)(2,1)S(1)}, u32[]{:S(2)}, u32[]{:S(2)}) collective-permute-start(bf16[64,1024]{1,0:T(8,128)(2,1)S(1)} %bitcast.28), channel_id=1, source_target_pairs={{0,8},{1,9},{2,10},{3,11},{4,12},{5,13},{6,14},{7,15},{8,0},{9,1},... | collective-permute-start | bytes 393224 | tf_op jit(solution)/shard_map/ppermute | solution.py:31
  22.7 1.0 %collective-permute-start.13 = (bf16[128,1024]{1,0:T(8,128)(2,1)S(1)}, bf16[128,1024]{1,0:T(8,128)(2,1)S(1)}, u32[]{:S(2)}, u32[]{:S(2)}) collective-permute-start(bf16[128,1024]{1,0:T(8,128)(2,1)S(1)} %pad_maximum_fusion.4), channel_id=1, source_target_pairs={{0,4},{1,3},{2,6},{3,1},{4,0},{5,7},{6,2},{7,5},{8,12},{9,11},{10,... | collective-permute-start | bytes 786440 | tf_op jit(solution)/shard_map/ppermute | solution.py:31
  23.8 3.5 %collective-permute-done.15 = bf16[64,1024]{1,0:T(8,128)(2,1)S(1)} collective-permute-done((bf16[64,1024]{1,0:T(8,128)(2,1)S(1)}, bf16[64,1024]{1,0:T(8,128)(2,1)S(1)}, u32[]{:S(2)}, u32[]{:S(2)}) %collective-permute-start.15) | collective-permute-done | bytes 131104 | tf_op jit(solution)/shard_map/ppermute | solution.py:31
  27.3 3.0 %collective-permute-start.16 = (bf16[128,1024]{1,0:T(8,128)(2,1)S(1)}, bf16[128,1024]{1,0:T(8,128)(2,1)S(1)}, u32[]{:S(2)}, u32[]{:S(2)}) collective-permute-start(bf16[128,1024]{1,0:T(8,128)(2,1)S(1)} %pad_maximum_fusion.5), channel_id=1, source_target_pairs={{0,4},{1,3},{2,6},{3,1},{4,0},{5,7},{6,2},{7,5},{8,12},{9,11},{10,... | collective-permute-start | bytes 786440 | tf_op jit(solution)/shard_map/ppermute | solution.py:31
  30.4 1.1 %collective-permute-start.3 = (bf16[256,1152]{1,0:T(8,128)(2,1)S(1)}, bf16[256,1152]{1,0:T(8,128)(2,1)}, u32[]{:S(2)}, u32[]{:S(2)}) collective-permute-start(bf16[256,1152]{1,0:T(8,128)(2,1)S(1)} %pad_maximum_fusion.refs_0_.refs_2_), channel_id=1, source_target_pairs={{0,2},{1,5},{2,0},{3,7},{4,6},{5,1},{6,4},{7,3},{8,10},{9,13},{10,... | collective-permute-start | bytes 1769480 | tf_op jit(solution)/shard_map/ppermute | solution.py:31
  31.5 1.4 %collective-permute-done.13 = bf16[128,1024]{1,0:T(8,128)(2,1)S(1)} collective-permute-done((bf16[128,1024]{1,0:T(8,128)(2,1)S(1)}, bf16[128,1024]{1,0:T(8,128)(2,1)S(1)}, u32[]{:S(2)}, u32[]{:S(2)}) %collective-permute-start.13) | collective-permute-done | bytes 262176 | tf_op jit(solution)/shard_map/ppermute | solution.py:31
  32.9 0.9 %collective-permute-start.14 = (bf16[256,1024]{1,0:T(8,128)(2,1)S(1)}, bf16[256,1024]{1,0:T(8,128)(2,1)}, u32[]{:S(2)}, u32[]{:S(2)}) collective-permute-start(bf16[256,1024]{1,0:T(8,128)(2,1)S(1)} %pad_maximum_fusion.1.refs_0_), channel_id=1, source_target_pairs={{0,2},{1,5},{2,0},{3,7},{4,6},{5,1},{6,4},{7,3},{8,10},{9,13},{10,... | collective-permute-start | bytes 1572872 | tf_op jit(solution)/shard_map/ppermute | solution.py:31
  33.8 4.7 %collective-permute-done.16 = bf16[128,1024]{1,0:T(8,128)(2,1)S(1)} collective-permute-done((bf16[128,1024]{1,0:T(8,128)(2,1)S(1)}, bf16[128,1024]{1,0:T(8,128)(2,1)S(1)}, u32[]{:S(2)}, u32[]{:S(2)}) %collective-permute-start.16) | collective-permute-done | bytes 262176 | tf_op jit(solution)/shard_map/ppermute | solution.py:31
  38.5 0.9 %collective-permute-start.17 = (bf16[256,1024]{1,0:T(8,128)(2,1)S(1)}, bf16[256,1024]{1,0:T(8,128)(2,1)}, u32[]{:S(2)}, u32[]{:S(2)}) collective-permute-start(bf16[256,1024]{1,0:T(8,128)(2,1)S(1)} %pad_maximum_fusion.2.refs_1_), channel_id=1, source_target_pairs={{0,2},{1,5},{2,0},{3,7},{4,6},{5,1},{6,4},{7,3},{8,10},{9,13},{10,... | collective-permute-start | bytes 1572872 | tf_op jit(solution)/shard_map/ppermute | solution.py:31
  39.4 1.3 %collective-permute-start = (bf16[64,1024]{1,0:T(8,128)(2,1)S(1)}, bf16[64,1024]{1,0:T(8,128)(2,1)S(1)}, u32[]{:S(2)}, u32[]{:S(2)}) collective-permute-start(bf16[64,1024]{1,0:T(8,128)(2,1)S(1)} %bitcast.33), channel_id=1, source_target_pairs={{0,16},{1,17},{2,18},{3,19},{4,20},{5,21},{6,22},{7,23},{8,24},{9,... | collective-permute-start | bytes 393224 | tf_op jit(solution)/shard_map/ppermute | solution.py:26
  41.4 2.1 %shard_map.114.refs_1_.refs_3_ = bf16[2816,1024]{1,0:T(8,128)(2,1)S(1)} custom-call(bf16[1024,768]{1,0:T(8,128)(2,1)S(1)} %constant_dynamic-update-slice_fusion.refs_0_, bf16[384,1024]{1,0:T(8,128)(2,1)} %bitcast.12.refs_1_, bf16[1024,768]{1,0:T(8,128)(2,1)} %collective-permute-done.4.refs_2_, bf16[384,1024]{1,0:T(8,128)(2,1)} %collective-permute-done.5.refs_3_), custom_call_target="tpu_custom_call" | custom-call | flops 1 | bytes 1 | tf_op jit(solution)/shard_map/pallas_call | solution.py:175
  43.5 3.7 %shard_map.115 = (bf16[128,1024]{1,0:T(8,128)(2,1)S(1)}, bf16[128,1024]{1,0:T(8,128)(2,1)S(1)}) custom-call(s32[1]{0:T(128)} %bitcast.1.me_ref, bf16[256,1152]{1,0:T(8,128)(2,1)} %collective-permute-done.3.refs_0_.refs_2_, bf16[2816,1024]{1,0:T(8,128)(2,1)S(1)} %shard_map.114.refs_1_.refs_3_), custom_call_target="tpu_custom_call" | custom-call | flops 1207959552 | bytes 589824 | tf_op jit(solution)/shard_map/pallas_call | solution.py:266
  47.2 1.4 %collective-permute-start.6 = (bf16[128,1024]{1,0:T(8,128)(2,1)S(1)}, bf16[128,1024]{1,0:T(8,128)(2,1)S(1)}, u32[]{:S(2)}, u32[]{:S(2)}) collective-permute-start(bf16[128,1024]{1,0:T(8,128)(2,1)S(1)} %get-tuple-element.23), channel_id=1, source_target_pairs={{0,2},{1,5},{2,0},{3,7},{4,6},{5,1},{6,4},{7,3},{8,10},{9,13},{10,... | collective-permute-start | bytes 786440 | tf_op jit(solution)/shard_map/ppermute | solution.py:31
  48.6 2.6 %shard_map.116 = f32[256,1024]{1,0:T(8,128)S(1)} custom-call(s32[1]{0:T(128)} %bitcast.1.me_ref, bf16[256,1152]{1,0:T(8,128)(2,1)S(1)} %pad_maximum_fusion.refs_0_.refs_2_, bf16[2816,1024]{1,0:T(8,128)(2,1)S(1)} %shard_map.114.refs_1_.refs_3_), custom_call_target="tpu_custom_call" | custom-call | flops 1207959552 | bytes 589824 | tf_op jit(solution)/shard_map/pallas_call | solution.py:266
  51.3 0.8 collective-permute-start.8
  52.0 4.4 %shard_map.117 = (bf16[128,1024]{1,0:T(8,128)(2,1)S(1)}, bf16[128,1024]{1,0:T(8,128)(2,1)S(1)}) custom-call(s32[1]{0:T(128)} %bitcast.1.me_ref, bf16[256,1024]{1,0:T(8,128)(2,1)} %collective-permute-done.14.refs_0_, bf16[256,1024]{1,0:T(8,128)(2,1)} %collective-permute-done.17.refs_1_, bf16[256,1152]{1,0:T(8,128)(2,1)} %collective-permute-done.3.refs_0_.refs_2_, ...), custom_call_target="tpu_custom_call" | custom-call | flops 2013265920 | bytes 1638400 | tf_op jit(solution)/shard_map/pallas_call | solution.py:266
  56.5 1.4 %collective-permute-start.18 = (bf16[128,1024]{1,0:T(8,128)(2,1)S(1)}, bf16[128,1024]{1,0:T(8,128)(2,1)S(1)}, u32[]{:S(2)}, u32[]{:S(2)}) collective-permute-start(bf16[128,1024]{1,0:T(8,128)(2,1)S(1)} %get-tuple-element.30), channel_id=1, source_target_pairs={{0,2},{1,5},{2,0},{3,7},{4,6},{5,1},{6,4},{7,3},{8,10},{9,13},{10,... | collective-permute-start | bytes 786440 | tf_op jit(solution)/shard_map/ppermute | solution.py:31
  57.9 1.0 %collective-permute-start.7 = (bf16[128,1024]{1,0:T(8,128)(2,1)S(1)}, bf16[128,1024]{1,0:T(8,128)(2,1)S(1)}, u32[]{:S(2)}, u32[]{:S(2)}) collective-permute-start(bf16[128,1024]{1,0:T(8,128)(2,1)S(1)} %add_convert_fusion.3), channel_id=1, source_target_pairs={{0,4},{1,3},{2,6},{3,1},{4,0},{5,7},{6,2},{7,5},{8,12},{9,11},{10,... | collective-permute-start | bytes 786440 | tf_op jit(solution)/shard_map/ppermute | solution.py:31
  59.0 4.5 %shard_map.118 = f32[256,1024]{1,0:T(8,128)S(1)} custom-call(s32[1]{0:T(128)} %bitcast.1.me_ref, bf16[256,1024]{1,0:T(8,128)(2,1)S(1)} %pad_maximum_fusion.1.refs_0_, bf16[256,1024]{1,0:T(8,128)(2,1)S(1)} %pad_maximum_fusion.2.refs_1_, bf16[256,1152]{1,0:T(8,128)(2,1)S(1)} %pad_maximum_fusion.refs_0_.refs_2_, bf16[2816,1024]{1,0:T(8,128)(2,1)S(1)} %shard_map.114.refs_1_.refs_3_), custom_call_target="tpu_custom_call" | custom-call | flops 2013265920 | bytes 1638400 | tf_op jit(solution)/shard_map/pallas_call | solution.py:266
  63.5 1.1 %collective-permute-done.18 = bf16[128,1024]{1,0:T(8,128)(2,1)S(1)} collective-permute-done((bf16[128,1024]{1,0:T(8,128)(2,1)S(1)}, bf16[128,1024]{1,0:T(8,128)(2,1)S(1)}, u32[]{:S(2)}, u32[]{:S(2)}) %collective-permute-start.18) | collective-permute-done | bytes 262176 | tf_op jit(solution)/shard_map/ppermute | solution.py:31
  64.6 1.2 %collective-permute-start.20 = (bf16[128,1024]{1,0:T(8,128)(2,1)S(1)}, bf16[128,1024]{1,0:T(8,128)(2,1)S(1)}, u32[]{:S(2)}, u32[]{:S(2)}) collective-permute-start(bf16[128,1024]{1,0:T(8,128)(2,1)S(1)} %get-tuple-element.31), channel_id=1, source_target_pairs={{0,2},{1,5},{2,0},{3,7},{4,6},{5,1},{6,4},{7,3},{8,10},{9,13},{10,... | collective-permute-start | bytes 786440 | tf_op jit(solution)/shard_map/ppermute | solution.py:31
  65.9 1.7 %collective-permute-start.19 = (bf16[128,1024]{1,0:T(8,128)(2,1)S(1)}, bf16[128,1024]{1,0:T(8,128)(2,1)S(1)}, u32[]{:S(2)}, u32[]{:S(2)}) collective-permute-start(bf16[128,1024]{1,0:T(8,128)(2,1)S(1)} %add_convert_fusion.1), channel_id=1, source_target_pairs={{0,4},{1,3},{2,6},{3,1},{4,0},{5,7},{6,2},{7,5},{8,12},{9,11},{10,... | collective-permute-start | bytes 786440 | tf_op jit(solution)/shard_map/ppermute | solution.py:31
  67.8 3.4 %collective-permute-start.10 = (bf16[64,1024]{1,0:T(8,128)(2,1)S(1)}, bf16[64,1024]{1,0:T(8,128)(2,1)S(1)}, u32[]{:S(2)}, u32[]{:S(2)}) collective-permute-start(bf16[64,1024]{1,0:T(8,128)(2,1)S(1)} %get-tuple-element.35), channel_id=1, source_target_pairs={{0,24},{1,25},{2,26},{3,27},{4,28},{5,29},{6,30},{7,31},{8,16},{9,... | collective-permute-start | bytes 393224 | tf_op jit(solution)/shard_map/ppermute | solution.py:26
  71.7 1.5 %collective-permute-start.9 = (bf16[64,1024]{1,0:T(8,128)(2,1)S(1)}, bf16[64,1024]{1,0:T(8,128)(2,1)S(1)}, u32[]{:S(2)}, u32[]{:S(2)}) collective-permute-start(bf16[64,1024]{1,0:T(8,128)(2,1)S(1)} %get-tuple-element.34), channel_id=1, source_target_pairs={{0,16},{1,17},{2,18},{3,19},{4,20},{5,21},{6,22},{7,23},{8,24},{9,... | collective-permute-start | bytes 393224 | tf_op jit(solution)/shard_map/ppermute | solution.py:26
  73.3 3.7 %collective-permute-start.22 = (bf16[64,1024]{1,0:T(8,128)(2,1)S(1)}, bf16[64,1024]{1,0:T(8,128)(2,1)S(1)}, u32[]{:S(2)}, u32[]{:S(2)}) collective-permute-start(bf16[64,1024]{1,0:T(8,128)(2,1)S(1)} %get-tuple-element.33), channel_id=1, source_target_pairs={{0,24},{1,25},{2,26},{3,27},{4,28},{5,29},{6,30},{7,31},{8,16},{9,... | collective-permute-start | bytes 393224 | tf_op jit(solution)/shard_map/ppermute | solution.py:26
  77.0 0.9 %collective-permute-start.21 = (bf16[64,1024]{1,0:T(8,128)(2,1)S(1)}, bf16[64,1024]{1,0:T(8,128)(2,1)S(1)}, u32[]{:S(2)}, u32[]{:S(2)}) collective-permute-start(bf16[64,1024]{1,0:T(8,128)(2,1)S(1)} %get-tuple-element.32), channel_id=1, source_target_pairs={{0,16},{1,17},{2,18},{3,19},{4,20},{5,21},{6,22},{7,23},{8,24},{9,... | collective-permute-start | bytes 393224 | tf_op jit(solution)/shard_map/ppermute | solution.py:26
  77.9 0.7 fusion
  78.6 4.1 %collective-permute-done.22 = bf16[64,1024]{1,0:T(8,128)(2,1)S(1)} collective-permute-done((bf16[64,1024]{1,0:T(8,128)(2,1)S(1)}, bf16[64,1024]{1,0:T(8,128)(2,1)S(1)}, u32[]{:S(2)}, u32[]{:S(2)}) %collective-permute-start.22) | collective-permute-done | bytes 131104 | tf_op jit(solution)/shard_map/ppermute | solution.py:26
  (46 shorter events, 3.8 us)
Async XLA Ops:
  0.6 3.1 %copy-start.1 = (bf16[1,1,1024,384]{3,2,1,0:T(8,128)(2,1)S(1)}, bf16[1,1,1024,384]{3,2,1,0:T(8,128)(2,1)}, u32[]{:S(2)}) copy-start(bf16[1,1,1024,384]{3,2,1,0:T(8,128)(2,1)} %param.18) | copy-start | bytes 2359300
  2.4 2.0 %copy-start = (bf16[64,1152]{1,0:T(8,128)(2,1)S(1)}, bf16[64,1152]{1,0:T(8,128)(2,1)}, u32[]{:S(2)}) copy-start(bf16[64,1152]{1,0:T(8,128)(2,1)} %shard_map.113) | copy-start | bytes 442372
  2.4 5.6 %copy-start.2 = (bf16[1,64,1024]{2,1,0:T(8,128)(2,1)S(1)}, bf16[1,64,1024]{2,1,0:T(8,128)(2,1)}, u32[]{:S(2)}) copy-start(bf16[1,64,1024]{2,1,0:T(8,128)(2,1)} %param.13) | copy-start | bytes 393220
  2.4 16.9 %copy-start.3 = (bf16[1,64,1024]{2,1,0:T(8,128)(2,1)S(1)}, bf16[1,64,1024]{2,1,0:T(8,128)(2,1)}, u32[]{:S(2)}) copy-start(bf16[1,64,1024]{2,1,0:T(8,128)(2,1)} %param.16) | copy-start | bytes 393220
  3.9 36.9 %collective-permute-start.4 = (bf16[1024,768]{1,0:T(8,128)(2,1)S(1)}, bf16[1024,768]{1,0:T(8,128)(2,1)}, u32[]{:S(2)}, u32[]{:S(2)}) collective-permute-start(bf16[1024,768]{1,0:T(8,128)(2,1)S(1)} %constant_dynamic-update-slice_fusion.refs_0_), channel_id=1, source_target_pairs={{0,1},{1,0},{2,3},{3,2},{4,5},{5,4},{6,7},{7,6},{8,9},{9,8},{10,11... | collective-permute-start | bytes 4718600 | tf_op jit(solution)/shard_map/ppermute | solution.py:31
  4.4 14.3 %collective-permute-start.1 = (bf16[64,1152]{1,0:T(8,128)(2,1)S(1)}, bf16[64,1152]{1,0:T(8,128)(2,1)S(1)}, u32[]{:S(2)}, u32[]{:S(2)}) collective-permute-start(bf16[64,1152]{1,0:T(8,128)(2,1)S(1)} %copy-done), channel_id=1, source_target_pairs={{0,8},{1,9},{2,10},{3,11},{4,12},{5,13},{6,14},{7,15},{8,0},{9,1},... | collective-permute-start | bytes 442376 | tf_op jit(solution)/shard_map/ppermute | solution.py:31
  8.1 14.7 %collective-permute-start.12 = (bf16[64,1024]{1,0:T(8,128)(2,1)S(1)}, bf16[64,1024]{1,0:T(8,128)(2,1)S(1)}, u32[]{:S(2)}, u32[]{:S(2)}) collective-permute-start(bf16[64,1024]{1,0:T(8,128)(2,1)S(1)} %bitcast.25), channel_id=1, source_target_pairs={{0,8},{1,9},{2,10},{3,11},{4,12},{5,13},{6,14},{7,15},{8,0},{9,1},... | collective-permute-start | bytes 393224 | tf_op jit(solution)/shard_map/ppermute | solution.py:31
  18.8 11.6 %collective-permute-start.2 = (bf16[128,1152]{1,0:T(8,128)(2,1)S(1)}, bf16[128,1152]{1,0:T(8,128)(2,1)S(1)}, u32[]{:S(2)}, u32[]{:S(2)}) collective-permute-start(bf16[128,1152]{1,0:T(8,128)(2,1)S(1)} %pad_maximum_fusion.3), channel_id=1, source_target_pairs={{0,4},{1,3},{2,6},{3,1},{4,0},{5,7},{6,2},{7,5},{8,12},{9,11},{10,... | collective-permute-start | bytes 884744 | tf_op jit(solution)/shard_map/ppermute | solution.py:31
  19.3 7.9 %collective-permute-start.15 = (bf16[64,1024]{1,0:T(8,128)(2,1)S(1)}, bf16[64,1024]{1,0:T(8,128)(2,1)S(1)}, u32[]{:S(2)}, u32[]{:S(2)}) collective-permute-start(bf16[64,1024]{1,0:T(8,128)(2,1)S(1)} %bitcast.28), channel_id=1, source_target_pairs={{0,8},{1,9},{2,10},{3,11},{4,12},{5,13},{6,14},{7,15},{8,0},{9,1},... | collective-permute-start | bytes 393224 | tf_op jit(solution)/shard_map/ppermute | solution.py:31
  22.7 16.7 %collective-permute-start.5 = (bf16[384,1024]{1,0:T(8,128)(2,1)}, bf16[384,1024]{1,0:T(8,128)(2,1)}, u32[]{:S(2)}, u32[]{:S(2)}) collective-permute-start(bf16[384,1024]{1,0:T(8,128)(2,1)} %bitcast.12.refs_1_), channel_id=1, source_target_pairs={{0,1},{1,0},{2,3},{3,2},{4,5},{5,4},{6,7},{7,6},{8,9},{9,8},{10,11... | collective-permute-start | bytes 2359304 | tf_op jit(solution)/shard_map/ppermute | solution.py:31
  22.7 10.1 %collective-permute-start.13 = (bf16[128,1024]{1,0:T(8,128)(2,1)S(1)}, bf16[128,1024]{1,0:T(8,128)(2,1)S(1)}, u32[]{:S(2)}, u32[]{:S(2)}) collective-permute-start(bf16[128,1024]{1,0:T(8,128)(2,1)S(1)} %pad_maximum_fusion.4), channel_id=1, source_target_pairs={{0,4},{1,3},{2,6},{3,1},{4,0},{5,7},{6,2},{7,5},{8,12},{9,11},{10,... | collective-permute-start | bytes 786440 | tf_op jit(solution)/shard_map/ppermute | solution.py:31
  27.3 12.1 %copy-start.4 = (bf16[1,64,1024]{2,1,0:T(8,128)(2,1)S(1)}, bf16[1,64,1024]{2,1,0:T(8,128)(2,1)}, u32[]{:S(2)}) copy-start(bf16[1,64,1024]{2,1,0:T(8,128)(2,1)} %param.10) | copy-start | bytes 393220
  27.3 11.2 %collective-permute-start.16 = (bf16[128,1024]{1,0:T(8,128)(2,1)S(1)}, bf16[128,1024]{1,0:T(8,128)(2,1)S(1)}, u32[]{:S(2)}, u32[]{:S(2)}) collective-permute-start(bf16[128,1024]{1,0:T(8,128)(2,1)S(1)} %pad_maximum_fusion.5), channel_id=1, source_target_pairs={{0,4},{1,3},{2,6},{3,1},{4,0},{5,7},{6,2},{7,5},{8,12},{9,11},{10,... | collective-permute-start | bytes 786440 | tf_op jit(solution)/shard_map/ppermute | solution.py:31
  30.4 13.2 %collective-permute-start.3 = (bf16[256,1152]{1,0:T(8,128)(2,1)S(1)}, bf16[256,1152]{1,0:T(8,128)(2,1)}, u32[]{:S(2)}, u32[]{:S(2)}) collective-permute-start(bf16[256,1152]{1,0:T(8,128)(2,1)S(1)} %pad_maximum_fusion.refs_0_.refs_2_), channel_id=1, source_target_pairs={{0,2},{1,5},{2,0},{3,7},{4,6},{5,1},{6,4},{7,3},{8,10},{9,13},{10,... | collective-permute-start | bytes 1769480 | tf_op jit(solution)/shard_map/ppermute | solution.py:31
  32.9 18.3 %collective-permute-start.14 = (bf16[256,1024]{1,0:T(8,128)(2,1)S(1)}, bf16[256,1024]{1,0:T(8,128)(2,1)}, u32[]{:S(2)}, u32[]{:S(2)}) collective-permute-start(bf16[256,1024]{1,0:T(8,128)(2,1)S(1)} %pad_maximum_fusion.1.refs_0_), channel_id=1, source_target_pairs={{0,2},{1,5},{2,0},{3,7},{4,6},{5,1},{6,4},{7,3},{8,10},{9,13},{10,... | collective-permute-start | bytes 1572872 | tf_op jit(solution)/shard_map/ppermute | solution.py:31
  38.5 13.5 %collective-permute-start.17 = (bf16[256,1024]{1,0:T(8,128)(2,1)S(1)}, bf16[256,1024]{1,0:T(8,128)(2,1)}, u32[]{:S(2)}, u32[]{:S(2)}) collective-permute-start(bf16[256,1024]{1,0:T(8,128)(2,1)S(1)} %pad_maximum_fusion.2.refs_1_), channel_id=1, source_target_pairs={{0,2},{1,5},{2,0},{3,7},{4,6},{5,1},{6,4},{7,3},{8,10},{9,13},{10,... | collective-permute-start | bytes 1572872 | tf_op jit(solution)/shard_map/ppermute | solution.py:31
  39.4 37.6 %collective-permute-start = (bf16[64,1024]{1,0:T(8,128)(2,1)S(1)}, bf16[64,1024]{1,0:T(8,128)(2,1)S(1)}, u32[]{:S(2)}, u32[]{:S(2)}) collective-permute-start(bf16[64,1024]{1,0:T(8,128)(2,1)S(1)} %bitcast.33), channel_id=1, source_target_pairs={{0,16},{1,17},{2,18},{3,19},{4,20},{5,21},{6,22},{7,23},{8,24},{9,... | collective-permute-start | bytes 393224 | tf_op jit(solution)/shard_map/ppermute | solution.py:26
  40.7 37.9 %collective-permute-start.11 = (bf16[64,1024]{1,0:T(8,128)(2,1)S(1)}, bf16[64,1024]{1,0:T(8,128)(2,1)S(1)}, u32[]{:S(2)}, u32[]{:S(2)}) collective-permute-start(bf16[64,1024]{1,0:T(8,128)(2,1)S(1)} %bitcast.31), channel_id=1, source_target_pairs={{0,16},{1,17},{2,18},{3,19},{4,20},{5,21},{6,22},{7,23},{8,24},{9,... | collective-permute-start | bytes 393224 | tf_op jit(solution)/shard_map/ppermute | solution.py:26
  47.2 10.6 %collective-permute-start.6 = (bf16[128,1024]{1,0:T(8,128)(2,1)S(1)}, bf16[128,1024]{1,0:T(8,128)(2,1)S(1)}, u32[]{:S(2)}, u32[]{:S(2)}) collective-permute-start(bf16[128,1024]{1,0:T(8,128)(2,1)S(1)} %get-tuple-element.23), channel_id=1, source_target_pairs={{0,2},{1,5},{2,0},{3,7},{4,6},{5,1},{6,4},{7,3},{8,10},{9,13},{10,... | collective-permute-start | bytes 786440 | tf_op jit(solution)/shard_map/ppermute | solution.py:31
  51.3 14.7 %collective-permute-start.8 = (bf16[128,1024]{1,0:T(8,128)(2,1)S(1)}, bf16[128,1024]{1,0:T(8,128)(2,1)S(1)}, u32[]{:S(2)}, u32[]{:S(2)}) collective-permute-start(bf16[128,1024]{1,0:T(8,128)(2,1)S(1)} %get-tuple-element.24), channel_id=1, source_target_pairs={{0,2},{1,5},{2,0},{3,7},{4,6},{5,1},{6,4},{7,3},{8,10},{9,13},{10,... | collective-permute-start | bytes 786440 | tf_op jit(solution)/shard_map/ppermute | solution.py:31
  56.5 8.1 %collective-permute-start.18 = (bf16[128,1024]{1,0:T(8,128)(2,1)S(1)}, bf16[128,1024]{1,0:T(8,128)(2,1)S(1)}, u32[]{:S(2)}, u32[]{:S(2)}) collective-permute-start(bf16[128,1024]{1,0:T(8,128)(2,1)S(1)} %get-tuple-element.30), channel_id=1, source_target_pairs={{0,2},{1,5},{2,0},{3,7},{4,6},{5,1},{6,4},{7,3},{8,10},{9,13},{10,... | collective-permute-start | bytes 786440 | tf_op jit(solution)/shard_map/ppermute | solution.py:31
  57.9 9.7 %collective-permute-start.7 = (bf16[128,1024]{1,0:T(8,128)(2,1)S(1)}, bf16[128,1024]{1,0:T(8,128)(2,1)S(1)}, u32[]{:S(2)}, u32[]{:S(2)}) collective-permute-start(bf16[128,1024]{1,0:T(8,128)(2,1)S(1)} %add_convert_fusion.3), channel_id=1, source_target_pairs={{0,4},{1,3},{2,6},{3,1},{4,0},{5,7},{6,2},{7,5},{8,12},{9,11},{10,... | collective-permute-start | bytes 786440 | tf_op jit(solution)/shard_map/ppermute | solution.py:31
  64.6 7.0 %collective-permute-start.20 = (bf16[128,1024]{1,0:T(8,128)(2,1)S(1)}, bf16[128,1024]{1,0:T(8,128)(2,1)S(1)}, u32[]{:S(2)}, u32[]{:S(2)}) collective-permute-start(bf16[128,1024]{1,0:T(8,128)(2,1)S(1)} %get-tuple-element.31), channel_id=1, source_target_pairs={{0,2},{1,5},{2,0},{3,7},{4,6},{5,1},{6,4},{7,3},{8,10},{9,13},{10,... | collective-permute-start | bytes 786440 | tf_op jit(solution)/shard_map/ppermute | solution.py:31
  65.9 7.2 %collective-permute-start.19 = (bf16[128,1024]{1,0:T(8,128)(2,1)S(1)}, bf16[128,1024]{1,0:T(8,128)(2,1)S(1)}, u32[]{:S(2)}, u32[]{:S(2)}) collective-permute-start(bf16[128,1024]{1,0:T(8,128)(2,1)S(1)} %add_convert_fusion.1), channel_id=1, source_target_pairs={{0,4},{1,3},{2,6},{3,1},{4,0},{5,7},{6,2},{7,5},{8,12},{9,11},{10,... | collective-permute-start | bytes 786440 | tf_op jit(solution)/shard_map/ppermute | solution.py:31
  67.8 10.2 %collective-permute-start.10 = (bf16[64,1024]{1,0:T(8,128)(2,1)S(1)}, bf16[64,1024]{1,0:T(8,128)(2,1)S(1)}, u32[]{:S(2)}, u32[]{:S(2)}) collective-permute-start(bf16[64,1024]{1,0:T(8,128)(2,1)S(1)} %get-tuple-element.35), channel_id=1, source_target_pairs={{0,24},{1,25},{2,26},{3,27},{4,28},{5,29},{6,30},{7,31},{8,16},{9,... | collective-permute-start | bytes 393224 | tf_op jit(solution)/shard_map/ppermute | solution.py:26
  71.7 6.3 %collective-permute-start.9 = (bf16[64,1024]{1,0:T(8,128)(2,1)S(1)}, bf16[64,1024]{1,0:T(8,128)(2,1)S(1)}, u32[]{:S(2)}, u32[]{:S(2)}) collective-permute-start(bf16[64,1024]{1,0:T(8,128)(2,1)S(1)} %get-tuple-element.34), channel_id=1, source_target_pairs={{0,16},{1,17},{2,18},{3,19},{4,20},{5,21},{6,22},{7,23},{8,24},{9,... | collective-permute-start | bytes 393224 | tf_op jit(solution)/shard_map/ppermute | solution.py:26
  73.3 9.4 %collective-permute-start.22 = (bf16[64,1024]{1,0:T(8,128)(2,1)S(1)}, bf16[64,1024]{1,0:T(8,128)(2,1)S(1)}, u32[]{:S(2)}, u32[]{:S(2)}) collective-permute-start(bf16[64,1024]{1,0:T(8,128)(2,1)S(1)} %get-tuple-element.33), channel_id=1, source_target_pairs={{0,24},{1,25},{2,26},{3,27},{4,28},{5,29},{6,30},{7,31},{8,16},{9,... | collective-permute-start | bytes 393224 | tf_op jit(solution)/shard_map/ppermute | solution.py:26
  77.0 5.7 %collective-permute-start.21 = (bf16[64,1024]{1,0:T(8,128)(2,1)S(1)}, bf16[64,1024]{1,0:T(8,128)(2,1)S(1)}, u32[]{:S(2)}, u32[]{:S(2)}) collective-permute-start(bf16[64,1024]{1,0:T(8,128)(2,1)S(1)} %get-tuple-element.32), channel_id=1, source_target_pairs={{0,16},{1,17},{2,18},{3,19},{4,20},{5,21},{6,22},{7,23},{8,24},{9,... | collective-permute-start | bytes 393224 | tf_op jit(solution)/shard_map/ppermute | solution.py:26
